TPU v7x, 32 devices: a whole 2x2x4 slice. The times are simulated.
32 devices in a mesh: lon: 2 (over y), mem: 16 (over z, x, core).
Axes of the slice: x: 2, y: 2, z: 4, core: 2. Of those that a mesh axis runs over, the one named last changes fastest.
Arguments:
- ensemble: float32 [16, 24576], P('mem', 'lon')
- increments: bfloat16 [16, 24576], P('mem', 'lon'), may hold values from -6 to 6
- offsets: int32 [48, 7], P('lon'), may hold values from -12 to 12, as said below
- taper: bfloat16 [8, 512, 512], replicated
Outputs:
- covariance_product: float32 [16, 24576], P('mem', 'lon')
Inputs may be any that keep to these rules, and one draw needn't show every extreme that they name: Each row lists 7 different nonzero offsets in ascending order.
All inputs are finite; a program needn't handle non-finite values.
Results may differ from a plain program's by a relative error of at most 0.008.
Values may be sent and summed in bfloat16 or wider, within the bound.
No kernel may reach another device: no remote copies, remote signals or barrier semaphores. Data moves between devices by JAX's collectives and lax.ppermute only.
A program may use at most 64 MiB of HBM per device.

v0:
```python
import jax
import jax.numpy as jnp
from jax import lax
from jax.sharding import PartitionSpec as P


def extended_2(block, sides, width):
    for axis, dim in sides:
        count = lax.axis_size(axis)
        forward = [(i, i + 1) for i in range(count - 1)]
        forward.append((count - 1, 0))
        backward = [(target, source) for source, target in forward]
        low = lax.ppermute(
            lax.slice_in_dim(block, block.shape[dim] - width, None, axis=dim), axis, forward
        )
        high = lax.ppermute(lax.slice_in_dim(block, 0, width, axis=dim), axis, backward)
        block = jnp.concatenate([low, block, high], axis=dim)
    return block


def taper_apply(extended, offsets, taper):
    vectors = extended.shape[0]
    block_count = offsets.shape[0]
    block_size = taper.shape[1]
    reach_blocks = block_count // 2
    blocks = extended.reshape(vectors, block_count + 2 * reach_blocks, block_size)
    block_rows = jnp.arange(block_count, dtype=jnp.int32) + reach_blocks
    indices = jnp.concatenate([block_rows[:, None], block_rows[:, None] + offsets], axis=1)
    picked = jnp.take(blocks, indices, axis=1)
    tapered = jnp.einsum("qrsb,sab->qra", picked, taper, preferred_element_type=jnp.float32)
    return tapered.reshape(vectors, block_count * block_size)


def extend_product(factor_one, factor_two, rim_width):
    weighted = (factor_one.astype(jnp.float32) * factor_two.astype(jnp.float32)).astype(
        jnp.bfloat16
    )
    return extended_2(weighted, (("lon", 1),), rim_width)


def on_device(ensemble, increments, offsets, taper):
    member_count = lax.axis_size("mem") * ensemble.shape[0]
    rim_width = offsets.shape[0] // 2 * taper.shape[1]
    ens_mean = lax.psum(jnp.sum(ensemble, axis=0), "mem") / member_count
    perturb = (ensemble - ens_mean[None, :]).astype(jnp.bfloat16)
    increments_all = lax.all_gather(increments, "mem", axis=0, tiled=True)
    extended = extend_product(perturb, increments_all, rim_width)
    tapered = taper_apply(extended, offsets, taper)
    summed = lax.psum_scatter(
        perturb.astype(jnp.float32) * tapered, "mem", scatter_dimension=0, tiled=True
    )
    return summed / (member_count - 1)


def solution(mesh):
    return jax.shard_map(
        on_device,
        mesh=mesh,
        in_specs=(P("mem", "lon"), P("mem", "lon"), P("lon", None), P()),
        out_specs=P("mem", "lon"),
        check_vma=False,
    )
```

profile of v0, /device:TPU:0, one launch (start us, length us, event | category | flops | bytes accessed | tf_op | source)
XLA Modules:
  0.0 211.6 jit_solution(10847090803187922535)
XLA Ops:
  6.5 0.0 copy-start
  6.5 0.0 all-reduce.3.cloned.1.call-start
  6.5 63.8 %psum.7 = f32[12288]{0:T(1024)S(1)} all-reduce(f32[12288]{0:T(1024)} %bitcast.42), channel_id=1, replica_groups=mesh['lon'=2,'mem'=16] {'mem'}, use_global_device_ids=true, to_apply=%region_0.0 | all-reduce | flops 12288 | bytes 98304 | tf_op jit(solution)/shard_map/psum | solution.py:44
  70.3 0.9 convert_convert_fusion
  71.2 20.1 %all-gather = bf16[16,1,12288]{2,1,0:T(2,128)(2,1)S(1)} all-gather(bf16[1,1,12288]{2,1,0:T(2,128)(2,1)} %bitcast.44), channel_id=1, replica_groups=mesh['lon'=2,'mem'=16] {'mem'}, dimensions={0}, use_global_device_ids=true | all-gather | bytes 417792 | tf_op jit(solution)/shard_map/all_gather | solution.py:46
  91.2 0.4 fusion.11
  91.7 1.6 collective-permute-start
  93.3 0.5 collective-permute-start.1
  93.8 0.0 copy-done
  93.9 0.1 copy.22
  93.9 0.1 reshape.98
  94.1 0.1 copy.19
  94.2 5.4 %collective-permute-done = bf16[16,6144]{1,0:T(8,128)(2,1)S(1)} collective-permute-done((bf16[16,6144]{1,0:T(8,128)(2,1)S(1)}, bf16[16,6144]{1,0:T(8,128)(2,1)S(1)}, u32[]{:S(2)}, u32[]{:S(2)}) %collective-permute-start) | collective-permute-done | bytes 196640 | tf_op jit(solution)/shard_map/ppermute | solution.py:13
  99.5 3.6 %collective-permute-done.1 = bf16[16,6144]{1,0:T(8,128)(2,1)S(1)} collective-permute-done((bf16[16,6144]{1,0:T(8,128)(2,1)S(1)}, bf16[16,6144]{1,0:T(8,128)(2,1)S(1)}, u32[]{:S(2)}, u32[]{:S(2)}) %collective-permute-start.1) | collective-permute-done | bytes 196640 | tf_op jit(solution)/shard_map/ppermute | solution.py:16
  103.2 0.1 pad_maximum_fusion
  103.2 0.1 copy.30
  103.3 2.6 %gather_fusion = bf16[192,16,512]{2,1,0:T(8,128)(2,1)} fusion(bf16[16,48,512]{2,0,1:T(8,128)(2,1)S(1)} %bitcast.36, s32[1024]{0:T(1024)S(1)} %pad_clamp_fusion), kind=kCustom, calls=%fused_computation | custom fusion | bytes 6292224 | tf_op jit(solution)/shard_map/jit(_take)/gather | solution.py:29
  106.0 5.0 %fusion.6 = f32[24,2,8,512]{3,2,1,0:T(8,128)S(1)} fusion(bf16[8,512,512]{2,1,0:T(8,128)(2,1)} %param.7, bf16[24,8,16,512]{3,2,1,0:T(8,128)(2,1)} %bitcast.39, pred[24,8]{1,0:T(8,128)(4,1)S(1)} %copy.19), kind=kOutput, calls=%fused_computation.7 | convolution fusion | flops 1612185600 | bytes 8126656 | tf_op jit(solution)/shard_map/qrsb,sab->qra/dot_general | solution.py:30
  110.9 0.0 copy-start.1
  110.9 0.1 copy.27
  111.0 1.0 broadcast_multiply_fusion
  112.0 0.0 all-reduce.3.cloned.1.call-update
  112.0 0.0 copy-done.1
  112.0 0.6 dynamic-slice
  112.6 89.8 %all-reduce.3.cloned.1.call-done = f32[16,12288]{1,0:T(8,128)} async-done(((f32[16,12288]{1,0:T(8,128)}), f32[16,12288]{1,0:T(8,128)}) %all-reduce.3.cloned.1.call-update) | async-done | bytes 786448
  202.5 2.3 %dynamic-slice_multiply_fusion = f32[1,12288]{1,0:T(1,128)} fusion(f32[16,12288]{1,0:T(8,128)} %all-reduce.3.cloned.1.call-done, u32[]{:T(128)} %bitcast.15), kind=kLoop, calls=%fused_computation.13 | loop fusion | flops 12288 | bytes 98308 | tf_op jit(solution)/shard_map/div | solution.py:52
  (10 shorter events, 0.1 us)
Async XLA Ops:
  6.5 87.3 %copy-start = (s32[24,7]{0,1:T(8,128)S(1)}, s32[24,7]{0,1:T(8,128)}, u32[]{:S(2)}) copy-start(s32[24,7]{0,1:T(8,128)} %param.6) | copy-start | bytes 2020
  6.5 196.0 %all-reduce.3.cloned.1.call-start = ((), (), s32[]{:S(2)}) async-start(), calls=%async_computation | async-start | bytes 1572864
  91.7 7.8 %collective-permute-start = (bf16[16,6144]{1,0:T(8,128)(2,1)S(1)}, bf16[16,6144]{1,0:T(8,128)(2,1)S(1)}, u32[]{:S(2)}, u32[]{:S(2)}) collective-permute-start(bf16[16,6144]{1,0:T(8,128)(2,1)S(1)} %get-tuple-element.5), channel_id=1, source_target_pairs={{0,16},{16,0},{1,17},{17,1},{2,18},{18,2},{3,19},{19,3},{4,20},{20... | collective-permute-start | bytes 589832 | tf_op jit(solution)/shard_map/ppermute | solution.py:13
  93.3 9.8 %collective-permute-start.1 = (bf16[16,6144]{1,0:T(8,128)(2,1)S(1)}, bf16[16,6144]{1,0:T(8,128)(2,1)S(1)}, u32[]{:S(2)}, u32[]{:S(2)}) collective-permute-start(bf16[16,6144]{1,0:T(8,128)(2,1)S(1)} %get-tuple-element.6), channel_id=1, source_target_pairs={{16,0},{0,16},{17,1},{1,17},{18,2},{2,18},{19,3},{3,19},{20,4},{4,... | collective-permute-start | bytes 589832 | tf_op jit(solution)/shard_map/ppermute | solution.py:16
  110.9 1.1 copy-start.1
Sparse Core Ops, SparseCore 0:
  112.1 90.3 all-reduce.2
where the time goes:
time: 212 us
  waiting for transfers between devices  98.9 us (47%)
  blocking collectives  83.8 us (40%)
  between operations  13.5 us (6%)
  matrix products  4.97 us (2%)
  other arithmetic  4.67 us (2%)
  local copies, waits for them, and re-layouts  3.72 us (2%)
    unnamed x2, waiting for transfers between devices  89.9 us
    psum x1, blocking collectives, on_device(): ens_mean = lax.psum(jnp.sum(ensemble, axis=0), 'mem') / member_count  63.8 us
    all_gather x1, blocking collectives, on_device(): increments_all = lax.all_gather(increments, 'mem', axis=0, tiled=True)  20.1 us
    ppermute x1, waiting for transfers between devices, extended_2(): lax.ppermute(lax.slice_in_dim(block, block.shape[dim] - width, None, axis...  5.35 us
    dot_general x1, matrix products, taper_apply(): jnp.einsum('qrsb,sab->qra', picked, taper, preferred_element_type=jnp.flo...  4.97 us
  transfers between devices with their start and end apart: 3, of which 3 were waited for; matrix products, arithmetic and copies ran while one was open for 0% of the time, Pallas kernels for 0%

commit v1 on v0

v1 whole, which is shorter than its diff:
```python
import functools

import jax
import jax.numpy as jnp
from jax import lax
from jax.experimental import pallas as pl
from jax.experimental.pallas import tpu as pltpu
from jax.sharding import PartitionSpec as P

LANES = 128
SUB = 8


def product_kernel(
    group, off_ref, *refs
):
    own, other = refs[:4], refs[4:8]
    inc_own, inc_other, taper_hbm, out_ref = refs[8:12]
    tiles, pert, wide, picked_from, picked, acc, sems = refs[12:]
    slots, block_size, _ = tiles.shape
    members = 4 * group
    rows = inc_own.shape[0]
    quarters = block_size // LANES
    block_count = rows // quarters
    copies = []
    for s in range(slots):
        copies.append(pltpu.make_async_copy(taper_hbm.at[s], tiles.at[s], sems.at[s]))
        copies[-1].start()

    def weigh(side, groups, inc_ref, keep):
        def chunk(r, carry):
            at = pl.multiple_of(r * 2 * SUB, 2 * SUB)
            inc = inc_ref[pl.ds(at, 2 * SUB), :].astype(jnp.float32)
            states = [
                groups[g][j, pl.ds(at, 2 * SUB), :]
                for g in range(4)
                for j in range(group)
            ]
            total = states[0]
            for state in states[1:]:
                total = total + state
            mean = total * (1.0 / members)
            for m, state in enumerate(states):
                p = (state - mean).astype(jnp.bfloat16).astype(jnp.float32)
                if keep:
                    pert[pl.ds(m * rows + at, 2 * SUB), :] = p
                wide[pl.ds(m * rows + at, 2 * SUB), :] = p * inc
            return carry

        lax.fori_loop(0, rows // (2 * SUB), chunk, 0)

        def spread(i, carry):
            for q in range(quarters):
                part = wide[pl.ds(i * quarters + q, members, rows), :]
                picked_from[side * block_count + i, :, q * LANES : (q + 1) * LANES] = (
                    part.astype(jnp.bfloat16)
                )
            return carry

        lax.fori_loop(0, block_count, spread, 0, unroll=4)

    weigh(1, other, inc_other, False)
    weigh(0, own, inc_own, True)

    contract = (((1,), (1,)), ((), ()))
    copies[0].wait()
    vectors = block_count * members
    acc[...] = lax.dot_general(
        picked_from[0:block_count].reshape(vectors, block_size),
        tiles[0],
        contract,
        preferred_element_type=jnp.float32,
    )
    for s in range(1, slots):
        for i in range(block_count):
            place = i + off_ref[s - 1, i]
            place = jnp.where(place < 0, place + 2 * block_count, place)
            picked[i * members : (i + 1) * members, :] = picked_from[place]
        copies[s].wait()
        acc[...] += lax.dot_general(
            picked[...], tiles[s], contract, preferred_element_type=jnp.float32
        )

    scale = 1.0 / (members - 1)
    for i in range(block_count):
        for q in range(quarters):
            lanes = slice(q * LANES, (q + 1) * LANES)
            term = (
                pert[pl.ds(i * quarters + q, members, rows), :]
                * acc[i * members : (i + 1) * members, lanes]
            )
            row = jnp.sum(term, axis=0, keepdims=True) * scale
            out_ref[:, i * block_size + q * LANES : i * block_size + (q + 1) * LANES] = row


def mover(lon_size, mem_size):
    def one(x, step, mem_of):
        perm = []
        for l in range(lon_size):
            for m in range(mem_size):
                source = ((l + step) % lon_size) * mem_size + mem_of(m)
                perm.append((source, l * mem_size + m))
        return lax.ppermute(x, ("lon", "mem"), perm)

    def move(x, across, mem_of):
        if not across:
            return one(x, 0, mem_of)
        if lon_size == 2:
            return one(x, 1, mem_of)
        half = x.shape[-2] // 2
        right = one(x[..., :half, :], 1, mem_of)
        left = one(x[..., half:, :], -1, mem_of)
        return jnp.concatenate([right, left], axis=-2)

    return move


def on_device(ensemble, increments, offsets, taper):
    lon_size, mem_size = lax.axis_size("lon"), lax.axis_size("mem")
    group = mem_size // 4
    slots, block_size, _ = taper.shape
    block_count = offsets.shape[0]
    columns = ensemble.shape[1]
    rows = columns // LANES
    move = mover(lon_size, mem_size)

    state = ensemble.reshape(1, rows, LANES)
    inc = increments.reshape(rows, LANES)
    inc_other = move(inc, True, lambda m: m)
    states = [state]
    for d in range(1, group):
        states.append(move(state, False, lambda m: (m + 4 * d) % mem_size))
    mine = jnp.concatenate(states, axis=0)
    groups = [
        mine,
        move(mine, False, lambda m: m ^ 2),
        move(mine, True, lambda m: m),
        move(mine, True, lambda m: m ^ 2),
    ]
    groups += [move(g, False, lambda m: m ^ 1) for g in groups]
    own = [groups[i] for i in (0, 1, 4, 5)]
    other = [groups[i] for i in (2, 3, 6, 7)]

    vectors = mem_size * block_count
    whole = pl.BlockSpec(memory_space=pltpu.VMEM)
    return pl.pallas_call(
        functools.partial(product_kernel, group),
        out_shape=jax.ShapeDtypeStruct((1, columns), jnp.float32),
        in_specs=[pl.BlockSpec(memory_space=pltpu.SMEM)]
        + [whole] * 10
        + [pl.BlockSpec(memory_space=pl.ANY)],
        out_specs=whole,
        scratch_shapes=[
            pltpu.VMEM((slots, block_size, block_size), jnp.bfloat16),
            pltpu.VMEM((mem_size * rows, LANES), jnp.float32),
            pltpu.VMEM((mem_size * rows, LANES), jnp.float32),
            pltpu.VMEM((2 * block_count, mem_size, block_size), jnp.bfloat16),
            pltpu.VMEM((vectors, block_size), jnp.bfloat16),
            pltpu.VMEM((vectors, block_size), jnp.float32),
            pltpu.SemaphoreType.DMA((slots,)),
        ],
        compiler_params=pltpu.CompilerParams(vmem_limit_bytes=48 * 1024 * 1024),
    )(offsets.T, *own, *other, inc, inc_other, taper)


def solution(mesh):
    return jax.shard_map(
        on_device,
        mesh=mesh,
        in_specs=(P("mem", "lon"), P("mem", "lon"), P("lon", None), P()),
        out_specs=P("mem", "lon"),
        check_vma=False,
    )
```

time: 212 us -> 36.2 us (0.17)
  waiting for transfers between devices: 98.9 us -> 13.2 us
  blocking collectives: 83.8 us -> 0 us
  between operations: 13.5 us -> 0.03 us
  starting transfers between devices: 2.09 us -> 12.2 us
  Pallas kernels: 0 us -> 5.81 us
  matrix products: 4.97 us -> 0 us
  other arithmetic: 4.67 us -> 1.75 us
    unnamed x2 -> x0, waiting for transfers between devices: 89.9 us -> none
    psum x1 -> x0, blocking collectives: 63.8 us -> none  [on_device(): ens_mean = lax.psum(jnp.sum(ensemble, axis=0), 'mem') / member_count]
    all_gather x1 -> x0, blocking collectives: 20.1 us -> none  [on_device(): increments_all = lax.all_gather(increments, 'mem', axis=0, tiled=True)]
    ppermute x2 -> x11, starting transfers between devices: 2.09 us -> 12.2 us  [one(): return lax.ppermute(x, ('lon', 'mem'), perm)]
    pallas_call x0 -> x1, Pallas kernels: none -> 5.81 us  [on_device(): pl.pallas_call(functools.partial(product_kernel, group), out_shape=jax.Sh...]
    dot_general x1 -> x0, matrix products: 4.97 us -> none  [taper_apply(): jnp.einsum('qrsb,sab->qra', picked, taper, preferred_element_type=jnp.flo...]
    ppermute x2 -> x11, waiting for transfers between devices: 9 us -> 13.2 us  [one(): return lax.ppermute(x, ('lon', 'mem'), perm)]
    gather x1 -> x0, local copies, waits for them, and re-layouts: 2.65 us -> none  [taper_apply(): picked = jnp.take(blocks, indices, axis=1)]
  transfers between devices with their start and end apart: 3 -> 11, of which waited for: 3 -> 6; matrix products, arithmetic and copies ran while one was open for 0% -> 3% of each run, Pallas kernels for 0% -> 0%
where the time goes in v1:
time: 36.2 us; the launch traced here: 35.9 us
  waiting for transfers between devices  13.2 us (36%)
  starting transfers between devices  12.2 us (34%)
  Pallas kernels  5.81 us (16%)
  local copies, waits for them, and re-layouts  2.87 us (8%)
  other arithmetic  1.75 us (5%)
    ppermute x11, waiting for transfers between devices, one(): return lax.ppermute(x, ('lon', 'mem'), perm)  13.2 us
    ppermute x11, starting transfers between devices, one(): return lax.ppermute(x, ('lon', 'mem'), perm)  12.2 us
    pallas_call x1, Pallas kernels, on_device(): pl.pallas_call(functools.partial(product_kernel, group), out_shape=jax.Sh...  5.81 us
    unnamed x4, local copies, waits for them, and re-layouts  2.87 us
    unnamed x1, other arithmetic  0.93 us
    concatenate x1, other arithmetic, on_device(): mine = jnp.concatenate(states, axis=0)  0.82 us
  transfers between devices with their start and end apart: 11, of which 6 were waited for; matrix products, arithmetic and copies ran while one was open for 3% of the time, Pallas kernels for 0%

profile of v1, /device:TPU:0, one launch (start us, length us, event | category | flops | bytes accessed | tf_op | source)
XLA Modules:
  0.0 35.9 jit_solution(14584634498673896276)
XLA Ops:
  0.0 3.0 %collective-permute-start.2 = (f32[1,96,128]{2,1,0:T(8,128)}, f32[1,96,128]{2,1,0:T(8,128)S(1)}, u32[]{:S(2)}, u32[]{:S(2)}) collective-permute-start(f32[1,96,128]{2,1,0:T(8,128)} %bitcast.6), channel_id=1, source_target_pairs={{12,0},{13,1},{14,2},{15,3},{0,4},{1,5},{2,6},{3,7},{4,8},{5,9},{6... | collective-permute-start | bytes 147464 | tf_op jit(solution)/shard_map/ppermute | solution.py:103
  3.0 2.6 %collective-permute-start.1 = (f32[1,96,128]{2,1,0:T(8,128)}, f32[1,96,128]{2,1,0:T(8,128)S(1)}, u32[]{:S(2)}, u32[]{:S(2)}) collective-permute-start(f32[1,96,128]{2,1,0:T(8,128)} %bitcast.7), channel_id=1, source_target_pairs={{8,0},{9,1},{10,2},{11,3},{12,4},{13,5},{14,6},{15,7},{0,8},{1,9},... | collective-permute-start | bytes 147464 | tf_op jit(solution)/shard_map/ppermute | solution.py:103
  5.6 1.3 %collective-permute-start = (f32[1,96,128]{2,1,0:T(8,128)}, f32[1,96,128]{2,1,0:T(8,128)S(1)}, u32[]{:S(2)}, u32[]{:S(2)}) collective-permute-start(f32[1,96,128]{2,1,0:T(8,128)} %bitcast.8), channel_id=1, source_target_pairs={{4,0},{5,1},{6,2},{7,3},{8,4},{9,5},{10,6},{11,7},{12,8},{13,9},{1... | collective-permute-start | bytes 147464 | tf_op jit(solution)/shard_map/ppermute | solution.py:103
  7.0 0.5 %collective-permute-done.2 = f32[1,96,128]{2,1,0:T(8,128)S(1)} collective-permute-done((f32[1,96,128]{2,1,0:T(8,128)}, f32[1,96,128]{2,1,0:T(8,128)S(1)}, u32[]{:S(2)}, u32[]{:S(2)}) %collective-permute-start.2) | collective-permute-done | bytes 49184 | tf_op jit(solution)/shard_map/ppermute | solution.py:103
  7.4 2.0 %collective-permute-done.1 = f32[1,96,128]{2,1,0:T(8,128)S(1)} collective-permute-done((f32[1,96,128]{2,1,0:T(8,128)}, f32[1,96,128]{2,1,0:T(8,128)S(1)}, u32[]{:S(2)}, u32[]{:S(2)}) %collective-permute-start.1) | collective-permute-done | bytes 49184 | tf_op jit(solution)/shard_map/ppermute | solution.py:103
  9.4 0.5 %collective-permute-done = f32[1,96,128]{2,1,0:T(8,128)S(1)} collective-permute-done((f32[1,96,128]{2,1,0:T(8,128)}, f32[1,96,128]{2,1,0:T(8,128)S(1)}, u32[]{:S(2)}, u32[]{:S(2)}) %collective-permute-start) | collective-permute-done | bytes 49184 | tf_op jit(solution)/shard_map/ppermute | solution.py:103
  9.9 0.8 %pad_maximum_fusion.refs_0_ = f32[4,96,128]{2,1,0:T(8,128)S(1)} fusion(f32[1,96,128]{2,1,0:T(8,128)S(1)} %collective-permute-done.2, f32[1,96,128]{2,1,0:T(8,128)S(1)} %collective-permute-done.1, f32[1,96,128]{2,1,0:T(8,128)S(1)} %collective-permute-done, f32[1,96,128]{2,1,0:T(8,128)} %bitcast.9), kind=kLoop, calls=%fused_computation | loop fusion | flops 147456 | bytes 393216 | tf_op jit(solution)/shard_map/concatenate | solution.py:133
  10.8 2.6 %collective-permute-start.7 = (f32[4,96,128]{2,1,0:T(8,128)S(1)}, f32[4,96,128]{2,1,0:T(8,128)S(1)}, u32[]{:S(2)}, u32[]{:S(2)}) collective-permute-start(f32[4,96,128]{2,1,0:T(8,128)S(1)} %pad_maximum_fusion.refs_0_), channel_id=1, source_target_pairs={{18,0},{19,1},{16,2},{17,3},{22,4},{23,5},{20,6},{21,7},{26,8},{27... | collective-permute-start | bytes 589832 | tf_op jit(solution)/shard_map/ppermute | solution.py:103
  13.4 0.5 %collective-permute-start.6 = (f32[4,96,128]{2,1,0:T(8,128)S(1)}, f32[4,96,128]{2,1,0:T(8,128)S(1)}, u32[]{:S(2)}, u32[]{:S(2)}) collective-permute-start(f32[4,96,128]{2,1,0:T(8,128)S(1)} %pad_maximum_fusion.refs_0_), channel_id=1, source_target_pairs={{16,0},{17,1},{18,2},{19,3},{20,4},{21,5},{22,6},{23,7},{24,8},{25... | collective-permute-start | bytes 589832 | tf_op jit(solution)/shard_map/ppermute | solution.py:103
  13.9 0.4 %collective-permute-start.3 = (f32[4,96,128]{2,1,0:T(8,128)S(1)}, f32[4,96,128]{2,1,0:T(8,128)S(1)}, u32[]{:S(2)}, u32[]{:S(2)}) collective-permute-start(f32[4,96,128]{2,1,0:T(8,128)S(1)} %pad_maximum_fusion.refs_0_), channel_id=1, source_target_pairs={{2,0},{3,1},{0,2},{1,3},{6,4},{7,5},{4,6},{5,7},{10,8},{11,9},{8,1... | collective-permute-start | bytes 589832 | tf_op jit(solution)/shard_map/ppermute | solution.py:103
  14.3 0.0 collective-permute-start.4
  14.3 5.2 %collective-permute-done.7.refs_5_ = f32[4,96,128]{2,1,0:T(8,128)S(1)} collective-permute-done((f32[4,96,128]{2,1,0:T(8,128)S(1)}, f32[4,96,128]{2,1,0:T(8,128)S(1)}, u32[]{:S(2)}, u32[]{:S(2)}) %collective-permute-start.7) | collective-permute-done | bytes 196640 | tf_op jit(solution)/shard_map/ppermute | solution.py:103
  19.6 0.0 collective-permute-start.9
  19.6 2.3 %collective-permute-done.6.refs_4_ = f32[4,96,128]{2,1,0:T(8,128)S(1)} collective-permute-done((f32[4,96,128]{2,1,0:T(8,128)S(1)}, f32[4,96,128]{2,1,0:T(8,128)S(1)}, u32[]{:S(2)}, u32[]{:S(2)}) %collective-permute-start.6) | collective-permute-done | bytes 196640 | tf_op jit(solution)/shard_map/ppermute | solution.py:103
  21.8 0.0 collective-permute-start.8
  21.8 0.0 collective-permute-done.3.refs_1_
  21.8 0.5 %collective-permute-start.5 = (f32[4,96,128]{2,1,0:T(8,128)S(1)}, f32[4,96,128]{2,1,0:T(8,128)S(1)}, u32[]{:S(2)}, u32[]{:S(2)}) collective-permute-start(f32[4,96,128]{2,1,0:T(8,128)S(1)} %collective-permute-done.3.refs_1_), channel_id=1, source_target_pairs={{1,0},{0,1},{3,2},{2,3},{5,4},{4,5},{7,6},{6,7},{9,8},{8,9},{11,10... | collective-permute-start | bytes 589832 | tf_op jit(solution)/shard_map/ppermute | solution.py:103
  22.3 0.9 %reduce = bf16[12288]{0:T(1024)(128)(2,1)S(1)} reduce(bf16[1,12288]{1,0:T(2,128)(2,1)} %param.5, bf16[]{:T(256)} %constant.2), dimensions={0}, to_apply=%param.5.reduce_sub_computation | reduce | bytes 49154 | tf_op args[1]
  23.3 1.2 %collective-permute-start.10 = (bf16[96,128]{1,0:T(8,128)(2,1)S(1)}, bf16[96,128]{1,0:T(8,128)(2,1)S(1)}, u32[]{:S(2)}, u32[]{:S(2)}) collective-permute-start(bf16[96,128]{1,0:T(8,128)(2,1)S(1)} %bitcast.3), channel_id=1, source_target_pairs={{16,0},{17,1},{18,2},{19,3},{20,4},{21,5},{22,6},{23,7},{24,8},{25... | collective-permute-start | bytes 73736 | tf_op jit(solution)/shard_map/ppermute | solution.py:103
  24.4 2.7 %collective-permute-done.10.refs_9_ = bf16[96,128]{1,0:T(8,128)(2,1)S(1)} collective-permute-done((bf16[96,128]{1,0:T(8,128)(2,1)S(1)}, bf16[96,128]{1,0:T(8,128)(2,1)S(1)}, u32[]{:S(2)}, u32[]{:S(2)}) %collective-permute-start.10) | collective-permute-done | bytes 24608 | tf_op jit(solution)/shard_map/ppermute | solution.py:103
  27.2 0.0 collective-permute-done.4.refs_2_
  27.2 0.0 collective-permute-done.9.refs_7_
  27.2 0.0 collective-permute-done.8.refs_6_
  27.2 0.0 collective-permute-done.5.refs_3_
  27.2 0.0 copy-start
  27.2 2.2 %copy-done = bf16[8,512,512]{2,1,0:T(8,128)(2,1)S(1)} copy-done((bf16[8,512,512]{2,1,0:T(8,128)(2,1)S(1)}, bf16[8,512,512]{2,1,0:T(8,128)(2,1)}, u32[]{:S(2)}) %copy-start) | copy-done | bytes 4194328
  29.4 0.0 copy-start.1
  29.4 0.7 %copy-done.1 = s32[24,7]{0,1:T(8,128)S(1)} copy-done((s32[24,7]{0,1:T(8,128)S(1)}, s32[24,7]{0,1:T(8,128)}, u32[]{:S(2)}) %copy-start.1) | copy-done | bytes 696
  30.1 5.8 %shard_map.46 = f32[1,12288]{1,0:T(1,128)} custom-call(s32[7,24]{1,0:T(8,128)S(1)} %bitcast.5, f32[4,96,128]{2,1,0:T(8,128)S(1)} %pad_maximum_fusion.refs_0_, f32[4,96,128]{2,1,0:T(8,128)S(1)} %collective-permute-done.3.refs_1_, f32[4,96,128]{2,1,0:T(8,128)S(1)} %collective-permute-done.4.refs_2_, f32[4,96,128]{2,1,0:T(8,128)S(1)} %collective-permute-done.5.refs_3_, ...), custom_call_target="tpu_custom_call" | custom-call | tf_op jit(solution)/shard_map/pallas_call | solution.py:146
Async XLA Ops:
  0.0 7.4 %collective-permute-start.2 = (f32[1,96,128]{2,1,0:T(8,128)}, f32[1,96,128]{2,1,0:T(8,128)S(1)}, u32[]{:S(2)}, u32[]{:S(2)}) collective-permute-start(f32[1,96,128]{2,1,0:T(8,128)} %bitcast.6), channel_id=1, source_target_pairs={{12,0},{13,1},{14,2},{15,3},{0,4},{1,5},{2,6},{3,7},{4,8},{5,9},{6... | collective-permute-start | bytes 147464 | tf_op jit(solution)/shard_map/ppermute | solution.py:103
  3.0 6.4 %collective-permute-start.1 = (f32[1,96,128]{2,1,0:T(8,128)}, f32[1,96,128]{2,1,0:T(8,128)S(1)}, u32[]{:S(2)}, u32[]{:S(2)}) collective-permute-start(f32[1,96,128]{2,1,0:T(8,128)} %bitcast.7), channel_id=1, source_target_pairs={{8,0},{9,1},{10,2},{11,3},{12,4},{13,5},{14,6},{15,7},{0,8},{1,9},... | collective-permute-start | bytes 147464 | tf_op jit(solution)/shard_map/ppermute | solution.py:103
  5.6 4.3 %collective-permute-start = (f32[1,96,128]{2,1,0:T(8,128)}, f32[1,96,128]{2,1,0:T(8,128)S(1)}, u32[]{:S(2)}, u32[]{:S(2)}) collective-permute-start(f32[1,96,128]{2,1,0:T(8,128)} %bitcast.8), channel_id=1, source_target_pairs={{4,0},{5,1},{6,2},{7,3},{8,4},{9,5},{10,6},{11,7},{12,8},{13,9},{1... | collective-permute-start | bytes 147464 | tf_op jit(solution)/shard_map/ppermute | solution.py:103
  10.8 8.8 %collective-permute-start.7 = (f32[4,96,128]{2,1,0:T(8,128)S(1)}, f32[4,96,128]{2,1,0:T(8,128)S(1)}, u32[]{:S(2)}, u32[]{:S(2)}) collective-permute-start(f32[4,96,128]{2,1,0:T(8,128)S(1)} %pad_maximum_fusion.refs_0_), channel_id=1, source_target_pairs={{18,0},{19,1},{16,2},{17,3},{22,4},{23,5},{20,6},{21,7},{26,8},{27... | collective-permute-start | bytes 589832 | tf_op jit(solution)/shard_map/ppermute | solution.py:103
  13.4 8.4 %collective-permute-start.6 = (f32[4,96,128]{2,1,0:T(8,128)S(1)}, f32[4,96,128]{2,1,0:T(8,128)S(1)}, u32[]{:S(2)}, u32[]{:S(2)}) collective-permute-start(f32[4,96,128]{2,1,0:T(8,128)S(1)} %pad_maximum_fusion.refs_0_), channel_id=1, source_target_pairs={{16,0},{17,1},{18,2},{19,3},{20,4},{21,5},{22,6},{23,7},{24,8},{25... | collective-permute-start | bytes 589832 | tf_op jit(solution)/shard_map/ppermute | solution.py:103
  13.9 7.9 %collective-permute-start.3 = (f32[4,96,128]{2,1,0:T(8,128)S(1)}, f32[4,96,128]{2,1,0:T(8,128)S(1)}, u32[]{:S(2)}, u32[]{:S(2)}) collective-permute-start(f32[4,96,128]{2,1,0:T(8,128)S(1)} %pad_maximum_fusion.refs_0_), channel_id=1, source_target_pairs={{2,0},{3,1},{0,2},{1,3},{6,4},{7,5},{4,6},{5,7},{10,8},{11,9},{8,1... | collective-permute-start | bytes 589832 | tf_op jit(solution)/shard_map/ppermute | solution.py:103
  14.3 12.9 %collective-permute-start.4 = (f32[4,96,128]{2,1,0:T(8,128)S(1)}, f32[4,96,128]{2,1,0:T(8,128)S(1)}, u32[]{:S(2)}, u32[]{:S(2)}) collective-permute-start(f32[4,96,128]{2,1,0:T(8,128)S(1)} %pad_maximum_fusion.refs_0_), channel_id=1, source_target_pairs={{1,0},{0,1},{3,2},{2,3},{5,4},{4,5},{7,6},{6,7},{9,8},{8,9},{11,10... | collective-permute-start | bytes 589832 | tf_op jit(solution)/shard_map/ppermute | solution.py:103
  19.6 7.6 %collective-permute-start.9 = (f32[4,96,128]{2,1,0:T(8,128)S(1)}, f32[4,96,128]{2,1,0:T(8,128)S(1)}, u32[]{:S(2)}, u32[]{:S(2)}) collective-permute-start(f32[4,96,128]{2,1,0:T(8,128)S(1)} %collective-permute-done.7.refs_5_), channel_id=1, source_target_pairs={{1,0},{0,1},{3,2},{2,3},{5,4},{4,5},{7,6},{6,7},{9,8},{8,9},{11,10... | collective-permute-start | bytes 589832 | tf_op jit(solution)/shard_map/ppermute | solution.py:103
  21.8 5.4 %collective-permute-start.8 = (f32[4,96,128]{2,1,0:T(8,128)S(1)}, f32[4,96,128]{2,1,0:T(8,128)S(1)}, u32[]{:S(2)}, u32[]{:S(2)}) collective-permute-start(f32[4,96,128]{2,1,0:T(8,128)S(1)} %collective-permute-done.6.refs_4_), channel_id=1, source_target_pairs={{1,0},{0,1},{3,2},{2,3},{5,4},{4,5},{7,6},{6,7},{9,8},{8,9},{11,10... | collective-permute-start | bytes 589832 | tf_op jit(solution)/shard_map/ppermute | solution.py:103
  21.8 5.4 %collective-permute-start.5 = (f32[4,96,128]{2,1,0:T(8,128)S(1)}, f32[4,96,128]{2,1,0:T(8,128)S(1)}, u32[]{:S(2)}, u32[]{:S(2)}) collective-permute-start(f32[4,96,128]{2,1,0:T(8,128)S(1)} %collective-permute-done.3.refs_1_), channel_id=1, source_target_pairs={{1,0},{0,1},{3,2},{2,3},{5,4},{4,5},{7,6},{6,7},{9,8},{8,9},{11,10... | collective-permute-start | bytes 589832 | tf_op jit(solution)/shard_map/ppermute | solution.py:103
  23.3 3.9 %collective-permute-start.10 = (bf16[96,128]{1,0:T(8,128)(2,1)S(1)}, bf16[96,128]{1,0:T(8,128)(2,1)S(1)}, u32[]{:S(2)}, u32[]{:S(2)}) collective-permute-start(bf16[96,128]{1,0:T(8,128)(2,1)S(1)} %bitcast.3), channel_id=1, source_target_pairs={{16,0},{17,1},{18,2},{19,3},{20,4},{21,5},{22,6},{23,7},{24,8},{25... | collective-permute-start | bytes 73736 | tf_op jit(solution)/shard_map/ppermute | solution.py:103
  27.2 2.2 %copy-start = (bf16[8,512,512]{2,1,0:T(8,128)(2,1)S(1)}, bf16[8,512,512]{2,1,0:T(8,128)(2,1)}, u32[]{:S(2)}) copy-start(bf16[8,512,512]{2,1,0:T(8,128)(2,1)} %refs_10_.1) | copy-start | bytes 12582916
  29.4 0.7 %copy-start.1 = (s32[24,7]{0,1:T(8,128)S(1)}, s32[24,7]{0,1:T(8,128)}, u32[]{:S(2)}) copy-start(s32[24,7]{0,1:T(8,128)} %param.6) | copy-start | bytes 2020

commit v2 on v1

v2 whole, which is shorter than its diff:
```python
import functools

import jax
import jax.numpy as jnp
from jax import lax
from jax.experimental import pallas as pl
from jax.experimental.pallas import tpu as pltpu
from jax.sharding import PartitionSpec as P

LANES = 128
SUB = 8
VMEM_LIMIT = 51 * 1024 * 1024


def product_kernel(group, places, *refs):
    own, other = refs[:4], refs[4:8]
    inc_own, inc_other, taper_hbm, out_ref = refs[8:12]
    tiles, pert, picked_from, picked, acc, sems = refs[12:]
    slots, block_size, _ = tiles.shape
    members = 4 * group
    rows = own[0].shape[1]
    pitch = pert.shape[0] // members
    quarters = block_size // LANES
    block_count = rows // quarters
    copies = []
    for s in range(slots):
        copies.append(pltpu.make_async_copy(taper_hbm.at[s], tiles.at[s], sems.at[s]))
        copies[-1].start()

    def weigh(side, groups, inc_ref):
        def chunk(r, carry):
            at = pl.multiple_of(r * SUB, SUB)
            states = [
                groups[g][j, pl.ds(at, SUB), :] for g in range(4) for j in range(group)
            ]
            total = states[0]
            for state in states[1:]:
                total = total + state
            mean = total * (1.0 / members)
            for m, state in enumerate(states):
                pert[pl.ds(m * pitch + at, SUB), :] = (
                    (state - mean).astype(jnp.bfloat16).astype(jnp.float32)
                )
            return carry

        lax.fori_loop(0, rows // SUB, chunk, 0, unroll=2)

        for i in range(block_count):
            for q in range(quarters):
                lanes = slice(q * LANES, (q + 1) * LANES)
                at = i * quarters + q
                inc = inc_ref[:, at * LANES : (at + 1) * LANES].astype(jnp.float32)
                part = pert[pl.ds(at, members, pitch), :] * inc
                picked_from[side * block_count + i, :, lanes] = part.astype(jnp.bfloat16)

    weigh(1, other, inc_other)
    weigh(0, own, inc_own)

    contract = (((1,), (1,)), ((), ()))
    copies[0].wait()
    vectors = block_count * members
    acc[...] = lax.dot_general(
        picked_from[0:block_count].reshape(vectors, block_size),
        tiles[0],
        contract,
        preferred_element_type=jnp.float32,
    )
    for s in range(1, slots):
        for i in range(block_count):
            rows_of = slice(i * members, (i + 1) * members)
            picked[s - 1, rows_of, :] = picked_from[places[s - 1, i]]
        copies[s].wait()
        acc[...] += lax.dot_general(
            picked[s - 1], tiles[s], contract, preferred_element_type=jnp.float32
        )

    scale = 1.0 / (members - 1)
    for i in range(block_count):
        for q in range(quarters):
            lanes = slice(q * LANES, (q + 1) * LANES)
            term = (
                pert[pl.ds(i * quarters + q, members, pitch), :]
                * acc[i * members : (i + 1) * members, lanes]
            )
            row = jnp.sum(term, axis=0, keepdims=True) * scale
            out_ref[:, i * block_size + q * LANES : i * block_size + (q + 1) * LANES] = row


def mover(lon_size, mem_size):
    def one(x, step, mem_of):
        perm = []
        for l in range(lon_size):
            for m in range(mem_size):
                source = ((l + step) % lon_size) * mem_size + mem_of(m)
                perm.append((source, l * mem_size + m))
        return lax.ppermute(x, ("lon", "mem"), perm)

    def move(x, across, mem_of):
        if not across:
            return one(x, 0, mem_of)
        if lon_size == 2:
            return one(x, 1, mem_of)
        axis = x.ndim - 2 if x.shape[-2] > 1 else x.ndim - 1
        right, left = jnp.split(x, 2, axis=axis)
        return jnp.concatenate([one(right, 1, mem_of), one(left, -1, mem_of)], axis=axis)

    return move


def on_device(ensemble, increments, offsets, taper):
    lon_size, mem_size = lax.axis_size("lon"), lax.axis_size("mem")
    group = mem_size // 4
    slots, block_size, _ = taper.shape
    block_count = offsets.shape[0]
    columns = ensemble.shape[1]
    rows = columns // LANES
    move = mover(lon_size, mem_size)

    state = ensemble.reshape(rows, LANES)
    inc_other = move(increments.reshape(1, columns), True, lambda m: m)
    lines = [[j + 4 * i for i in range(group)] for j in range(4)]
    sent = jnp.broadcast_to(state, (group, rows, LANES))
    mine = lax.all_to_all(sent, "mem", 0, 0, axis_index_groups=lines, tiled=True)
    inc_own = increments.astype(jnp.float32)
    places = jnp.arange(block_count, dtype=jnp.int32) + offsets.T
    places = jnp.where(places < 0, places + 2 * block_count, places)
    mine, inc_other, inc_own, places = lax.optimization_barrier(
        (mine, inc_other, inc_own, places)
    )
    groups = [
        mine,
        move(mine, False, lambda m: m ^ 2),
        move(mine, True, lambda m: m),
        move(mine, True, lambda m: m ^ 2),
    ]
    groups += [move(g, False, lambda m: m ^ 1) for g in groups]
    own = [groups[i] for i in (0, 1, 4, 5)]
    other = [groups[i] for i in (2, 3, 6, 7)]

    vectors = mem_size * block_count
    whole = pl.BlockSpec(memory_space=pltpu.VMEM)
    return pl.pallas_call(
        functools.partial(product_kernel, group),
        out_shape=jax.ShapeDtypeStruct((1, columns), jnp.float32),
        in_specs=[pl.BlockSpec(memory_space=pltpu.SMEM)]
        + [whole] * 10
        + [pl.BlockSpec(memory_space=pltpu.HBM)],
        out_specs=whole,
        scratch_shapes=[
            pltpu.VMEM((slots, block_size, block_size), jnp.bfloat16),
            pltpu.VMEM((mem_size * (rows + 1), LANES), jnp.float32),
            pltpu.VMEM((2 * block_count, mem_size, block_size), jnp.bfloat16),
            pltpu.VMEM((slots - 1, vectors, block_size), jnp.bfloat16),
            pltpu.VMEM((vectors, block_size), jnp.float32),
            pltpu.SemaphoreType.DMA((slots,)),
        ],
        compiler_params=pltpu.CompilerParams(vmem_limit_bytes=VMEM_LIMIT),
    )(places, *own, *other, inc_own, inc_other, taper)


def solution(mesh):
    return jax.shard_map(
        on_device,
        mesh=mesh,
        in_specs=(P("mem", "lon"), P("mem", "lon"), P("lon", None), P()),
        out_specs=P("mem", "lon"),
        check_vma=False,
    )
```

time: 36.2 us -> 31.8 us (0.88)
  waiting for transfers between devices: 13.2 us -> 11.6 us
  local copies, waits for them, and re-layouts: 2.87 us -> 1.48 us
  Pallas kernels: 5.81 us -> 4.9 us
  starting transfers between devices: 12.2 us -> 11.8 us
    ppermute x11 -> x8, starting transfers between devices: 12.2 us -> 5.52 us  [one(): return lax.ppermute(x, ('lon', 'mem'), perm)]
    all_to_all x0 -> x1, starting transfers between devices: none -> 6.32 us  [on_device(): lax.all_to_all(sent, 'mem', 0, 0, axis_index_groups=lines, tiled=True)]
    ppermute x11 -> x8, waiting for transfers between devices: 13.2 us -> 8.42 us  [one(): return lax.ppermute(x, ('lon', 'mem'), perm)]
    all_to_all x0 -> x1, waiting for transfers between devices: none -> 3.21 us  [on_device(): lax.all_to_all(sent, 'mem', 0, 0, axis_index_groups=lines, tiled=True)]
    unnamed x4 -> x0, local copies, waits for them, and re-layouts: 2.87 us -> none
    broadcast_in_dim x0 -> x1, local copies, waits for them, and re-layouts: none -> 1.48 us  [on_device(): sent = jnp.broadcast_to(state, (group, rows, LANES))]
    unnamed x1 -> x0, other arithmetic: 0.93 us -> none
    pallas_call x1, Pallas kernels: 5.81 us -> 4.9 us  [on_device(): pl.pallas_call(functools.partial(product_kernel, group), out_shape=jax.Sh...]
  transfers between devices with their start and end apart: 11 -> 9, of which waited for: 6 -> 6; matrix products, arithmetic and copies ran while one was open for 3% -> 5% of each run, Pallas kernels for 0% -> 0%
where the time goes in v2:
time: 31.8 us; the launch traced here: 31.4 us
  starting transfers between devices  11.8 us (37%)
  waiting for transfers between devices  11.6 us (36%)
  Pallas kernels  4.9 us (15%)
  other arithmetic  1.54 us (5%)
  local copies, waits for them, and re-layouts  1.48 us (5%)
    ppermute x8, waiting for transfers between devices, one(): return lax.ppermute(x, ('lon', 'mem'), perm)  8.42 us
    all_to_all x1, starting transfers between devices, on_device(): lax.all_to_all(sent, 'mem', 0, 0, axis_index_groups=lines, tiled=True)  6.32 us
    ppermute x8, starting transfers between devices, one(): return lax.ppermute(x, ('lon', 'mem'), perm)  5.52 us
    pallas_call x1, Pallas kernels, on_device(): pl.pallas_call(functools.partial(product_kernel, group), out_shape=jax.Sh...  4.9 us
    all_to_all x1, waiting for transfers between devices, on_device(): lax.all_to_all(sent, 'mem', 0, 0, axis_index_groups=lines, tiled=True)  3.21 us
    broadcast_in_dim x1, local copies, waits for them, and re-layouts, on_device(): sent = jnp.broadcast_to(state, (group, rows, LANES))  1.48 us
    convert_element_type x1, other arithmetic, on_device(): inc_own = increments.astype(jnp.float32)  0.85 us
    select_n x1, other arithmetic, on_device(): places = jnp.where(places < 0, places + 2 * block_count, places)  0.69 us
  transfers between devices with their start and end apart: 9, of which 6 were waited for; matrix products, arithmetic and copies ran while one was open for 5% of the time, Pallas kernels for 0%

profile of v2, /device:TPU:0, one launch (start us, length us, event | category | flops | bytes accessed | tf_op | source)
XLA Modules:
  0.0 31.4 jit_solution(17249704497890823299)
XLA Ops:
  0.0 1.5 %broadcast_in_dim.4 = f32[4,96,128]{2,1,0:T(8,128)} broadcast(f32[96,128]{1,0:T(8,128)} %bitcast.5), dimensions={1,2} | broadcast | bytes 245760 | tf_op jit(solution)/shard_map/broadcast_in_dim | solution.py:122
  1.5 6.3 %all-to-all-start = ((f32[4,96,128]{2,1,0:T(8,128)}), f32[4,96,128]{2,1,0:T(8,128)S(1)}, u32[]{:S(2)}, u32[]{:S(2)}) async-start(f32[4,96,128]{2,1,0:T(8,128)} %broadcast_in_dim.4), calls=%async_computation | async-start | bytes 393216 | tf_op jit(solution)/shard_map/all_to_all | solution.py:123
  7.8 1.5 %collective-permute-start = (bf16[1,12288]{1,0:T(2,128)(2,1)}, bf16[1,12288]{1,0:T(2,128)(2,1)S(1)}, u32[]{:S(2)}, u32[]{:S(2)}) collective-permute-start(bf16[1,12288]{1,0:T(2,128)(2,1)} %param.5), channel_id=1, source_target_pairs={{16,0},{17,1},{18,2},{19,3},{20,4},{21,5},{22,6},{23,7},{24,8},{25... | collective-permute-start | bytes 73736 | tf_op jit(solution)/shard_map/ppermute | solution.py:96
  9.3 0.7 %compare_select_fusion.places = s32[7,24]{1,0:T(8,128)S(1)} fusion(s32[24,7]{0,1:T(8,128)} %param.6), kind=kLoop, calls=%fused_computation | loop fusion | flops 672 | bytes 1344 | tf_op jit(solution)/shard_map/jit(_where)/select_n | solution.py:126
  10.0 0.8 %convert_element_type.3.refs_8_ = f32[1,12288]{1,0:T(1,128)S(1)} convert(bf16[1,12288]{1,0:T(2,128)(2,1)} %param.5) | non-fusion elementwise | flops 12288 | bytes 73728 | tf_op jit(solution)/shard_map/convert_element_type | solution.py:124
  10.9 1.2 %collective-permute-done.refs_9_ = bf16[1,12288]{1,0:T(2,128)(2,1)S(1)} collective-permute-done((bf16[1,12288]{1,0:T(2,128)(2,1)}, bf16[1,12288]{1,0:T(2,128)(2,1)S(1)}, u32[]{:S(2)}, u32[]{:S(2)}) %collective-permute-start) | collective-permute-done | bytes 24608 | tf_op jit(solution)/shard_map/ppermute | solution.py:96
  12.1 3.2 %all-to-all-done.refs_0_ = f32[4,96,128]{2,1,0:T(8,128)S(1)} async-done(((f32[4,96,128]{2,1,0:T(8,128)}), f32[4,96,128]{2,1,0:T(8,128)S(1)}, u32[]{:S(2)}, u32[]{:S(2)}) %all-to-all-start) | async-done | bytes 196640 | tf_op jit(solution)/shard_map/all_to_all | solution.py:123
  15.3 2.4 %collective-permute-start.5 = (f32[4,96,128]{2,1,0:T(8,128)S(1)}, f32[4,96,128]{2,1,0:T(8,128)S(1)}, u32[]{:S(2)}, u32[]{:S(2)}) collective-permute-start(f32[4,96,128]{2,1,0:T(8,128)S(1)} %all-to-all-done.refs_0_), channel_id=1, source_target_pairs={{18,0},{19,1},{16,2},{17,3},{22,4},{23,5},{20,6},{21,7},{26,8},{27... | collective-permute-start | bytes 589832 | tf_op jit(solution)/shard_map/ppermute | solution.py:96
  17.8 0.5 %collective-permute-start.4 = (f32[4,96,128]{2,1,0:T(8,128)S(1)}, f32[4,96,128]{2,1,0:T(8,128)S(1)}, u32[]{:S(2)}, u32[]{:S(2)}) collective-permute-start(f32[4,96,128]{2,1,0:T(8,128)S(1)} %all-to-all-done.refs_0_), channel_id=1, source_target_pairs={{16,0},{17,1},{18,2},{19,3},{20,4},{21,5},{22,6},{23,7},{24,8},{25... | collective-permute-start | bytes 589832 | tf_op jit(solution)/shard_map/ppermute | solution.py:96
  18.3 0.5 %collective-permute-start.1 = (f32[4,96,128]{2,1,0:T(8,128)S(1)}, f32[4,96,128]{2,1,0:T(8,128)S(1)}, u32[]{:S(2)}, u32[]{:S(2)}) collective-permute-start(f32[4,96,128]{2,1,0:T(8,128)S(1)} %all-to-all-done.refs_0_), channel_id=1, source_target_pairs={{2,0},{3,1},{0,2},{1,3},{6,4},{7,5},{4,6},{5,7},{10,8},{11,9},{8,1... | collective-permute-start | bytes 589832 | tf_op jit(solution)/shard_map/ppermute | solution.py:96
  18.8 0.0 collective-permute-start.2
  18.8 4.0 %collective-permute-done.5.refs_5_ = f32[4,96,128]{2,1,0:T(8,128)S(1)} collective-permute-done((f32[4,96,128]{2,1,0:T(8,128)S(1)}, f32[4,96,128]{2,1,0:T(8,128)S(1)}, u32[]{:S(2)}, u32[]{:S(2)}) %collective-permute-start.5) | collective-permute-done | bytes 196640 | tf_op jit(solution)/shard_map/ppermute | solution.py:96
  22.8 0.0 collective-permute-start.7
  22.8 1.9 %collective-permute-done.4.refs_4_ = f32[4,96,128]{2,1,0:T(8,128)S(1)} collective-permute-done((f32[4,96,128]{2,1,0:T(8,128)S(1)}, f32[4,96,128]{2,1,0:T(8,128)S(1)}, u32[]{:S(2)}, u32[]{:S(2)}) %collective-permute-start.4) | collective-permute-done | bytes 196640 | tf_op jit(solution)/shard_map/ppermute | solution.py:96
  24.8 0.0 collective-permute-start.6
  24.8 0.0 collective-permute-done.1.refs_1_
  24.8 0.5 %collective-permute-start.3 = (f32[4,96,128]{2,1,0:T(8,128)S(1)}, f32[4,96,128]{2,1,0:T(8,128)S(1)}, u32[]{:S(2)}, u32[]{:S(2)}) collective-permute-start(f32[4,96,128]{2,1,0:T(8,128)S(1)} %collective-permute-done.1.refs_1_), channel_id=1, source_target_pairs={{1,0},{0,1},{3,2},{2,3},{5,4},{4,5},{7,6},{6,7},{9,8},{8,9},{11,10... | collective-permute-start | bytes 589832 | tf_op jit(solution)/shard_map/ppermute | solution.py:96
  25.3 0.0 collective-permute-done.2.refs_2_
  25.3 0.0 collective-permute-done.7.refs_7_
  25.3 0.9 %collective-permute-done.6.refs_6_ = f32[4,96,128]{2,1,0:T(8,128)S(1)} collective-permute-done((f32[4,96,128]{2,1,0:T(8,128)S(1)}, f32[4,96,128]{2,1,0:T(8,128)S(1)}, u32[]{:S(2)}, u32[]{:S(2)}) %collective-permute-start.6) | collective-permute-done | bytes 196640 | tf_op jit(solution)/shard_map/ppermute | solution.py:96
  26.2 0.3 collective-permute-done.3.refs_3_
  26.5 4.9 %shard_map.46 = f32[1,12288]{1,0:T(1,128)} custom-call(s32[7,24]{1,0:T(8,128)S(1)} %compare_select_fusion.places, f32[4,96,128]{2,1,0:T(8,128)S(1)} %all-to-all-done.refs_0_, f32[4,96,128]{2,1,0:T(8,128)S(1)} %collective-permute-done.1.refs_1_, f32[4,96,128]{2,1,0:T(8,128)S(1)} %collective-permute-done.2.refs_2_, ...), custom_call_target="tpu_custom_call" | custom-call | tf_op jit(solution)/shard_map/pallas_call | solution.py:142
Async XLA Ops:
  1.5 13.8 %all-to-all-start = ((f32[4,96,128]{2,1,0:T(8,128)}), f32[4,96,128]{2,1,0:T(8,128)S(1)}, u32[]{:S(2)}, u32[]{:S(2)}) async-start(f32[4,96,128]{2,1,0:T(8,128)} %broadcast_in_dim.4), calls=%async_computation | async-start | bytes 393216 | tf_op jit(solution)/shard_map/all_to_all | solution.py:123
  7.8 4.3 %collective-permute-start = (bf16[1,12288]{1,0:T(2,128)(2,1)}, bf16[1,12288]{1,0:T(2,128)(2,1)S(1)}, u32[]{:S(2)}, u32[]{:S(2)}) collective-permute-start(bf16[1,12288]{1,0:T(2,128)(2,1)} %param.5), channel_id=1, source_target_pairs={{16,0},{17,1},{18,2},{19,3},{20,4},{21,5},{22,6},{23,7},{24,8},{25... | collective-permute-start | bytes 73736 | tf_op jit(solution)/shard_map/ppermute | solution.py:96
  15.3 7.5 %collective-permute-start.5 = (f32[4,96,128]{2,1,0:T(8,128)S(1)}, f32[4,96,128]{2,1,0:T(8,128)S(1)}, u32[]{:S(2)}, u32[]{:S(2)}) collective-permute-start(f32[4,96,128]{2,1,0:T(8,128)S(1)} %all-to-all-done.refs_0_), channel_id=1, source_target_pairs={{18,0},{19,1},{16,2},{17,3},{22,4},{23,5},{20,6},{21,7},{26,8},{27... | collective-permute-start | bytes 589832 | tf_op jit(solution)/shard_map/ppermute | solution.py:96
  17.8 7.0 %collective-permute-start.4 = (f32[4,96,128]{2,1,0:T(8,128)S(1)}, f32[4,96,128]{2,1,0:T(8,128)S(1)}, u32[]{:S(2)}, u32[]{:S(2)}) collective-permute-start(f32[4,96,128]{2,1,0:T(8,128)S(1)} %all-to-all-done.refs_0_), channel_id=1, source_target_pairs={{16,0},{17,1},{18,2},{19,3},{20,4},{21,5},{22,6},{23,7},{24,8},{25... | collective-permute-start | bytes 589832 | tf_op jit(solution)/shard_map/ppermute | solution.py:96
  18.3 6.5 %collective-permute-start.1 = (f32[4,96,128]{2,1,0:T(8,128)S(1)}, f32[4,96,128]{2,1,0:T(8,128)S(1)}, u32[]{:S(2)}, u32[]{:S(2)}) collective-permute-start(f32[4,96,128]{2,1,0:T(8,128)S(1)} %all-to-all-done.refs_0_), channel_id=1, source_target_pairs={{2,0},{3,1},{0,2},{1,3},{6,4},{7,5},{4,6},{5,7},{10,8},{11,9},{8,1... | collective-permute-start | bytes 589832 | tf_op jit(solution)/shard_map/ppermute | solution.py:96
  18.8 6.5 %collective-permute-start.2 = (f32[4,96,128]{2,1,0:T(8,128)S(1)}, f32[4,96,128]{2,1,0:T(8,128)S(1)}, u32[]{:S(2)}, u32[]{:S(2)}) collective-permute-start(f32[4,96,128]{2,1,0:T(8,128)S(1)} %all-to-all-done.refs_0_), channel_id=1, source_target_pairs={{1,0},{0,1},{3,2},{2,3},{5,4},{4,5},{7,6},{6,7},{9,8},{8,9},{11,10... | collective-permute-start | bytes 589832 | tf_op jit(solution)/shard_map/ppermute | solution.py:96
  22.8 2.5 %collective-permute-start.7 = (f32[4,96,128]{2,1,0:T(8,128)S(1)}, f32[4,96,128]{2,1,0:T(8,128)S(1)}, u32[]{:S(2)}, u32[]{:S(2)}) collective-permute-start(f32[4,96,128]{2,1,0:T(8,128)S(1)} %collective-permute-done.5.refs_5_), channel_id=1, source_target_pairs={{1,0},{0,1},{3,2},{2,3},{5,4},{4,5},{7,6},{6,7},{9,8},{8,9},{11,10... | collective-permute-start | bytes 589832 | tf_op jit(solution)/shard_map/ppermute | solution.py:96
  24.8 1.4 %collective-permute-start.6 = (f32[4,96,128]{2,1,0:T(8,128)S(1)}, f32[4,96,128]{2,1,0:T(8,128)S(1)}, u32[]{:S(2)}, u32[]{:S(2)}) collective-permute-start(f32[4,96,128]{2,1,0:T(8,128)S(1)} %collective-permute-done.4.refs_4_), channel_id=1, source_target_pairs={{1,0},{0,1},{3,2},{2,3},{5,4},{4,5},{7,6},{6,7},{9,8},{8,9},{11,10... | collective-permute-start | bytes 589832 | tf_op jit(solution)/shard_map/ppermute | solution.py:96
  24.8 1.7 %collective-permute-start.3 = (f32[4,96,128]{2,1,0:T(8,128)S(1)}, f32[4,96,128]{2,1,0:T(8,128)S(1)}, u32[]{:S(2)}, u32[]{:S(2)}) collective-permute-start(f32[4,96,128]{2,1,0:T(8,128)S(1)} %collective-permute-done.1.refs_1_), channel_id=1, source_target_pairs={{1,0},{0,1},{3,2},{2,3},{5,4},{4,5},{7,6},{6,7},{9,8},{8,9},{11,10... | collective-permute-start | bytes 589832 | tf_op jit(solution)/shard_map/ppermute | solution.py:96

commit v3 on v2

--- a/solution.py
+++ b/solution.py
@@ -13,12 +13,12 @@
 
 
 def product_kernel(group, places, *refs):
-    own, other = refs[:4], refs[4:8]
-    inc_own, inc_other, taper_hbm, out_ref = refs[8:12]
-    tiles, pert, picked_from, picked, acc, sems = refs[12:]
+    own, other = (refs[:4], refs[4:8]), (refs[8:12], refs[12:16])
+    inc_own, inc_other, taper_hbm, out_ref = refs[16:20]
+    tiles, pert, picked_from, picked, acc, sems = refs[20:]
     slots, block_size, _ = tiles.shape
     members = 4 * group
-    rows = own[0].shape[1]
+    rows = own[0][0].shape[0]
     pitch = pert.shape[0] // members
     quarters = block_size // LANES
     block_count = rows // quarters
@@ -27,23 +27,25 @@
         copies.append(pltpu.make_async_copy(taper_hbm.at[s], tiles.at[s], sems.at[s]))
         copies[-1].start()
 
-    def weigh(side, groups, inc_ref):
+    def weigh(side, bases, diffs, inc_ref):
         def chunk(r, carry):
-            at = pl.multiple_of(r * SUB, SUB)
-            states = [
-                groups[g][j, pl.ds(at, SUB), :] for g in range(4) for j in range(group)
+            at = pl.multiple_of(r * 2 * SUB, 2 * SUB)
+            starts = [ref[pl.ds(at, 2 * SUB), :] for ref in bases]
+            steps = [
+                [ref[j, pl.ds(at, 2 * SUB), :].astype(jnp.float32) for j in range(group - 1)]
+                for ref in diffs
             ]
-            total = states[0]
-            for state in states[1:]:
-                total = total + state
+            total = sum(step for line in steps for step in line) + group * sum(starts)
             mean = total * (1.0 / members)
-            for m, state in enumerate(states):
-                pert[pl.ds(m * pitch + at, SUB), :] = (
-                    (state - mean).astype(jnp.bfloat16).astype(jnp.float32)
-                )
+            m = 0
+            for start, line in zip(starts, steps):
+                start = start - mean
+                for value in [start] + [start + step for step in line]:
+                    pert[pl.ds(m * pitch + at, 2 * SUB), :] = value
+                    m += 1
             return carry
 
-        lax.fori_loop(0, rows // SUB, chunk, 0, unroll=2)
+        lax.fori_loop(0, rows // (2 * SUB), chunk, 0, unroll=2)
 
         for i in range(block_count):
             for q in range(quarters):
@@ -53,8 +55,8 @@
                 part = pert[pl.ds(at, members, pitch), :] * inc
                 picked_from[side * block_count + i, :, lanes] = part.astype(jnp.bfloat16)
 
-    weigh(1, other, inc_other)
-    weigh(0, own, inc_own)
+    weigh(1, *other, inc_other)
+    weigh(0, *own, inc_own)
 
     contract = (((1,), (1,)), ((), ()))
     copies[0].wait()
@@ -115,27 +117,38 @@
     columns = ensemble.shape[1]
     rows = columns // LANES
     move = mover(lon_size, mem_size)
+    same, beside = (lambda m: m), (lambda m: m ^ 2)
 
-    state = ensemble.reshape(rows, LANES)
-    inc_other = move(increments.reshape(1, columns), True, lambda m: m)
-    lines = [[j + 4 * i for i in range(group)] for j in range(4)]
-    sent = jnp.broadcast_to(state, (group, rows, LANES))
-    mine = lax.all_to_all(sent, "mem", 0, 0, axis_index_groups=lines, tiled=True)
+    base = ensemble.reshape(rows, LANES)
+    inc_other = move(increments.reshape(1, columns), True, same)
+    partner = move(base, False, lambda m: m ^ 1)
+    bases = [
+        move(base, False, beside),
+        move(base, True, same),
+        move(base, True, beside),
+    ]
+    line = [
+        move(base, False, lambda m: (m + 4 * d) % mem_size) for d in reversed(range(1, group))
+    ]
     inc_own = increments.astype(jnp.float32)
     places = jnp.arange(block_count, dtype=jnp.int32) + offsets.T
     places = jnp.where(places < 0, places + 2 * block_count, places)
-    mine, inc_other, inc_own, places = lax.optimization_barrier(
-        (mine, inc_other, inc_own, places)
+    line, bases, partner, inc_other, inc_own, places = lax.optimization_barrier(
+        (line, bases, partner, inc_other, inc_own, places)
     )
-    groups = [
-        mine,
-        move(mine, False, lambda m: m ^ 2),
-        move(mine, True, lambda m: m),
-        move(mine, True, lambda m: m ^ 2),
+
+    diff = (jnp.stack(line) - base[None]).astype(jnp.bfloat16)
+    base = jnp.where(places[0, 0] < 2 * block_count, base, 0.0)
+    diffs = [
+        diff,
+        move(diff, False, beside),
+        move(diff, True, same),
+        move(diff, True, beside),
     ]
-    groups += [move(g, False, lambda m: m ^ 1) for g in groups]
-    own = [groups[i] for i in (0, 1, 4, 5)]
-    other = [groups[i] for i in (2, 3, 6, 7)]
+    bases = [base] + bases + [partner] + [move(x, False, lambda m: m ^ 1) for x in bases]
+    diffs += [move(x, False, lambda m: m ^ 1) for x in diffs]
+    own, other = (0, 1, 4, 5), (2, 3, 6, 7)
+    operands = [arrays[i] for side in (own, other) for arrays in (bases, diffs) for i in side]
 
     vectors = mem_size * block_count
     whole = pl.BlockSpec(memory_space=pltpu.VMEM)
@@ -143,7 +156,7 @@
         functools.partial(product_kernel, group),
         out_shape=jax.ShapeDtypeStruct((1, columns), jnp.float32),
         in_specs=[pl.BlockSpec(memory_space=pltpu.SMEM)]
-        + [whole] * 10
+        + [whole] * 18
         + [pl.BlockSpec(memory_space=pltpu.HBM)],
         out_specs=whole,
         scratch_shapes=[
@@ -155,7 +168,7 @@
             pltpu.SemaphoreType.DMA((slots,)),
         ],
         compiler_params=pltpu.CompilerParams(vmem_limit_bytes=VMEM_LIMIT),
-    )(places, *own, *other, inc_own, inc_other, taper)
+    )(places, *operands, inc_own, inc_other, taper)
 
 
 def solution(mesh):

time: 31.8 us -> 32.3 us (1.016)
  waiting for transfers between devices: 11.6 us -> 6.63 us
  starting transfers between devices: 11.8 us -> 16 us
  other arithmetic: 1.54 us -> 3.16 us
  local copies, waits for them, and re-layouts: 1.48 us -> 0.51 us
  between operations: 0.01 us -> 0.74 us
    ppermute x8 -> x18, starting transfers between devices: 5.52 us -> 16 us  [one(): return lax.ppermute(x, ('lon', 'mem'), perm)]
    all_to_all x1 -> x0, starting transfers between devices: 6.32 us -> none  [on_device(): lax.all_to_all(sent, 'mem', 0, 0, axis_index_groups=lines, tiled=True)]
    all_to_all x1 -> x0, waiting for transfers between devices: 3.21 us -> none  [on_device(): lax.all_to_all(sent, 'mem', 0, 0, axis_index_groups=lines, tiled=True)]
    ppermute x8 -> x18, waiting for transfers between devices: 8.42 us -> 6.63 us  [one(): return lax.ppermute(x, ('lon', 'mem'), perm)]
    broadcast_in_dim x1 -> x0, local copies, waits for them, and re-layouts: 1.48 us -> none  [on_device(): sent = jnp.broadcast_to(state, (group, rows, LANES))]
    convert_element_type x0 -> x1, other arithmetic: none -> 0.81 us  [on_device(): diff = (jnp.stack(line) - base[None]).astype(jnp.bfloat16)]
    select_n x0 -> x1, other arithmetic: none -> 0.8 us  [on_device(): base = jnp.where(places[0, 0] < 2 * block_count, base, 0.0)]
    slice x0 -> x1, local copies, waits for them, and re-layouts: none -> 0.51 us  [on_device(): base = jnp.where(places[0, 0] < 2 * block_count, base, 0.0)]
  transfers between devices with their start and end apart: 9 -> 18, of which waited for: 6 -> 6; matrix products, arithmetic and copies ran while one was open for 5% -> 9% of each run, Pallas kernels for 0% -> 0%
where the time goes in v3:
time: 32.3 us; the launch traced here: 32 us
  starting transfers between devices  16 us (50%)
  waiting for transfers between devices  6.63 us (21%)
  Pallas kernels  4.9 us (15%)
  other arithmetic  3.16 us (10%)
  between operations  0.74 us (2%)
  local copies, waits for them, and re-layouts  0.51 us (2%)
    ppermute x18, starting transfers between devices, one(): return lax.ppermute(x, ('lon', 'mem'), perm)  16 us
    ppermute x18, waiting for transfers between devices, one(): return lax.ppermute(x, ('lon', 'mem'), perm)  6.63 us
    pallas_call x1, Pallas kernels, on_device(): pl.pallas_call(functools.partial(product_kernel, group), out_shape=jax.Sh...  4.9 us
    convert_element_type x1, other arithmetic, on_device(): inc_own = increments.astype(jnp.float32)  0.85 us
    convert_element_type x1, other arithmetic, on_device(): diff = (jnp.stack(line) - base[None]).astype(jnp.bfloat16)  0.81 us
    select_n x1, other arithmetic, on_device(): base = jnp.where(places[0, 0] < 2 * block_count, base, 0.0)  0.8 us
    select_n x1, other arithmetic, on_device(): places = jnp.where(places < 0, places + 2 * block_count, places)  0.69 us
  transfers between devices with their start and end apart: 18, of which 6 were waited for; matrix products, arithmetic and copies ran while one was open for 9% of the time, Pallas kernels for 0%

profile of v3, /device:TPU:0, one launch (start us, length us, event | category | flops | bytes accessed | tf_op | source)
XLA Modules:
  0.0 32.0 jit_solution(8915739388169875390)
XLA Ops:
  0.0 0.5 %collective-permute-start.6 = (f32[96,128]{1,0:T(8,128)}, f32[96,128]{1,0:T(8,128)S(1)}, u32[]{:S(2)}, u32[]{:S(2)}) collective-permute-start(f32[96,128]{1,0:T(8,128)} %bitcast.9), channel_id=1, source_target_pairs={{1,0},{0,1},{3,2},{2,3},{5,4},{4,5},{7,6},{6,7},{9,8},{8,9},{11,10... | collective-permute-start | bytes 147464 | tf_op jit(solution)/shard_map/ppermute | solution.py:98
  0.5 3.4 %collective-permute-start.5 = (f32[96,128]{1,0:T(8,128)}, f32[96,128]{1,0:T(8,128)S(1)}, u32[]{:S(2)}, u32[]{:S(2)}) collective-permute-start(f32[96,128]{1,0:T(8,128)} %bitcast.10), channel_id=1, source_target_pairs={{18,0},{19,1},{16,2},{17,3},{22,4},{23,5},{20,6},{21,7},{26,8},{27... | collective-permute-start | bytes 147464 | tf_op jit(solution)/shard_map/ppermute | solution.py:98
  3.9 0.5 %collective-permute-start.7 = (bf16[1,12288]{1,0:T(2,128)(2,1)}, bf16[1,12288]{1,0:T(2,128)(2,1)S(1)}, u32[]{:S(2)}, u32[]{:S(2)}) collective-permute-start(bf16[1,12288]{1,0:T(2,128)(2,1)} %param.5), channel_id=1, source_target_pairs={{16,0},{17,1},{18,2},{19,3},{20,4},{21,5},{22,6},{23,7},{24,8},{25... | collective-permute-start | bytes 73736 | tf_op jit(solution)/shard_map/ppermute | solution.py:98
  4.4 1.5 %collective-permute-start.4 = (f32[96,128]{1,0:T(8,128)}, f32[96,128]{1,0:T(8,128)S(1)}, u32[]{:S(2)}, u32[]{:S(2)}) collective-permute-start(f32[96,128]{1,0:T(8,128)} %bitcast.11), channel_id=1, source_target_pairs={{16,0},{17,1},{18,2},{19,3},{20,4},{21,5},{22,6},{23,7},{24,8},{25... | collective-permute-start | bytes 147464 | tf_op jit(solution)/shard_map/ppermute | solution.py:98
  5.9 0.5 %collective-permute-start.3 = (f32[96,128]{1,0:T(8,128)}, f32[96,128]{1,0:T(8,128)S(1)}, u32[]{:S(2)}, u32[]{:S(2)}) collective-permute-start(f32[96,128]{1,0:T(8,128)} %bitcast.12), channel_id=1, source_target_pairs={{2,0},{3,1},{0,2},{1,3},{6,4},{7,5},{4,6},{5,7},{10,8},{11,9},{8,1... | collective-permute-start | bytes 147464 | tf_op jit(solution)/shard_map/ppermute | solution.py:98
  6.5 2.0 %collective-permute-done.7.refs_17_ = bf16[1,12288]{1,0:T(2,128)(2,1)S(1)} collective-permute-done((bf16[1,12288]{1,0:T(2,128)(2,1)}, bf16[1,12288]{1,0:T(2,128)(2,1)S(1)}, u32[]{:S(2)}, u32[]{:S(2)}) %collective-permute-start.7) | collective-permute-done | bytes 24608 | tf_op jit(solution)/shard_map/ppermute | solution.py:98
  8.5 3.6 %collective-permute-start.2 = (f32[96,128]{1,0:T(8,128)}, f32[96,128]{1,0:T(8,128)S(1)}, u32[]{:S(2)}, u32[]{:S(2)}) collective-permute-start(f32[96,128]{1,0:T(8,128)} %bitcast.13), channel_id=1, source_target_pairs={{4,0},{5,1},{6,2},{7,3},{8,4},{9,5},{10,6},{11,7},{12,8},{13,9},{1... | collective-permute-start | bytes 147464 | tf_op jit(solution)/shard_map/ppermute | solution.py:98
  12.1 0.0 collective-permute-done.6.refs_2_
  12.1 0.0 collective-permute-start.1
  12.1 0.0 collective-permute-done.5.refs_9_
  12.1 1.0 %collective-permute-start = (f32[96,128]{1,0:T(8,128)}, f32[96,128]{1,0:T(8,128)S(1)}, u32[]{:S(2)}, u32[]{:S(2)}) collective-permute-start(f32[96,128]{1,0:T(8,128)} %bitcast.15), channel_id=1, source_target_pairs={{12,0},{13,1},{14,2},{15,3},{0,4},{1,5},{2,6},{3,7},{4,8},{5,9},{6... | collective-permute-start | bytes 147464 | tf_op jit(solution)/shard_map/ppermute | solution.py:98
  13.1 0.7 %compare_select_fusion.places = s32[7,24]{1,0:T(8,128)S(1)} fusion(s32[24,7]{0,1:T(8,128)} %param.6), kind=kLoop, calls=%fused_computation.3 | loop fusion | flops 672 | bytes 1344 | tf_op jit(solution)/shard_map/jit(_where)/select_n | solution.py:135
  13.8 0.8 %convert_element_type.6.refs_16_ = f32[1,12288]{1,0:T(1,128)S(1)} convert(bf16[1,12288]{1,0:T(2,128)(2,1)} %param.5) | non-fusion elementwise | flops 12288 | bytes 73728 | tf_op jit(solution)/shard_map/convert_element_type | solution.py:133
  14.7 0.0 collective-permute-done.4.refs_8_
  14.7 0.0 collective-permute-done.3.refs_1_
  14.7 0.0 collective-permute-done.2
  14.7 2.6 %collective-permute-done.1 = f32[96,128]{1,0:T(8,128)S(1)} collective-permute-done((f32[96,128]{1,0:T(8,128)}, f32[96,128]{1,0:T(8,128)S(1)}, u32[]{:S(2)}, u32[]{:S(2)}) %collective-permute-start.1) | collective-permute-done | bytes 49184 | tf_op jit(solution)/shard_map/ppermute | solution.py:98
  17.3 1.0 %collective-permute-done = f32[96,128]{1,0:T(8,128)S(1)} collective-permute-done((f32[96,128]{1,0:T(8,128)}, f32[96,128]{1,0:T(8,128)S(1)}, u32[]{:S(2)}, u32[]{:S(2)}) %collective-permute-start) | collective-permute-done | bytes 49184 | tf_op jit(solution)/shard_map/ppermute | solution.py:98
  18.3 0.8 %fusion.refs_4_ = bf16[3,96,128]{2,1,0:T(8,128)(2,1)S(1)} fusion(f32[1,96,128]{2,1,0:T(8,128)S(1)} %bitcast.18, f32[1,96,128]{2,1,0:T(8,128)S(1)} %bitcast.19, f32[1,96,128]{2,1,0:T(8,128)S(1)} %bitcast.20, f32[96,128]{1,0:T(8,128)} %bitcast.16), kind=kLoop, calls=%fused_computation.1 | loop fusion | flops 147456 | bytes 270336 | tf_op jit(solution)/shard_map/convert_element_type | solution.py:140
  19.1 1.7 %collective-permute-start.15 = (bf16[3,96,128]{2,1,0:T(8,128)(2,1)S(1)}, bf16[3,96,128]{2,1,0:T(8,128)(2,1)S(1)}, u32[]{:S(2)}, u32[]{:S(2)}) collective-permute-start(bf16[3,96,128]{2,1,0:T(8,128)(2,1)S(1)} %fusion.refs_4_), channel_id=1, source_target_pairs={{18,0},{19,1},{16,2},{17,3},{22,4},{23,5},{20,6},{21,7},{26,8},{27... | collective-permute-start | bytes 221192 | tf_op jit(solution)/shard_map/ppermute | solution.py:98
  20.8 0.6 %collective-permute-start.14 = (bf16[3,96,128]{2,1,0:T(8,128)(2,1)S(1)}, bf16[3,96,128]{2,1,0:T(8,128)(2,1)S(1)}, u32[]{:S(2)}, u32[]{:S(2)}) collective-permute-start(bf16[3,96,128]{2,1,0:T(8,128)(2,1)S(1)} %fusion.refs_4_), channel_id=1, source_target_pairs={{16,0},{17,1},{18,2},{19,3},{20,4},{21,5},{22,6},{23,7},{24,8},{25... | collective-permute-start | bytes 221192 | tf_op jit(solution)/shard_map/ppermute | solution.py:98
  21.4 1.2 %collective-permute-start.9 = (bf16[3,96,128]{2,1,0:T(8,128)(2,1)S(1)}, bf16[3,96,128]{2,1,0:T(8,128)(2,1)S(1)}, u32[]{:S(2)}, u32[]{:S(2)}) collective-permute-start(bf16[3,96,128]{2,1,0:T(8,128)(2,1)S(1)} %fusion.refs_4_), channel_id=1, source_target_pairs={{2,0},{3,1},{0,2},{1,3},{6,4},{7,5},{4,6},{5,7},{10,8},{11,9},{8,1... | collective-permute-start | bytes 221192 | tf_op jit(solution)/shard_map/ppermute | solution.py:98
  22.6 0.0 collective-permute-start.8
  22.7 0.5 %collective-permute-start.12 = (f32[96,128]{1,0:T(8,128)S(1)}, f32[96,128]{1,0:T(8,128)S(1)}, u32[]{:S(2)}, u32[]{:S(2)}) collective-permute-start(f32[96,128]{1,0:T(8,128)S(1)} %collective-permute-done.4.refs_8_), channel_id=1, source_target_pairs={{1,0},{0,1},{3,2},{2,3},{5,4},{4,5},{7,6},{6,7},{9,8},{8,9},{11,10... | collective-permute-start | bytes 147464 | tf_op jit(solution)/shard_map/ppermute | solution.py:98
  23.2 0.5 %slice.3 = s32[1,1]{1,0:T(1,128)} slice(s32[7,24]{1,0:T(8,128)S(1)} %compare_select_fusion.places), slice={[0:1], [0:1]} | slice | bytes 8 | tf_op jit(solution)/shard_map/slice | solution.py:141
  24.3 0.0 collective-permute-done.8.refs_3_
  24.3 0.1 collective-permute-start.10
  24.4 0.0 collective-permute-done.12.refs_10_
  24.4 0.5 %collective-permute-start.13 = (f32[96,128]{1,0:T(8,128)S(1)}, f32[96,128]{1,0:T(8,128)S(1)}, u32[]{:S(2)}, u32[]{:S(2)}) collective-permute-start(f32[96,128]{1,0:T(8,128)S(1)} %collective-permute-done.5.refs_9_), channel_id=1, source_target_pairs={{1,0},{0,1},{3,2},{2,3},{5,4},{4,5},{7,6},{6,7},{9,8},{8,9},{11,10... | collective-permute-start | bytes 147464 | tf_op jit(solution)/shard_map/ppermute | solution.py:98
  24.9 0.0 collective-permute-done.15.refs_13_
  24.9 0.1 collective-permute-start.17
  25.0 0.2 collective-permute-done.14.refs_12_
  25.2 0.2 collective-permute-start.16
  25.4 0.4 %collective-permute-done.9.refs_5_ = bf16[3,96,128]{2,1,0:T(8,128)(2,1)S(1)} collective-permute-done((bf16[3,96,128]{2,1,0:T(8,128)(2,1)S(1)}, bf16[3,96,128]{2,1,0:T(8,128)(2,1)S(1)}, u32[]{:S(2)}, u32[]{:S(2)}) %collective-permute-start.9) | collective-permute-done | bytes 73760 | tf_op jit(solution)/shard_map/ppermute | solution.py:98
  25.8 0.0 collective-permute-start.11
  25.8 0.8 %broadcast_select_fusion.refs_0_ = f32[96,128]{1,0:T(8,128)S(1)} fusion(f32[96,128]{1,0:T(8,128)} %bitcast.17, pred[]{:T(512)} %bitcast.2), kind=kLoop, calls=%fused_computation.2 | loop fusion | flops 12288 | bytes 98305 | tf_op jit(solution)/shard_map/jit(_where)/select_n | solution.py:141
  26.6 0.0 collective-permute-done.13.refs_11_
  26.6 0.0 collective-permute-done.10.refs_6_
  26.6 0.0 collective-permute-done.17.refs_15_
  26.6 0.0 collective-permute-done.16.refs_14_
  26.6 0.4 %collective-permute-done.11.refs_7_ = bf16[3,96,128]{2,1,0:T(8,128)(2,1)S(1)} collective-permute-done((bf16[3,96,128]{2,1,0:T(8,128)(2,1)S(1)}, bf16[3,96,128]{2,1,0:T(8,128)(2,1)S(1)}, u32[]{:S(2)}, u32[]{:S(2)}) %collective-permute-start.11) | collective-permute-done | bytes 73760 | tf_op jit(solution)/shard_map/ppermute | solution.py:98
  27.1 4.9 %shard_map.46 = f32[1,12288]{1,0:T(1,128)} custom-call(s32[7,24]{1,0:T(8,128)S(1)} %compare_select_fusion.places, f32[96,128]{1,0:T(8,128)S(1)} %broadcast_select_fusion.refs_0_, f32[96,128]{1,0:T(8,128)S(1)} %collective-permute-done.3.refs_1_, f32[96,128]{1,0:T(8,128)S(1)} %collective-permute-done.6.refs_2_, f32[96,128]{1,0:T(8,128)S(1)} %collective-permute-done.8.refs_3_, ...), custom_call_target="tpu_custom_call" | custom-call | tf_op jit(solution)/shard_map/pallas_call | solution.py:155
Async XLA Ops:
  0.0 12.1 %collective-permute-start.6 = (f32[96,128]{1,0:T(8,128)}, f32[96,128]{1,0:T(8,128)S(1)}, u32[]{:S(2)}, u32[]{:S(2)}) collective-permute-start(f32[96,128]{1,0:T(8,128)} %bitcast.9), channel_id=1, source_target_pairs={{1,0},{0,1},{3,2},{2,3},{5,4},{4,5},{7,6},{6,7},{9,8},{8,9},{11,10... | collective-permute-start | bytes 147464 | tf_op jit(solution)/shard_map/ppermute | solution.py:98
  0.5 11.7 %collective-permute-start.5 = (f32[96,128]{1,0:T(8,128)}, f32[96,128]{1,0:T(8,128)S(1)}, u32[]{:S(2)}, u32[]{:S(2)}) collective-permute-start(f32[96,128]{1,0:T(8,128)} %bitcast.10), channel_id=1, source_target_pairs={{18,0},{19,1},{16,2},{17,3},{22,4},{23,5},{20,6},{21,7},{26,8},{27... | collective-permute-start | bytes 147464 | tf_op jit(solution)/shard_map/ppermute | solution.py:98
  3.9 4.6 %collective-permute-start.7 = (bf16[1,12288]{1,0:T(2,128)(2,1)}, bf16[1,12288]{1,0:T(2,128)(2,1)S(1)}, u32[]{:S(2)}, u32[]{:S(2)}) collective-permute-start(bf16[1,12288]{1,0:T(2,128)(2,1)} %param.5), channel_id=1, source_target_pairs={{16,0},{17,1},{18,2},{19,3},{20,4},{21,5},{22,6},{23,7},{24,8},{25... | collective-permute-start | bytes 73736 | tf_op jit(solution)/shard_map/ppermute | solution.py:98
  4.4 10.3 %collective-permute-start.4 = (f32[96,128]{1,0:T(8,128)}, f32[96,128]{1,0:T(8,128)S(1)}, u32[]{:S(2)}, u32[]{:S(2)}) collective-permute-start(f32[96,128]{1,0:T(8,128)} %bitcast.11), channel_id=1, source_target_pairs={{16,0},{17,1},{18,2},{19,3},{20,4},{21,5},{22,6},{23,7},{24,8},{25... | collective-permute-start | bytes 147464 | tf_op jit(solution)/shard_map/ppermute | solution.py:98
  5.9 8.8 %collective-permute-start.3 = (f32[96,128]{1,0:T(8,128)}, f32[96,128]{1,0:T(8,128)S(1)}, u32[]{:S(2)}, u32[]{:S(2)}) collective-permute-start(f32[96,128]{1,0:T(8,128)} %bitcast.12), channel_id=1, source_target_pairs={{2,0},{3,1},{0,2},{1,3},{6,4},{7,5},{4,6},{5,7},{10,8},{11,9},{8,1... | collective-permute-start | bytes 147464 | tf_op jit(solution)/shard_map/ppermute | solution.py:98
  8.5 6.2 %collective-permute-start.2 = (f32[96,128]{1,0:T(8,128)}, f32[96,128]{1,0:T(8,128)S(1)}, u32[]{:S(2)}, u32[]{:S(2)}) collective-permute-start(f32[96,128]{1,0:T(8,128)} %bitcast.13), channel_id=1, source_target_pairs={{4,0},{5,1},{6,2},{7,3},{8,4},{9,5},{10,6},{11,7},{12,8},{13,9},{1... | collective-permute-start | bytes 147464 | tf_op jit(solution)/shard_map/ppermute | solution.py:98
  12.1 5.2 %collective-permute-start.1 = (f32[96,128]{1,0:T(8,128)}, f32[96,128]{1,0:T(8,128)S(1)}, u32[]{:S(2)}, u32[]{:S(2)}) collective-permute-start(f32[96,128]{1,0:T(8,128)} %bitcast.14), channel_id=1, source_target_pairs={{8,0},{9,1},{10,2},{11,3},{12,4},{13,5},{14,6},{15,7},{0,8},{1,9},... | collective-permute-start | bytes 147464 | tf_op jit(solution)/shard_map/ppermute | solution.py:98
  12.1 6.2 %collective-permute-start = (f32[96,128]{1,0:T(8,128)}, f32[96,128]{1,0:T(8,128)S(1)}, u32[]{:S(2)}, u32[]{:S(2)}) collective-permute-start(f32[96,128]{1,0:T(8,128)} %bitcast.15), channel_id=1, source_target_pairs={{12,0},{13,1},{14,2},{15,3},{0,4},{1,5},{2,6},{3,7},{4,8},{5,9},{6... | collective-permute-start | bytes 147464 | tf_op jit(solution)/shard_map/ppermute | solution.py:98
  19.1 5.8 %collective-permute-start.15 = (bf16[3,96,128]{2,1,0:T(8,128)(2,1)S(1)}, bf16[3,96,128]{2,1,0:T(8,128)(2,1)S(1)}, u32[]{:S(2)}, u32[]{:S(2)}) collective-permute-start(bf16[3,96,128]{2,1,0:T(8,128)(2,1)S(1)} %fusion.refs_4_), channel_id=1, source_target_pairs={{18,0},{19,1},{16,2},{17,3},{22,4},{23,5},{20,6},{21,7},{26,8},{27... | collective-permute-start | bytes 221192 | tf_op jit(solution)/shard_map/ppermute | solution.py:98
  20.8 4.4 %collective-permute-start.14 = (bf16[3,96,128]{2,1,0:T(8,128)(2,1)S(1)}, bf16[3,96,128]{2,1,0:T(8,128)(2,1)S(1)}, u32[]{:S(2)}, u32[]{:S(2)}) collective-permute-start(bf16[3,96,128]{2,1,0:T(8,128)(2,1)S(1)} %fusion.refs_4_), channel_id=1, source_target_pairs={{16,0},{17,1},{18,2},{19,3},{20,4},{21,5},{22,6},{23,7},{24,8},{25... | collective-permute-start | bytes 221192 | tf_op jit(solution)/shard_map/ppermute | solution.py:98
  21.4 4.4 %collective-permute-start.9 = (bf16[3,96,128]{2,1,0:T(8,128)(2,1)S(1)}, bf16[3,96,128]{2,1,0:T(8,128)(2,1)S(1)}, u32[]{:S(2)}, u32[]{:S(2)}) collective-permute-start(bf16[3,96,128]{2,1,0:T(8,128)(2,1)S(1)} %fusion.refs_4_), channel_id=1, source_target_pairs={{2,0},{3,1},{0,2},{1,3},{6,4},{7,5},{4,6},{5,7},{10,8},{11,9},{8,1... | collective-permute-start | bytes 221192 | tf_op jit(solution)/shard_map/ppermute | solution.py:98
  22.6 1.7 %collective-permute-start.8 = (f32[96,128]{1,0:T(8,128)S(1)}, f32[96,128]{1,0:T(8,128)S(1)}, u32[]{:S(2)}, u32[]{:S(2)}) collective-permute-start(f32[96,128]{1,0:T(8,128)S(1)} %collective-permute-done.3.refs_1_), channel_id=1, source_target_pairs={{1,0},{0,1},{3,2},{2,3},{5,4},{4,5},{7,6},{6,7},{9,8},{8,9},{11,10... | collective-permute-start | bytes 147464 | tf_op jit(solution)/shard_map/ppermute | solution.py:98
  22.7 1.8 %collective-permute-start.12 = (f32[96,128]{1,0:T(8,128)S(1)}, f32[96,128]{1,0:T(8,128)S(1)}, u32[]{:S(2)}, u32[]{:S(2)}) collective-permute-start(f32[96,128]{1,0:T(8,128)S(1)} %collective-permute-done.4.refs_8_), channel_id=1, source_target_pairs={{1,0},{0,1},{3,2},{2,3},{5,4},{4,5},{7,6},{6,7},{9,8},{8,9},{11,10... | collective-permute-start | bytes 147464 | tf_op jit(solution)/shard_map/ppermute | solution.py:98
  24.3 2.3 %collective-permute-start.10 = (bf16[3,96,128]{2,1,0:T(8,128)(2,1)S(1)}, bf16[3,96,128]{2,1,0:T(8,128)(2,1)S(1)}, u32[]{:S(2)}, u32[]{:S(2)}) collective-permute-start(bf16[3,96,128]{2,1,0:T(8,128)(2,1)S(1)} %fusion.refs_4_), channel_id=1, source_target_pairs={{1,0},{0,1},{3,2},{2,3},{5,4},{4,5},{7,6},{6,7},{9,8},{8,9},{11,10... | collective-permute-start | bytes 221192 | tf_op jit(solution)/shard_map/ppermute | solution.py:98
  24.4 2.2 %collective-permute-start.13 = (f32[96,128]{1,0:T(8,128)S(1)}, f32[96,128]{1,0:T(8,128)S(1)}, u32[]{:S(2)}, u32[]{:S(2)}) collective-permute-start(f32[96,128]{1,0:T(8,128)S(1)} %collective-permute-done.5.refs_9_), channel_id=1, source_target_pairs={{1,0},{0,1},{3,2},{2,3},{5,4},{4,5},{7,6},{6,7},{9,8},{8,9},{11,10... | collective-permute-start | bytes 147464 | tf_op jit(solution)/shard_map/ppermute | solution.py:98
  24.9 1.7 %collective-permute-start.17 = (bf16[3,96,128]{2,1,0:T(8,128)(2,1)S(1)}, bf16[3,96,128]{2,1,0:T(8,128)(2,1)S(1)}, u32[]{:S(2)}, u32[]{:S(2)}) collective-permute-start(bf16[3,96,128]{2,1,0:T(8,128)(2,1)S(1)} %collective-permute-done.15.refs_13_), channel_id=1, source_target_pairs={{1,0},{0,1},{3,2},{2,3},{5,4},{4,5},{7,6},{6,7},{9,8},{8,9},{11,10... | collective-permute-start | bytes 221192 | tf_op jit(solution)/shard_map/ppermute | solution.py:98
  25.2 1.4 %collective-permute-start.16 = (bf16[3,96,128]{2,1,0:T(8,128)(2,1)S(1)}, bf16[3,96,128]{2,1,0:T(8,128)(2,1)S(1)}, u32[]{:S(2)}, u32[]{:S(2)}) collective-permute-start(bf16[3,96,128]{2,1,0:T(8,128)(2,1)S(1)} %collective-permute-done.14.refs_12_), channel_id=1, source_target_pairs={{1,0},{0,1},{3,2},{2,3},{5,4},{4,5},{7,6},{6,7},{9,8},{8,9},{11,10... | collective-permute-start | bytes 221192 | tf_op jit(solution)/shard_map/ppermute | solution.py:98
  25.8 1.3 %collective-permute-start.11 = (bf16[3,96,128]{2,1,0:T(8,128)(2,1)S(1)}, bf16[3,96,128]{2,1,0:T(8,128)(2,1)S(1)}, u32[]{:S(2)}, u32[]{:S(2)}) collective-permute-start(bf16[3,96,128]{2,1,0:T(8,128)(2,1)S(1)} %collective-permute-done.9.refs_5_), channel_id=1, source_target_pairs={{1,0},{0,1},{3,2},{2,3},{5,4},{4,5},{7,6},{6,7},{9,8},{8,9},{11,10... | collective-permute-start | bytes 221192 | tf_op jit(solution)/shard_map/ppermute | solution.py:98

commit v4 on v2

v4 whole, which is shorter than its diff:
```python
import functools

import jax
import jax.numpy as jnp
from jax import lax
from jax.experimental import pallas as pl
from jax.experimental.pallas import tpu as pltpu
from jax.sharding import PartitionSpec as P

LANES = 128
SUB = 8
VMEM_LIMIT = 51 * 1024 * 1024


def split_kernel(base_ref, inc_ref, split_ref, wide_ref):
    base = base_ref[...]
    high = base.astype(jnp.bfloat16)
    rest = base - high.astype(jnp.float32)
    middle = rest.astype(jnp.bfloat16)
    split_ref[0] = high
    split_ref[1] = middle
    split_ref[2] = (rest - middle.astype(jnp.float32)).astype(jnp.bfloat16)
    wide_ref[...] = inc_ref[...].astype(jnp.float32)


def pack_kernel(split_ref, *refs):
    line, out_ref = refs[:-1], refs[-1]
    high, middle, low = (split_ref[i].astype(jnp.float32) for i in range(3))
    base = high + middle + low
    out_ref[0:3] = split_ref[...]
    for j, ref in enumerate(line):
        out_ref[3 + j] = (ref[...] - base).astype(jnp.bfloat16)


def product_kernel(group, places, *refs):
    own, other = refs[:4], refs[4:8]
    inc_own, inc_other, taper_hbm, out_ref = refs[8:12]
    tiles, pert, picked_from, picked, acc, sems = refs[12:]
    slots, block_size, _ = taper_hbm.shape
    members = 4 * group
    rows = own[0].shape[1]
    pitch = pert.shape[0] // members
    quarters = block_size // LANES
    block_count = rows // quarters
    copies = []
    for s in range(slots):
        depth = slice(s * block_size, (s + 1) * block_size)
        copies.append(pltpu.make_async_copy(taper_hbm.at[s], tiles.at[:, depth], sems.at[s]))
        copies[-1].start()

    def weigh(side, groups, inc_ref):
        def chunk(r, carry):
            at = pl.multiple_of(r * 2 * SUB, 2 * SUB)
            starts, steps = [], []
            for ref in groups:
                parts = [
                    ref[j, pl.ds(at, 2 * SUB), :].astype(jnp.float32) for j in range(group + 2)
                ]
                starts.append(parts[0] + parts[1] + parts[2])
                steps.append(parts[3:])
            total = sum(step for line in steps for step in line) + group * sum(starts)
            mean = total * (1.0 / members)
            m = 0
            for start, line in zip(starts, steps):
                start = start - mean
                for value in [start] + [start + step for step in line]:
                    pert[pl.ds(m * pitch + at, 2 * SUB), :] = value
                    m += 1
            return carry

        lax.fori_loop(0, rows // (2 * SUB), chunk, 0, unroll=2)

        for i in range(block_count):
            for q in range(quarters):
                lanes = slice(q * LANES, (q + 1) * LANES)
                at = i * quarters + q
                inc = inc_ref[:, at * LANES : (at + 1) * LANES].astype(jnp.float32)
                part = pert[pl.ds(at, members, pitch), :] * inc
                picked_from[side * block_count + i, :, lanes] = part.astype(jnp.bfloat16)

    weigh(1, other, inc_other)
    weigh(0, own, inc_own)

    for i in range(block_count):
        rows_of = slice(i * members, (i + 1) * members)
        picked[rows_of, 0:block_size] = picked_from[i]
        for s in range(1, slots):
            depth = slice(s * block_size, (s + 1) * block_size)
            picked[rows_of, depth] = picked_from[places[s - 1, i]]
    for copy in copies:
        copy.wait()
    acc[...] = lax.dot_general(
        picked[...], tiles[...], (((1,), (1,)), ((), ())), preferred_element_type=jnp.float32
    )

    scale = 1.0 / (members - 1)
    for i in range(block_count):
        for q in range(quarters):
            lanes = slice(q * LANES, (q + 1) * LANES)
            term = (
                pert[pl.ds(i * quarters + q, members, pitch), :]
                * acc[i * members : (i + 1) * members, lanes]
            )
            row = jnp.sum(term, axis=0, keepdims=True) * scale
            out_ref[:, i * block_size + q * LANES : i * block_size + (q + 1) * LANES] = row


def mover(lon_size, mem_size):
    def one(x, step, mem_of):
        perm = []
        for l in range(lon_size):
            for m in range(mem_size):
                source = ((l + step) % lon_size) * mem_size + mem_of(m)
                perm.append((source, l * mem_size + m))
        return lax.ppermute(x, ("lon", "mem"), perm)

    def move(x, across, mem_of):
        if not across:
            return one(x, 0, mem_of)
        if lon_size == 2:
            return one(x, 1, mem_of)
        axis = x.ndim - 2 if x.shape[-2] > 1 else x.ndim - 1
        right, left = jnp.split(x, 2, axis=axis)
        return jnp.concatenate([one(right, 1, mem_of), one(left, -1, mem_of)], axis=axis)

    return move


def on_device(ensemble, increments, offsets, taper):
    lon_size, mem_size = lax.axis_size("lon"), lax.axis_size("mem")
    group = mem_size // 4
    slots, block_size, _ = taper.shape
    block_count = offsets.shape[0]
    columns = ensemble.shape[1]
    rows = columns // LANES
    move = mover(lon_size, mem_size)
    same, beside = (lambda m: m), (lambda m: m ^ 2)

    base = ensemble.reshape(rows, LANES)
    line = [
        move(base, False, lambda m: (m + 4 * d) % mem_size) for d in reversed(range(1, group))
    ]
    inc_other = move(increments.reshape(1, columns), True, same)
    places = jnp.arange(block_count, dtype=jnp.int32) + offsets.T
    places = jnp.where(places < 0, places + 2 * block_count, places)
    whole = pl.BlockSpec(memory_space=pltpu.VMEM)
    split, inc_own = pl.pallas_call(
        split_kernel,
        out_shape=(
            jax.ShapeDtypeStruct((3, rows, LANES), jnp.bfloat16),
            jax.ShapeDtypeStruct((1, columns), jnp.float32),
        ),
        in_specs=[whole] * 2,
        out_specs=(whole, whole),
    )(base, increments)
    split, inc_own, places, inc_other, line = lax.optimization_barrier(
        (split, inc_own, places, inc_other, line)
    )

    mine = pl.pallas_call(
        pack_kernel,
        out_shape=jax.ShapeDtypeStruct((group + 2, rows, LANES), jnp.bfloat16),
        in_specs=[whole] * group,
        out_specs=whole,
    )(split, *line)
    groups = [
        mine,
        move(mine, False, beside),
        move(mine, True, same),
        move(mine, True, beside),
    ]
    groups += [move(x, False, lambda m: m ^ 1) for x in groups]
    operands = [groups[i] for i in (0, 1, 4, 5, 2, 3, 6, 7)]

    vectors = mem_size * block_count
    return pl.pallas_call(
        functools.partial(product_kernel, group),
        out_shape=jax.ShapeDtypeStruct((1, columns), jnp.float32),
        in_specs=[pl.BlockSpec(memory_space=pltpu.SMEM)]
        + [whole] * 10
        + [pl.BlockSpec(memory_space=pltpu.HBM)],
        out_specs=whole,
        scratch_shapes=[
            pltpu.VMEM((block_size, slots * block_size), jnp.bfloat16),
            pltpu.VMEM((mem_size * (rows + 1), LANES), jnp.float32),
            pltpu.VMEM((2 * block_count, mem_size, block_size), jnp.bfloat16),
            pltpu.VMEM((vectors, slots * block_size), jnp.bfloat16),
            pltpu.VMEM((vectors, block_size), jnp.float32),
            pltpu.SemaphoreType.DMA((slots,)),
        ],
        compiler_params=pltpu.CompilerParams(vmem_limit_bytes=VMEM_LIMIT),
    )(places, *operands, inc_own, inc_other, taper)


def solution(mesh):
    return jax.shard_map(
        on_device,
        mesh=mesh,
        in_specs=(P("mem", "lon"), P("mem", "lon"), P("lon", None), P()),
        out_specs=P("mem", "lon"),
        check_vma=False,
    )
```

time: 31.8 us -> 30.9 us (0.972)
  waiting for transfers between devices: 11.6 us -> 7.56 us
  Pallas kernels: 4.9 us -> 8.36 us
  other arithmetic: 1.54 us -> 0.69 us
  local copies, waits for them, and re-layouts: 1.48 us -> 2.32 us
    all_to_all x1 -> x0, starting transfers between devices: 6.32 us -> none  [on_device(): lax.all_to_all(sent, 'mem', 0, 0, axis_index_groups=lines, tiled=True)]
    ppermute x8 -> x11, starting transfers between devices: 5.52 us -> 11.6 us  [one(): return lax.ppermute(x, ('lon', 'mem'), perm)]
    all_to_all x1 -> x0, waiting for transfers between devices: 3.21 us -> none  [on_device(): lax.all_to_all(sent, 'mem', 0, 0, axis_index_groups=lines, tiled=True)]
    pallas_call x0 -> x2, Pallas kernels: none -> 3.08 us  [the longest x1 1.6 us: on_device(): pl.pallas_call(pack_kernel, out_shape=jax.ShapeDtypeStruct((group + 2, ro...]
    unnamed x0 -> x10, local copies, waits for them, and re-layouts: none -> 2.32 us
    broadcast_in_dim x1 -> x0, local copies, waits for them, and re-layouts: 1.48 us -> none  [on_device(): sent = jnp.broadcast_to(state, (group, rows, LANES))]
    ppermute x8 -> x11, waiting for transfers between devices: 8.42 us -> 7.56 us  [one(): return lax.ppermute(x, ('lon', 'mem'), perm)]
    convert_element_type x1 -> x0, other arithmetic: 0.85 us -> none  [on_device(): inc_own = increments.astype(jnp.float32)]
  transfers between devices with their start and end apart: 9 -> 11, of which waited for: 6 -> 7; matrix products, arithmetic and copies ran while one was open for 5% -> 2% of each run, Pallas kernels for 0% -> 5%
where the time goes in v4:
time: 30.9 us; the launch traced here: 30.6 us
  starting transfers between devices  11.6 us (38%)
  Pallas kernels  8.36 us (27%)
  waiting for transfers between devices  7.56 us (24%)
  local copies, waits for them, and re-layouts  2.32 us (8%)
  other arithmetic  0.69 us (2%)
    ppermute x11, starting transfers between devices, one(): return lax.ppermute(x, ('lon', 'mem'), perm)  11.6 us
    ppermute x11, waiting for transfers between devices, one(): return lax.ppermute(x, ('lon', 'mem'), perm)  7.56 us
    pallas_call x1, Pallas kernels, on_device(): pl.pallas_call(functools.partial(product_kernel, group), out_shape=jax.Sh...  5.29 us
    unnamed x10, local copies, waits for them, and re-layouts  2.32 us
    pallas_call x1, Pallas kernels, on_device(): pl.pallas_call(pack_kernel, out_shape=jax.ShapeDtypeStruct((group + 2, ro...  1.6 us
    pallas_call x1, Pallas kernels, on_device(): pl.pallas_call(split_kernel, out_shape=(jax.ShapeDtypeStruct((3, rows, LA...  1.48 us
    select_n x1, other arithmetic, on_device(): places = jnp.where(places < 0, places + 2 * block_count, places)  0.69 us
  transfers between devices with their start and end apart: 11, of which 7 were waited for; matrix products, arithmetic and copies ran while one was open for 2% of the time, Pallas kernels for 5%

profile of v4, /device:TPU:0, one launch (start us, length us, event | category | flops | bytes accessed | tf_op | source)
XLA Modules:
  0.0 30.6 jit_solution(2660018835827343075)
XLA Ops:
  0.0 5.0 %collective-permute-start.3 = (f32[96,128]{1,0:T(8,128)}, f32[96,128]{1,0:T(8,128)S(1)}, u32[]{:S(2)}, u32[]{:S(2)}) collective-permute-start(f32[96,128]{1,0:T(8,128)} %bitcast.5), channel_id=1, source_target_pairs={{4,0},{5,1},{6,2},{7,3},{8,4},{9,5},{10,6},{11,7},{12,8},{13,9},{1... | collective-permute-start | bytes 147464 | tf_op jit(solution)/shard_map/ppermute | solution.py:115
  5.0 0.0 collective-permute-start.2
  5.1 1.0 %collective-permute-start.1 = (f32[96,128]{1,0:T(8,128)}, f32[96,128]{1,0:T(8,128)S(1)}, u32[]{:S(2)}, u32[]{:S(2)}) collective-permute-start(f32[96,128]{1,0:T(8,128)} %bitcast.7), channel_id=1, source_target_pairs={{12,0},{13,1},{14,2},{15,3},{0,4},{1,5},{2,6},{3,7},{4,8},{5,9},{6... | collective-permute-start | bytes 147464 | tf_op jit(solution)/shard_map/ppermute | solution.py:115
  6.1 1.5 %collective-permute-start = (bf16[1,12288]{1,0:T(2,128)(2,1)}, bf16[1,12288]{1,0:T(2,128)(2,1)S(1)}, u32[]{:S(2)}, u32[]{:S(2)}) collective-permute-start(bf16[1,12288]{1,0:T(2,128)(2,1)} %inc_ref.1), channel_id=1, source_target_pairs={{16,0},{17,1},{18,2},{19,3},{20,4},{21,5},{22,6},{23,7},{24,8},{25... | collective-permute-start | bytes 73736 | tf_op jit(solution)/shard_map/ppermute | solution.py:115
  7.6 0.7 %compare_select_fusion.places = s32[7,24]{1,0:T(8,128)S(1)} fusion(s32[24,7]{0,1:T(8,128)} %param.6), kind=kLoop, calls=%fused_computation | loop fusion | flops 672 | bytes 1344 | tf_op jit(solution)/shard_map/jit(_where)/select_n | solution.py:145
  8.3 1.5 %shard_map.46 = (bf16[3,96,128]{2,1,0:T(8,128)(2,1)}, f32[1,12288]{1,0:T(1,128)}) custom-call(f32[96,128]{1,0:T(8,128)} %bitcast.8, bf16[1,12288]{1,0:T(2,128)(2,1)} %inc_ref.1), custom_call_target="tpu_custom_call" | custom-call | tf_op jit(solution)/shard_map/pallas_call | solution.py:147
  9.8 0.6 %collective-permute-done.refs_9_ = bf16[1,12288]{1,0:T(2,128)(2,1)S(1)} collective-permute-done((bf16[1,12288]{1,0:T(2,128)(2,1)}, bf16[1,12288]{1,0:T(2,128)(2,1)S(1)}, u32[]{:S(2)}, u32[]{:S(2)}) %collective-permute-start) | collective-permute-done | bytes 24608 | tf_op jit(solution)/shard_map/ppermute | solution.py:115
  10.4 0.0 collective-permute-done.3.refs_2_
  10.4 0.0 copy-start.2
  10.4 0.0 collective-permute-done.2.refs_1_
  10.4 0.0 copy-start.3
  10.4 0.8 %collective-permute-done.1.refs_0_ = f32[96,128]{1,0:T(8,128)S(1)} collective-permute-done((f32[96,128]{1,0:T(8,128)}, f32[96,128]{1,0:T(8,128)S(1)}, u32[]{:S(2)}, u32[]{:S(2)}) %collective-permute-start.1) | collective-permute-done | bytes 49184 | tf_op jit(solution)/shard_map/ppermute | solution.py:115
  11.2 0.0 copy-start.4
  11.2 0.0 copy-done.2
  11.2 0.0 copy-done.3
  11.2 0.6 %copy-done.4 = f32[96,128]{1,0:T(8,128)} copy-done((f32[96,128]{1,0:T(8,128)}, f32[96,128]{1,0:T(8,128)S(1)}, u32[]{:S(2)}) %copy-start.4) | copy-done | bytes 49176
  11.8 1.6 %shard_map.47.refs_0_ = bf16[6,96,128]{2,1,0:T(8,128)(2,1)} custom-call(bf16[3,96,128]{2,1,0:T(8,128)(2,1)} %get-tuple-element.17.split_ref, f32[96,128]{1,0:T(8,128)} %copy-done.4, f32[96,128]{1,0:T(8,128)} %copy-done.3, f32[96,128]{1,0:T(8,128)} %copy-done.2), custom_call_target="tpu_custom_call" | custom-call | tf_op jit(solution)/shard_map/pallas_call | solution.py:160
  13.4 2.4 %collective-permute-start.8 = (bf16[6,96,128]{2,1,0:T(8,128)(2,1)}, bf16[6,96,128]{2,1,0:T(8,128)(2,1)S(1)}, u32[]{:S(2)}, u32[]{:S(2)}) collective-permute-start(bf16[6,96,128]{2,1,0:T(8,128)(2,1)} %shard_map.47.refs_0_), channel_id=1, source_target_pairs={{18,0},{19,1},{16,2},{17,3},{22,4},{23,5},{20,6},{21,7},{26,8},{27... | collective-permute-start | bytes 442376 | tf_op jit(solution)/shard_map/ppermute | solution.py:115
  15.8 0.5 %collective-permute-start.7 = (bf16[6,96,128]{2,1,0:T(8,128)(2,1)}, bf16[6,96,128]{2,1,0:T(8,128)(2,1)S(1)}, u32[]{:S(2)}, u32[]{:S(2)}) collective-permute-start(bf16[6,96,128]{2,1,0:T(8,128)(2,1)} %shard_map.47.refs_0_), channel_id=1, source_target_pairs={{16,0},{17,1},{18,2},{19,3},{20,4},{21,5},{22,6},{23,7},{24,8},{25... | collective-permute-start | bytes 442376 | tf_op jit(solution)/shard_map/ppermute | solution.py:115
  16.3 0.5 %collective-permute-start.4 = (bf16[6,96,128]{2,1,0:T(8,128)(2,1)}, bf16[6,96,128]{2,1,0:T(8,128)(2,1)S(1)}, u32[]{:S(2)}, u32[]{:S(2)}) collective-permute-start(bf16[6,96,128]{2,1,0:T(8,128)(2,1)} %shard_map.47.refs_0_), channel_id=1, source_target_pairs={{2,0},{3,1},{0,2},{1,3},{6,4},{7,5},{4,6},{5,7},{10,8},{11,9},{8,1... | collective-permute-start | bytes 442376 | tf_op jit(solution)/shard_map/ppermute | solution.py:115
  16.9 0.0 collective-permute-start.5
  16.9 4.3 %collective-permute-done.8.refs_5_ = bf16[6,96,128]{2,1,0:T(8,128)(2,1)S(1)} collective-permute-done((bf16[6,96,128]{2,1,0:T(8,128)(2,1)}, bf16[6,96,128]{2,1,0:T(8,128)(2,1)S(1)}, u32[]{:S(2)}, u32[]{:S(2)}) %collective-permute-start.8) | collective-permute-done | bytes 147488 | tf_op jit(solution)/shard_map/ppermute | solution.py:115
  21.2 0.0 collective-permute-start.10
  21.2 0.8 %collective-permute-done.7.refs_4_ = bf16[6,96,128]{2,1,0:T(8,128)(2,1)S(1)} collective-permute-done((bf16[6,96,128]{2,1,0:T(8,128)(2,1)}, bf16[6,96,128]{2,1,0:T(8,128)(2,1)S(1)}, u32[]{:S(2)}, u32[]{:S(2)}) %collective-permute-start.7) | collective-permute-done | bytes 147488 | tf_op jit(solution)/shard_map/ppermute | solution.py:115
  22.0 0.0 collective-permute-start.9
  22.0 0.0 collective-permute-done.4.refs_1_
  22.0 0.5 %collective-permute-start.6 = (bf16[6,96,128]{2,1,0:T(8,128)(2,1)S(1)}, bf16[6,96,128]{2,1,0:T(8,128)(2,1)S(1)}, u32[]{:S(2)}, u32[]{:S(2)}) collective-permute-start(bf16[6,96,128]{2,1,0:T(8,128)(2,1)S(1)} %collective-permute-done.4.refs_1_), channel_id=1, source_target_pairs={{1,0},{0,1},{3,2},{2,3},{5,4},{4,5},{7,6},{6,7},{9,8},{8,9},{11,10... | collective-permute-start | bytes 442376 | tf_op jit(solution)/shard_map/ppermute | solution.py:115
  22.5 0.0 collective-permute-done.5.refs_2_
  22.5 0.1 collective-permute-done.10.refs_7_
  22.6 0.8 %collective-permute-done.9.refs_6_ = bf16[6,96,128]{2,1,0:T(8,128)(2,1)S(1)} collective-permute-done((bf16[6,96,128]{2,1,0:T(8,128)(2,1)S(1)}, bf16[6,96,128]{2,1,0:T(8,128)(2,1)S(1)}, u32[]{:S(2)}, u32[]{:S(2)}) %collective-permute-start.9) | collective-permute-done | bytes 147488 | tf_op jit(solution)/shard_map/ppermute | solution.py:115
  23.3 0.2 collective-permute-done.6.refs_3_
  23.6 0.0 copy-start
  23.6 0.9 %copy-done = bf16[6,96,128]{2,1,0:T(8,128)(2,1)S(1)} copy-done((bf16[6,96,128]{2,1,0:T(8,128)(2,1)S(1)}, bf16[6,96,128]{2,1,0:T(8,128)(2,1)}, u32[]{:S(2)}) %copy-start) | copy-done | bytes 147480
  24.5 0.0 copy-start.1
  24.5 0.8 %copy-done.1 = f32[1,12288]{1,0:T(1,128)S(1)} copy-done((f32[1,12288]{1,0:T(1,128)S(1)}, f32[1,12288]{1,0:T(1,128)}, u32[]{:S(2)}) %copy-start.1) | copy-done | bytes 49176
  25.3 5.3 %shard_map.48 = f32[1,12288]{1,0:T(1,128)} custom-call(s32[7,24]{1,0:T(8,128)S(1)} %compare_select_fusion.places, bf16[6,96,128]{2,1,0:T(8,128)(2,1)S(1)} %copy-done, bf16[6,96,128]{2,1,0:T(8,128)(2,1)S(1)} %collective-permute-done.4.refs_1_, bf16[6,96,128]{2,1,0:T(8,128)(2,1)S(1)} %collective-permute-done.5.refs_2_, ...), custom_call_target="tpu_custom_call" | custom-call | tf_op jit(solution)/shard_map/pallas_call | solution.py:176
Async XLA Ops:
  0.0 10.4 %collective-permute-start.3 = (f32[96,128]{1,0:T(8,128)}, f32[96,128]{1,0:T(8,128)S(1)}, u32[]{:S(2)}, u32[]{:S(2)}) collective-permute-start(f32[96,128]{1,0:T(8,128)} %bitcast.5), channel_id=1, source_target_pairs={{4,0},{5,1},{6,2},{7,3},{8,4},{9,5},{10,6},{11,7},{12,8},{13,9},{1... | collective-permute-start | bytes 147464 | tf_op jit(solution)/shard_map/ppermute | solution.py:115
  5.0 5.3 %collective-permute-start.2 = (f32[96,128]{1,0:T(8,128)}, f32[96,128]{1,0:T(8,128)S(1)}, u32[]{:S(2)}, u32[]{:S(2)}) collective-permute-start(f32[96,128]{1,0:T(8,128)} %bitcast.6), channel_id=1, source_target_pairs={{8,0},{9,1},{10,2},{11,3},{12,4},{13,5},{14,6},{15,7},{0,8},{1,9},... | collective-permute-start | bytes 147464 | tf_op jit(solution)/shard_map/ppermute | solution.py:115
  5.1 6.1 %collective-permute-start.1 = (f32[96,128]{1,0:T(8,128)}, f32[96,128]{1,0:T(8,128)S(1)}, u32[]{:S(2)}, u32[]{:S(2)}) collective-permute-start(f32[96,128]{1,0:T(8,128)} %bitcast.7), channel_id=1, source_target_pairs={{12,0},{13,1},{14,2},{15,3},{0,4},{1,5},{2,6},{3,7},{4,8},{5,9},{6... | collective-permute-start | bytes 147464 | tf_op jit(solution)/shard_map/ppermute | solution.py:115
  6.1 4.3 %collective-permute-start = (bf16[1,12288]{1,0:T(2,128)(2,1)}, bf16[1,12288]{1,0:T(2,128)(2,1)S(1)}, u32[]{:S(2)}, u32[]{:S(2)}) collective-permute-start(bf16[1,12288]{1,0:T(2,128)(2,1)} %inc_ref.1), channel_id=1, source_target_pairs={{16,0},{17,1},{18,2},{19,3},{20,4},{21,5},{22,6},{23,7},{24,8},{25... | collective-permute-start | bytes 73736 | tf_op jit(solution)/shard_map/ppermute | solution.py:115
  10.4 0.8 %copy-start.2 = (f32[96,128]{1,0:T(8,128)}, f32[96,128]{1,0:T(8,128)S(1)}, u32[]{:S(2)}) copy-start(f32[96,128]{1,0:T(8,128)S(1)} %collective-permute-done.3.refs_2_) | copy-start | bytes 147460
  10.4 0.8 %copy-start.3 = (f32[96,128]{1,0:T(8,128)}, f32[96,128]{1,0:T(8,128)S(1)}, u32[]{:S(2)}) copy-start(f32[96,128]{1,0:T(8,128)S(1)} %collective-permute-done.2.refs_1_) | copy-start | bytes 147460
  11.2 0.6 %copy-start.4 = (f32[96,128]{1,0:T(8,128)}, f32[96,128]{1,0:T(8,128)S(1)}, u32[]{:S(2)}) copy-start(f32[96,128]{1,0:T(8,128)S(1)} %collective-permute-done.1.refs_0_) | copy-start | bytes 147460
  13.4 7.8 %collective-permute-start.8 = (bf16[6,96,128]{2,1,0:T(8,128)(2,1)}, bf16[6,96,128]{2,1,0:T(8,128)(2,1)S(1)}, u32[]{:S(2)}, u32[]{:S(2)}) collective-permute-start(bf16[6,96,128]{2,1,0:T(8,128)(2,1)} %shard_map.47.refs_0_), channel_id=1, source_target_pairs={{18,0},{19,1},{16,2},{17,3},{22,4},{23,5},{20,6},{21,7},{26,8},{27... | collective-permute-start | bytes 442376 | tf_op jit(solution)/shard_map/ppermute | solution.py:115
  15.8 6.2 %collective-permute-start.7 = (bf16[6,96,128]{2,1,0:T(8,128)(2,1)}, bf16[6,96,128]{2,1,0:T(8,128)(2,1)S(1)}, u32[]{:S(2)}, u32[]{:S(2)}) collective-permute-start(bf16[6,96,128]{2,1,0:T(8,128)(2,1)} %shard_map.47.refs_0_), channel_id=1, source_target_pairs={{16,0},{17,1},{18,2},{19,3},{20,4},{21,5},{22,6},{23,7},{24,8},{25... | collective-permute-start | bytes 442376 | tf_op jit(solution)/shard_map/ppermute | solution.py:115
  16.3 5.7 %collective-permute-start.4 = (bf16[6,96,128]{2,1,0:T(8,128)(2,1)}, bf16[6,96,128]{2,1,0:T(8,128)(2,1)S(1)}, u32[]{:S(2)}, u32[]{:S(2)}) collective-permute-start(bf16[6,96,128]{2,1,0:T(8,128)(2,1)} %shard_map.47.refs_0_), channel_id=1, source_target_pairs={{2,0},{3,1},{0,2},{1,3},{6,4},{7,5},{4,6},{5,7},{10,8},{11,9},{8,1... | collective-permute-start | bytes 442376 | tf_op jit(solution)/shard_map/ppermute | solution.py:115
  16.9 5.6 %collective-permute-start.5 = (bf16[6,96,128]{2,1,0:T(8,128)(2,1)}, bf16[6,96,128]{2,1,0:T(8,128)(2,1)S(1)}, u32[]{:S(2)}, u32[]{:S(2)}) collective-permute-start(bf16[6,96,128]{2,1,0:T(8,128)(2,1)} %shard_map.47.refs_0_), channel_id=1, source_target_pairs={{1,0},{0,1},{3,2},{2,3},{5,4},{4,5},{7,6},{6,7},{9,8},{8,9},{11,10... | collective-permute-start | bytes 442376 | tf_op jit(solution)/shard_map/ppermute | solution.py:115
  21.2 1.4 %collective-permute-start.10 = (bf16[6,96,128]{2,1,0:T(8,128)(2,1)S(1)}, bf16[6,96,128]{2,1,0:T(8,128)(2,1)S(1)}, u32[]{:S(2)}, u32[]{:S(2)}) collective-permute-start(bf16[6,96,128]{2,1,0:T(8,128)(2,1)S(1)} %collective-permute-done.8.refs_5_), channel_id=1, source_target_pairs={{1,0},{0,1},{3,2},{2,3},{5,4},{4,5},{7,6},{6,7},{9,8},{8,9},{11,10... | collective-permute-start | bytes 442376 | tf_op jit(solution)/shard_map/ppermute | solution.py:115
  22.0 1.4 %collective-permute-start.9 = (bf16[6,96,128]{2,1,0:T(8,128)(2,1)S(1)}, bf16[6,96,128]{2,1,0:T(8,128)(2,1)S(1)}, u32[]{:S(2)}, u32[]{:S(2)}) collective-permute-start(bf16[6,96,128]{2,1,0:T(8,128)(2,1)S(1)} %collective-permute-done.7.refs_4_), channel_id=1, source_target_pairs={{1,0},{0,1},{3,2},{2,3},{5,4},{4,5},{7,6},{6,7},{9,8},{8,9},{11,10... | collective-permute-start | bytes 442376 | tf_op jit(solution)/shard_map/ppermute | solution.py:115
  22.0 1.6 %collective-permute-start.6 = (bf16[6,96,128]{2,1,0:T(8,128)(2,1)S(1)}, bf16[6,96,128]{2,1,0:T(8,128)(2,1)S(1)}, u32[]{:S(2)}, u32[]{:S(2)}) collective-permute-start(bf16[6,96,128]{2,1,0:T(8,128)(2,1)S(1)} %collective-permute-done.4.refs_1_), channel_id=1, source_target_pairs={{1,0},{0,1},{3,2},{2,3},{5,4},{4,5},{7,6},{6,7},{9,8},{8,9},{11,10... | collective-permute-start | bytes 442376 | tf_op jit(solution)/shard_map/ppermute | solution.py:115
  23.6 0.9 %copy-start = (bf16[6,96,128]{2,1,0:T(8,128)(2,1)S(1)}, bf16[6,96,128]{2,1,0:T(8,128)(2,1)}, u32[]{:S(2)}) copy-start(bf16[6,96,128]{2,1,0:T(8,128)(2,1)} %shard_map.47.refs_0_) | copy-start | bytes 442372
  24.5 0.8 %copy-start.1 = (f32[1,12288]{1,0:T(1,128)S(1)}, f32[1,12288]{1,0:T(1,128)}, u32[]{:S(2)}) copy-start(f32[1,12288]{1,0:T(1,128)} %get-tuple-element.21.refs_8_) | copy-start | bytes 147460

commit v5 on v3

--- a/solution.py
+++ b/solution.py
@@ -10,15 +10,26 @@
 LANES = 128
 SUB = 8
 VMEM_LIMIT = 51 * 1024 * 1024
-
-
-def product_kernel(group, places, *refs):
-    own, other = (refs[:4], refs[4:8]), (refs[8:12], refs[12:16])
-    inc_own, inc_other, taper_hbm, out_ref = refs[16:20]
-    tiles, pert, picked_from, picked, acc, sems = refs[20:]
+PACK_COST = 20_000_000_000
+
+
+def pack_kernel(*refs):
+    diff_ref, bases_ref = refs[-2:]
+    bases, line = refs[:4], refs[4:-2]
+    base = bases[0][...]
+    for j, ref in enumerate(line):
+        diff_ref[j] = (ref[...] - base).astype(jnp.bfloat16)
+    for j, ref in enumerate(bases):
+        bases_ref[j] = ref[...]
+
+
+def product_kernel(group, off_ref, *refs):
+    bases, diffs = refs[:2], refs[2:10]
+    inc_own, inc_other, taper_hbm, out_ref = refs[10:14]
+    tiles, pert, picked_from, picked, acc, sems = refs[14:]
     slots, block_size, _ = tiles.shape
     members = 4 * group
-    rows = own[0][0].shape[0]
+    rows = bases[0].shape[1]
     pitch = pert.shape[0] // members
     quarters = block_size // LANES
     block_count = rows // quarters
@@ -27,13 +38,16 @@
         copies.append(pltpu.make_async_copy(taper_hbm.at[s], tiles.at[s], sems.at[s]))
         copies[-1].start()
 
-    def weigh(side, bases, diffs, inc_ref):
+    def weigh(side, inc_ref):
+        lines = [(c, 2 * side + j) for c in range(2) for j in range(2)]
+
         def chunk(r, carry):
             at = pl.multiple_of(r * 2 * SUB, 2 * SUB)
-            starts = [ref[pl.ds(at, 2 * SUB), :] for ref in bases]
+            here = pl.ds(at, 2 * SUB)
+            starts = [bases[c][j, here, :] for c, j in lines]
             steps = [
-                [ref[j, pl.ds(at, 2 * SUB), :].astype(jnp.float32) for j in range(group - 1)]
-                for ref in diffs
+                [diffs[4 * c + j][k, here, :].astype(jnp.float32) for k in range(group - 1)]
+                for c, j in lines
             ]
             total = sum(step for line in steps for step in line) + group * sum(starts)
             mean = total * (1.0 / members)
@@ -55,12 +69,12 @@
                 part = pert[pl.ds(at, members, pitch), :] * inc
                 picked_from[side * block_count + i, :, lanes] = part.astype(jnp.bfloat16)
 
-    weigh(1, *other, inc_other)
-    weigh(0, *own, inc_own)
+    weigh(1, inc_other)
+    weigh(0, inc_own)
 
     contract = (((1,), (1,)), ((), ()))
+    vectors = block_count * members
     copies[0].wait()
-    vectors = block_count * members
     acc[...] = lax.dot_general(
         picked_from[0:block_count].reshape(vectors, block_size),
         tiles[0],
@@ -70,7 +84,9 @@
     for s in range(1, slots):
         for i in range(block_count):
             rows_of = slice(i * members, (i + 1) * members)
-            picked[s - 1, rows_of, :] = picked_from[places[s - 1, i]]
+            place = i + off_ref[s - 1, i]
+            place = jnp.where(place < 0, place + 2 * block_count, place)
+            picked[s - 1, rows_of, :] = picked_from[place]
         copies[s].wait()
         acc[...] += lax.dot_general(
             picked[s - 1], tiles[s], contract, preferred_element_type=jnp.float32
@@ -120,43 +136,46 @@
     same, beside = (lambda m: m), (lambda m: m ^ 2)
 
     base = ensemble.reshape(rows, LANES)
-    inc_other = move(increments.reshape(1, columns), True, same)
-    partner = move(base, False, lambda m: m ^ 1)
-    bases = [
+    line = [
+        move(base, False, lambda m: (m + 4 * d) % mem_size) for d in reversed(range(1, group))
+    ]
+    around = [
         move(base, False, beside),
         move(base, True, same),
         move(base, True, beside),
     ]
-    line = [
-        move(base, False, lambda m: (m + 4 * d) % mem_size) for d in reversed(range(1, group))
-    ]
-    inc_own = increments.astype(jnp.float32)
-    places = jnp.arange(block_count, dtype=jnp.int32) + offsets.T
-    places = jnp.where(places < 0, places + 2 * block_count, places)
-    line, bases, partner, inc_other, inc_own, places = lax.optimization_barrier(
-        (line, bases, partner, inc_other, inc_own, places)
-    )
-
-    diff = (jnp.stack(line) - base[None]).astype(jnp.bfloat16)
-    base = jnp.where(places[0, 0] < 2 * block_count, base, 0.0)
+    inc_other = move(increments.reshape(1, columns), True, same)
+    inc_other, around, line = lax.optimization_barrier((inc_other, around, line))
+
+    whole = pl.BlockSpec(memory_space=pltpu.VMEM)
+    diff, bases = pl.pallas_call(
+        pack_kernel,
+        out_shape=(
+            jax.ShapeDtypeStruct((group - 1, rows, LANES), jnp.bfloat16),
+            jax.ShapeDtypeStruct((4, rows, LANES), jnp.float32),
+        ),
+        in_specs=[whole] * (group + 3),
+        out_specs=(whole,) * 2,
+        compiler_params=pltpu.CompilerParams(vmem_limit_bytes=4 * 1024 * 1024),
+        cost_estimate=pl.CostEstimate(
+            flops=PACK_COST, bytes_accessed=8 * columns * 4, transcendentals=0
+        ),
+    )(base, *around, *line)
     diffs = [
         diff,
         move(diff, False, beside),
         move(diff, True, same),
         move(diff, True, beside),
     ]
-    bases = [base] + bases + [partner] + [move(x, False, lambda m: m ^ 1) for x in bases]
+    bases = [bases, move(bases, False, lambda m: m ^ 1)]
     diffs += [move(x, False, lambda m: m ^ 1) for x in diffs]
-    own, other = (0, 1, 4, 5), (2, 3, 6, 7)
-    operands = [arrays[i] for side in (own, other) for arrays in (bases, diffs) for i in side]
 
     vectors = mem_size * block_count
-    whole = pl.BlockSpec(memory_space=pltpu.VMEM)
     return pl.pallas_call(
         functools.partial(product_kernel, group),
         out_shape=jax.ShapeDtypeStruct((1, columns), jnp.float32),
         in_specs=[pl.BlockSpec(memory_space=pltpu.SMEM)]
-        + [whole] * 18
+        + [whole] * 12
         + [pl.BlockSpec(memory_space=pltpu.HBM)],
         out_specs=whole,
         scratch_shapes=[
@@ -168,7 +187,7 @@
             pltpu.SemaphoreType.DMA((slots,)),
         ],
         compiler_params=pltpu.CompilerParams(vmem_limit_bytes=VMEM_LIMIT),
-    )(places, *operands, inc_own, inc_other, taper)
+    )(offsets.T, *bases, *diffs, increments, inc_other, taper)
 
 
 def solution(mesh):

time: 32.3 us -> 30.2 us (0.935)
  other arithmetic: 3.16 us -> 0 us
  waiting for transfers between devices: 6.63 us -> 7.84 us
  between operations: 0.74 us -> 0.04 us
  starting transfers between devices: 16 us -> 16.6 us
    convert_element_type x2 -> x0, other arithmetic: 1.66 us -> none  [the longest x1 0.85 us: on_device(): inc_own = increments.astype(jnp.float32)]
    select_n x2 -> x0, other arithmetic: 1.5 us -> none  [the longest x1 0.8 us: on_device(): base = jnp.where(places[0, 0] < 2 * block_count, base, 0.0)]
    ppermute x18 -> x15, waiting for transfers between devices: 6.63 us -> 7.84 us  [one(): return lax.ppermute(x, ('lon', 'mem'), perm)]
    unnamed x0 -> x6, local copies, waits for them, and re-layouts: none -> 0.81 us
    ppermute x18 -> x15, starting transfers between devices: 16 us -> 16.6 us  [one(): return lax.ppermute(x, ('lon', 'mem'), perm)]
    slice x1 -> x0, local copies, waits for them, and re-layouts: 0.51 us -> none  [on_device(): base = jnp.where(places[0, 0] < 2 * block_count, base, 0.0)]
  transfers between devices with their start and end apart: 18 -> 15, of which waited for: 6 -> 8; matrix products, arithmetic and copies ran while one was open for 9% -> 0% of each run, Pallas kernels for 0% -> 0%
where the time goes in v5:
time: 30.2 us; the launch traced here: 30.1 us
  starting transfers between devices  16.6 us (55%)
  waiting for transfers between devices  7.84 us (26%)
  Pallas kernels  4.81 us (16%)
  local copies, waits for them, and re-layouts  0.81 us (3%)
    ppermute x15, starting transfers between devices, one(): return lax.ppermute(x, ('lon', 'mem'), perm)  16.6 us
    ppermute x15, waiting for transfers between devices, one(): return lax.ppermute(x, ('lon', 'mem'), perm)  7.84 us
    pallas_call x1, Pallas kernels, on_device(): pl.pallas_call(functools.partial(product_kernel, group), out_shape=jax.Sh...  4.79 us
    unnamed x6, local copies, waits for them, and re-layouts  0.81 us
  transfers between devices with their start and end apart: 15, of which 8 were waited for; matrix products, arithmetic and copies ran while one was open for 0% of the time, Pallas kernels for 0%

profile of v5, /device:TPU:0, one launch (start us, length us, event | category | flops | bytes accessed | tf_op | source)
XLA Modules:
  0.0 30.1 jit_solution(7274465540129755020)
XLA Ops:
  0.0 0.0 copy-start
  0.0 0.0 copy-start.1
  0.0 5.0 %collective-permute-start.6 = (f32[96,128]{1,0:T(8,128)}, f32[96,128]{1,0:T(8,128)S(1)}, u32[]{:S(2)}, u32[]{:S(2)}) collective-permute-start(f32[96,128]{1,0:T(8,128)} %bitcast.3), channel_id=1, source_target_pairs={{4,0},{5,1},{6,2},{7,3},{8,4},{9,5},{10,6},{11,7},{12,8},{13,9},{1... | collective-permute-start | bytes 147464 | tf_op jit(solution)/shard_map/ppermute | solution.py:114
  5.1 1.5 %collective-permute-start = (bf16[1,12288]{1,0:T(2,128)(2,1)}, bf16[1,12288]{1,0:T(2,128)(2,1)S(1)}, u32[]{:S(2)}, u32[]{:S(2)}) collective-permute-start(bf16[1,12288]{1,0:T(2,128)(2,1)} %refs_10_.1), channel_id=1, source_target_pairs={{16,0},{17,1},{18,2},{19,3},{20,4},{21,5},{22,6},{23,7},{24,8},{25... | collective-permute-start | bytes 73736 | tf_op jit(solution)/shard_map/ppermute | solution.py:114
  6.6 0.0 collective-permute-start.5
  6.6 1.0 %collective-permute-start.4 = (f32[96,128]{1,0:T(8,128)}, f32[96,128]{1,0:T(8,128)S(1)}, u32[]{:S(2)}, u32[]{:S(2)}) collective-permute-start(f32[96,128]{1,0:T(8,128)} %bitcast.5), channel_id=1, source_target_pairs={{12,0},{13,1},{14,2},{15,3},{0,4},{1,5},{2,6},{3,7},{4,8},{5,9},{6... | collective-permute-start | bytes 147464 | tf_op jit(solution)/shard_map/ppermute | solution.py:114
  7.6 1.4 %collective-permute-start.3 = (f32[96,128]{1,0:T(8,128)}, f32[96,128]{1,0:T(8,128)S(1)}, u32[]{:S(2)}, u32[]{:S(2)}) collective-permute-start(f32[96,128]{1,0:T(8,128)} %bitcast.6), channel_id=1, source_target_pairs={{18,0},{19,1},{16,2},{17,3},{22,4},{23,5},{20,6},{21,7},{26,8},{27... | collective-permute-start | bytes 147464 | tf_op jit(solution)/shard_map/ppermute | solution.py:114
  9.0 0.3 %collective-permute-done.refs_11_ = bf16[1,12288]{1,0:T(2,128)(2,1)S(1)} collective-permute-done((bf16[1,12288]{1,0:T(2,128)(2,1)}, bf16[1,12288]{1,0:T(2,128)(2,1)S(1)}, u32[]{:S(2)}, u32[]{:S(2)}) %collective-permute-start) | collective-permute-done | bytes 24608 | tf_op jit(solution)/shard_map/ppermute | solution.py:114
  9.4 2.0 %collective-permute-start.2 = (f32[96,128]{1,0:T(8,128)}, f32[96,128]{1,0:T(8,128)S(1)}, u32[]{:S(2)}, u32[]{:S(2)}) collective-permute-start(f32[96,128]{1,0:T(8,128)} %bitcast.7), channel_id=1, source_target_pairs={{16,0},{17,1},{18,2},{19,3},{20,4},{21,5},{22,6},{23,7},{24,8},{25... | collective-permute-start | bytes 147464 | tf_op jit(solution)/shard_map/ppermute | solution.py:114
  11.4 0.0 collective-permute-done.6.refs_6_
  11.4 1.5 %collective-permute-start.1 = (f32[96,128]{1,0:T(8,128)}, f32[96,128]{1,0:T(8,128)S(1)}, u32[]{:S(2)}, u32[]{:S(2)}) collective-permute-start(f32[96,128]{1,0:T(8,128)} %bitcast.8), channel_id=1, source_target_pairs={{2,0},{3,1},{0,2},{1,3},{6,4},{7,5},{4,6},{5,7},{10,8},{11,9},{8,1... | collective-permute-start | bytes 147464 | tf_op jit(solution)/shard_map/ppermute | solution.py:114
  12.9 0.0 collective-permute-done.5.refs_5_
  12.9 0.0 collective-permute-done.4.refs_4_
  12.9 0.0 collective-permute-done.3.refs_3_
  12.9 0.8 %collective-permute-done.2.refs_2_ = f32[96,128]{1,0:T(8,128)S(1)} collective-permute-done((f32[96,128]{1,0:T(8,128)}, f32[96,128]{1,0:T(8,128)S(1)}, u32[]{:S(2)}, u32[]{:S(2)}) %collective-permute-start.2) | collective-permute-done | bytes 49184 | tf_op jit(solution)/shard_map/ppermute | solution.py:114
  13.7 2.0 %collective-permute-done.1.refs_1_ = f32[96,128]{1,0:T(8,128)S(1)} collective-permute-done((f32[96,128]{1,0:T(8,128)}, f32[96,128]{1,0:T(8,128)S(1)}, u32[]{:S(2)}, u32[]{:S(2)}) %collective-permute-start.1) | collective-permute-done | bytes 49184 | tf_op jit(solution)/shard_map/ppermute | solution.py:114
  15.7 0.0 copy-start.2
  15.7 0.8 %copy-done.2 = f32[1,12288]{1,0:T(1,128)S(1)} copy-done((f32[1,12288]{1,0:T(1,128)S(1)}, f32[1,12288]{1,0:T(1,128)}, u32[]{:S(2)}) %copy-start.2) | copy-done | bytes 49176
  16.5 0.1 collective-permute-start.7
  16.6 1.0 %collective-permute-start.10 = (bf16[3,96,128]{2,1,0:T(8,128)(2,1)S(1)}, bf16[3,96,128]{2,1,0:T(8,128)(2,1)S(1)}, u32[]{:S(2)}, u32[]{:S(2)}) collective-permute-start(bf16[3,96,128]{2,1,0:T(8,128)(2,1)S(1)} %get-tuple-element.21.refs_2_), channel_id=1, source_target_pairs={{18,0},{19,1},{16,2},{17,3},{22,4},{23,5},{20,6},{21,7},{26,8},{27... | collective-permute-start | bytes 221192 | tf_op jit(solution)/shard_map/ppermute | solution.py:114
  17.6 2.0 %collective-permute-start.9 = (bf16[3,96,128]{2,1,0:T(8,128)(2,1)S(1)}, bf16[3,96,128]{2,1,0:T(8,128)(2,1)S(1)}, u32[]{:S(2)}, u32[]{:S(2)}) collective-permute-start(bf16[3,96,128]{2,1,0:T(8,128)(2,1)S(1)} %get-tuple-element.21.refs_2_), channel_id=1, source_target_pairs={{16,0},{17,1},{18,2},{19,3},{20,4},{21,5},{22,6},{23,7},{24,8},{25... | collective-permute-start | bytes 221192 | tf_op jit(solution)/shard_map/ppermute | solution.py:114
  19.6 0.5 %collective-permute-start.8 = (bf16[3,96,128]{2,1,0:T(8,128)(2,1)S(1)}, bf16[3,96,128]{2,1,0:T(8,128)(2,1)S(1)}, u32[]{:S(2)}, u32[]{:S(2)}) collective-permute-start(bf16[3,96,128]{2,1,0:T(8,128)(2,1)S(1)} %get-tuple-element.21.refs_2_), channel_id=1, source_target_pairs={{2,0},{3,1},{0,2},{1,3},{6,4},{7,5},{4,6},{5,7},{10,8},{11,9},{8,1... | collective-permute-start | bytes 221192 | tf_op jit(solution)/shard_map/ppermute | solution.py:114
  20.2 0.0 collective-permute-start.11
  20.2 2.4 %collective-permute-done.10.refs_5_ = bf16[3,96,128]{2,1,0:T(8,128)(2,1)S(1)} collective-permute-done((bf16[3,96,128]{2,1,0:T(8,128)(2,1)S(1)}, bf16[3,96,128]{2,1,0:T(8,128)(2,1)S(1)}, u32[]{:S(2)}, u32[]{:S(2)}) %collective-permute-start.10) | collective-permute-done | bytes 73760 | tf_op jit(solution)/shard_map/ppermute | solution.py:114
  22.6 0.0 collective-permute-start.14
  22.6 1.2 %collective-permute-done.9.refs_4_ = bf16[3,96,128]{2,1,0:T(8,128)(2,1)S(1)} collective-permute-done((bf16[3,96,128]{2,1,0:T(8,128)(2,1)S(1)}, bf16[3,96,128]{2,1,0:T(8,128)(2,1)S(1)}, u32[]{:S(2)}, u32[]{:S(2)}) %collective-permute-start.9) | collective-permute-done | bytes 73760 | tf_op jit(solution)/shard_map/ppermute | solution.py:114
  23.8 0.1 collective-permute-start.13
  23.8 0.1 collective-permute-done.8.refs_3_
  24.0 0.3 %collective-permute-start.12 = (bf16[3,96,128]{2,1,0:T(8,128)(2,1)S(1)}, bf16[3,96,128]{2,1,0:T(8,128)(2,1)S(1)}, u32[]{:S(2)}, u32[]{:S(2)}) collective-permute-start(bf16[3,96,128]{2,1,0:T(8,128)(2,1)S(1)} %collective-permute-done.8.refs_3_), channel_id=1, source_target_pairs={{1,0},{0,1},{3,2},{2,3},{5,4},{4,5},{7,6},{6,7},{9,8},{8,9},{11,10... | collective-permute-start | bytes 221192 | tf_op jit(solution)/shard_map/ppermute | solution.py:114
  24.3 0.0 collective-permute-done.11.refs_6_
  24.3 0.0 collective-permute-done.14.refs_9_
  24.3 0.7 %collective-permute-done.13.refs_8_ = bf16[3,96,128]{2,1,0:T(8,128)(2,1)S(1)} collective-permute-done((bf16[3,96,128]{2,1,0:T(8,128)(2,1)S(1)}, bf16[3,96,128]{2,1,0:T(8,128)(2,1)S(1)}, u32[]{:S(2)}, u32[]{:S(2)}) %collective-permute-start.13) | collective-permute-done | bytes 73760 | tf_op jit(solution)/shard_map/ppermute | solution.py:114
  25.0 0.2 collective-permute-done.12.refs_7_
  25.3 0.0 collective-permute-done.7.refs_1_
  25.3 0.0 copy-done
  25.3 0.0 copy-done.1
  25.3 4.8 %shard_map.47 = f32[1,12288]{1,0:T(1,128)} custom-call(s32[7,24]{1,0:T(8,128)S(1)} %bitcast.2, f32[4,96,128]{2,1,0:T(8,128)S(1)} %get-tuple-element.20.refs_0_, f32[4,96,128]{2,1,0:T(8,128)S(1)} %collective-permute-done.7.refs_1_, bf16[3,96,128]{2,1,0:T(8,128)(2,1)S(1)} %get-tuple-element.21.refs_2_, bf16[3,96,128]{2,1,0:T(8,128)(2,1)S(1)} %collective-permute-done.8.refs_3_, ...), custom_call_target="tpu_custom_call" | custom-call | tf_op jit(solution)/shard_map/pallas_call | solution.py:174
  (1 shorter events, 0.0 us)
Async XLA Ops:
  0.0 25.3 %copy-start = (bf16[1,12288]{1,0:T(2,128)(2,1)S(1)}, bf16[1,12288]{1,0:T(2,128)(2,1)}, u32[]{:S(2)}) copy-start(bf16[1,12288]{1,0:T(2,128)(2,1)} %refs_10_.1) | copy-start | bytes 73732
  0.0 25.3 %copy-start.1 = (s32[24,7]{0,1:T(8,128)S(1)}, s32[24,7]{0,1:T(8,128)}, u32[]{:S(2)}) copy-start(s32[24,7]{0,1:T(8,128)} %param.6) | copy-start | bytes 2020
  0.0 11.4 %collective-permute-start.6 = (f32[96,128]{1,0:T(8,128)}, f32[96,128]{1,0:T(8,128)S(1)}, u32[]{:S(2)}, u32[]{:S(2)}) collective-permute-start(f32[96,128]{1,0:T(8,128)} %bitcast.3), channel_id=1, source_target_pairs={{4,0},{5,1},{6,2},{7,3},{8,4},{9,5},{10,6},{11,7},{12,8},{13,9},{1... | collective-permute-start | bytes 147464 | tf_op jit(solution)/shard_map/ppermute | solution.py:114
  5.1 4.3 %collective-permute-start = (bf16[1,12288]{1,0:T(2,128)(2,1)}, bf16[1,12288]{1,0:T(2,128)(2,1)S(1)}, u32[]{:S(2)}, u32[]{:S(2)}) collective-permute-start(bf16[1,12288]{1,0:T(2,128)(2,1)} %refs_10_.1), channel_id=1, source_target_pairs={{16,0},{17,1},{18,2},{19,3},{20,4},{21,5},{22,6},{23,7},{24,8},{25... | collective-permute-start | bytes 73736 | tf_op jit(solution)/shard_map/ppermute | solution.py:114
  6.6 6.3 %collective-permute-start.5 = (f32[96,128]{1,0:T(8,128)}, f32[96,128]{1,0:T(8,128)S(1)}, u32[]{:S(2)}, u32[]{:S(2)}) collective-permute-start(f32[96,128]{1,0:T(8,128)} %bitcast.4), channel_id=1, source_target_pairs={{8,0},{9,1},{10,2},{11,3},{12,4},{13,5},{14,6},{15,7},{0,8},{1,9},... | collective-permute-start | bytes 147464 | tf_op jit(solution)/shard_map/ppermute | solution.py:114
  6.6 6.3 %collective-permute-start.4 = (f32[96,128]{1,0:T(8,128)}, f32[96,128]{1,0:T(8,128)S(1)}, u32[]{:S(2)}, u32[]{:S(2)}) collective-permute-start(f32[96,128]{1,0:T(8,128)} %bitcast.5), channel_id=1, source_target_pairs={{12,0},{13,1},{14,2},{15,3},{0,4},{1,5},{2,6},{3,7},{4,8},{5,9},{6... | collective-permute-start | bytes 147464 | tf_op jit(solution)/shard_map/ppermute | solution.py:114
  7.6 5.3 %collective-permute-start.3 = (f32[96,128]{1,0:T(8,128)}, f32[96,128]{1,0:T(8,128)S(1)}, u32[]{:S(2)}, u32[]{:S(2)}) collective-permute-start(f32[96,128]{1,0:T(8,128)} %bitcast.6), channel_id=1, source_target_pairs={{18,0},{19,1},{16,2},{17,3},{22,4},{23,5},{20,6},{21,7},{26,8},{27... | collective-permute-start | bytes 147464 | tf_op jit(solution)/shard_map/ppermute | solution.py:114
  9.4 4.3 %collective-permute-start.2 = (f32[96,128]{1,0:T(8,128)}, f32[96,128]{1,0:T(8,128)S(1)}, u32[]{:S(2)}, u32[]{:S(2)}) collective-permute-start(f32[96,128]{1,0:T(8,128)} %bitcast.7), channel_id=1, source_target_pairs={{16,0},{17,1},{18,2},{19,3},{20,4},{21,5},{22,6},{23,7},{24,8},{25... | collective-permute-start | bytes 147464 | tf_op jit(solution)/shard_map/ppermute | solution.py:114
  11.4 4.3 %collective-permute-start.1 = (f32[96,128]{1,0:T(8,128)}, f32[96,128]{1,0:T(8,128)S(1)}, u32[]{:S(2)}, u32[]{:S(2)}) collective-permute-start(f32[96,128]{1,0:T(8,128)} %bitcast.8), channel_id=1, source_target_pairs={{2,0},{3,1},{0,2},{1,3},{6,4},{7,5},{4,6},{5,7},{10,8},{11,9},{8,1... | collective-permute-start | bytes 147464 | tf_op jit(solution)/shard_map/ppermute | solution.py:114
  15.7 0.8 %copy-start.2 = (f32[1,12288]{1,0:T(1,128)S(1)}, f32[1,12288]{1,0:T(1,128)}, u32[]{:S(2)}) copy-start(f32[1,12288]{1,0:T(1,128)} %param.4) | copy-start | bytes 147460
  16.5 8.7 %collective-permute-start.7 = (f32[4,96,128]{2,1,0:T(8,128)S(1)}, f32[4,96,128]{2,1,0:T(8,128)S(1)}, u32[]{:S(2)}, u32[]{:S(2)}) collective-permute-start(f32[4,96,128]{2,1,0:T(8,128)S(1)} %get-tuple-element.20.refs_0_), channel_id=1, source_target_pairs={{1,0},{0,1},{3,2},{2,3},{5,4},{4,5},{7,6},{6,7},{9,8},{8,9},{11,10... | collective-permute-start | bytes 589832 | tf_op jit(solution)/shard_map/ppermute | solution.py:114
  16.6 6.0 %collective-permute-start.10 = (bf16[3,96,128]{2,1,0:T(8,128)(2,1)S(1)}, bf16[3,96,128]{2,1,0:T(8,128)(2,1)S(1)}, u32[]{:S(2)}, u32[]{:S(2)}) collective-permute-start(bf16[3,96,128]{2,1,0:T(8,128)(2,1)S(1)} %get-tuple-element.21.refs_2_), channel_id=1, source_target_pairs={{18,0},{19,1},{16,2},{17,3},{22,4},{23,5},{20,6},{21,7},{26,8},{27... | collective-permute-start | bytes 221192 | tf_op jit(solution)/shard_map/ppermute | solution.py:114
  17.6 6.2 %collective-permute-start.9 = (bf16[3,96,128]{2,1,0:T(8,128)(2,1)S(1)}, bf16[3,96,128]{2,1,0:T(8,128)(2,1)S(1)}, u32[]{:S(2)}, u32[]{:S(2)}) collective-permute-start(bf16[3,96,128]{2,1,0:T(8,128)(2,1)S(1)} %get-tuple-element.21.refs_2_), channel_id=1, source_target_pairs={{16,0},{17,1},{18,2},{19,3},{20,4},{21,5},{22,6},{23,7},{24,8},{25... | collective-permute-start | bytes 221192 | tf_op jit(solution)/shard_map/ppermute | solution.py:114
  19.6 4.4 %collective-permute-start.8 = (bf16[3,96,128]{2,1,0:T(8,128)(2,1)S(1)}, bf16[3,96,128]{2,1,0:T(8,128)(2,1)S(1)}, u32[]{:S(2)}, u32[]{:S(2)}) collective-permute-start(bf16[3,96,128]{2,1,0:T(8,128)(2,1)S(1)} %get-tuple-element.21.refs_2_), channel_id=1, source_target_pairs={{2,0},{3,1},{0,2},{1,3},{6,4},{7,5},{4,6},{5,7},{10,8},{11,9},{8,1... | collective-permute-start | bytes 221192 | tf_op jit(solution)/shard_map/ppermute | solution.py:114
  20.2 4.1 %collective-permute-start.11 = (bf16[3,96,128]{2,1,0:T(8,128)(2,1)S(1)}, bf16[3,96,128]{2,1,0:T(8,128)(2,1)S(1)}, u32[]{:S(2)}, u32[]{:S(2)}) collective-permute-start(bf16[3,96,128]{2,1,0:T(8,128)(2,1)S(1)} %get-tuple-element.21.refs_2_), channel_id=1, source_target_pairs={{1,0},{0,1},{3,2},{2,3},{5,4},{4,5},{7,6},{6,7},{9,8},{8,9},{11,10... | collective-permute-start | bytes 221192 | tf_op jit(solution)/shard_map/ppermute | solution.py:114
  22.6 1.7 %collective-permute-start.14 = (bf16[3,96,128]{2,1,0:T(8,128)(2,1)S(1)}, bf16[3,96,128]{2,1,0:T(8,128)(2,1)S(1)}, u32[]{:S(2)}, u32[]{:S(2)}) collective-permute-start(bf16[3,96,128]{2,1,0:T(8,128)(2,1)S(1)} %collective-permute-done.10.refs_5_), channel_id=1, source_target_pairs={{1,0},{0,1},{3,2},{2,3},{5,4},{4,5},{7,6},{6,7},{9,8},{8,9},{11,10... | collective-permute-start | bytes 221192 | tf_op jit(solution)/shard_map/ppermute | solution.py:114
  23.8 1.3 %collective-permute-start.13 = (bf16[3,96,128]{2,1,0:T(8,128)(2,1)S(1)}, bf16[3,96,128]{2,1,0:T(8,128)(2,1)S(1)}, u32[]{:S(2)}, u32[]{:S(2)}) collective-permute-start(bf16[3,96,128]{2,1,0:T(8,128)(2,1)S(1)} %collective-permute-done.9.refs_4_), channel_id=1, source_target_pairs={{1,0},{0,1},{3,2},{2,3},{5,4},{4,5},{7,6},{6,7},{9,8},{8,9},{11,10... | collective-permute-start | bytes 221192 | tf_op jit(solution)/shard_map/ppermute | solution.py:114
  24.0 1.3 %collective-permute-start.12 = (bf16[3,96,128]{2,1,0:T(8,128)(2,1)S(1)}, bf16[3,96,128]{2,1,0:T(8,128)(2,1)S(1)}, u32[]{:S(2)}, u32[]{:S(2)}) collective-permute-start(bf16[3,96,128]{2,1,0:T(8,128)(2,1)S(1)} %collective-permute-done.8.refs_3_), channel_id=1, source_target_pairs={{1,0},{0,1},{3,2},{2,3},{5,4},{4,5},{7,6},{6,7},{9,8},{8,9},{11,10... | collective-permute-start | bytes 221192 | tf_op jit(solution)/shard_map/ppermute | solution.py:114

commit v6 on v5

--- a/solution.py
+++ b/solution.py
@@ -13,23 +13,36 @@
 PACK_COST = 20_000_000_000
 
 
-def pack_kernel(*refs):
-    diff_ref, bases_ref = refs[-2:]
-    bases, line = refs[:4], refs[4:-2]
-    base = bases[0][...]
+def split_kernel(base_ref, split_ref):
+    base = base_ref[...]
+    high = base.astype(jnp.bfloat16)
+    rest = base - high.astype(jnp.float32)
+    middle = rest.astype(jnp.bfloat16)
+    split_ref[0] = high
+    split_ref[1] = middle
+    split_ref[2] = (rest - middle.astype(jnp.float32)).astype(jnp.bfloat16)
+
+
+def joined(parts):
+    high, middle, low = (part.astype(jnp.float32) for part in parts)
+    return high + middle + low
+
+
+def pack_kernel(split_ref, *refs):
+    line, out_ref = refs[:-1], refs[-1]
+    base = joined([split_ref[i] for i in range(3)])
+    out_ref[0:3] = split_ref[...]
     for j, ref in enumerate(line):
-        diff_ref[j] = (ref[...] - base).astype(jnp.bfloat16)
-    for j, ref in enumerate(bases):
-        bases_ref[j] = ref[...]
+        out_ref[3 + j] = (ref[...] - base).astype(jnp.bfloat16)
 
 
 def product_kernel(group, off_ref, *refs):
-    bases, diffs = refs[:2], refs[2:10]
-    inc_own, inc_other, taper_hbm, out_ref = refs[10:14]
-    tiles, pert, picked_from, picked, acc, sems = refs[14:]
+    groups = refs[:8]
+    inc_own, inc_other, taper_hbm, out_ref = refs[8:12]
+    tiles, pert, picked_from, acc, sems = refs[12:]
     slots, block_size, _ = tiles.shape
     members = 4 * group
-    rows = bases[0].shape[1]
+    rows = groups[0].shape[1]
     pitch = pert.shape[0] // members
     quarters = block_size // LANES
     block_count = rows // quarters
@@ -39,15 +52,15 @@
         copies[-1].start()
 
     def weigh(side, inc_ref):
-        lines = [(c, 2 * side + j) for c in range(2) for j in range(2)]
+        lines = [groups[4 * c + 2 * side + j] for c in range(2) for j in range(2)]
 
         def chunk(r, carry):
             at = pl.multiple_of(r * 2 * SUB, 2 * SUB)
             here = pl.ds(at, 2 * SUB)
-            starts = [bases[c][j, here, :] for c, j in lines]
+            starts = [joined([ref[k, here, :] for k in range(3)]) for ref in lines]
             steps = [
-                [diffs[4 * c + j][k, here, :].astype(jnp.float32) for k in range(group - 1)]
-                for c, j in lines
+                [ref[3 + k, here, :].astype(jnp.float32) for k in range(group - 1)]
+                for ref in lines
             ]
             total = sum(step for line in steps for step in line) + group * sum(starts)
             mean = total * (1.0 / members)
@@ -82,14 +95,17 @@
         preferred_element_type=jnp.float32,
     )
     for s in range(1, slots):
+        chosen = []
         for i in range(block_count):
-            rows_of = slice(i * members, (i + 1) * members)
             place = i + off_ref[s - 1, i]
             place = jnp.where(place < 0, place + 2 * block_count, place)
-            picked[s - 1, rows_of, :] = picked_from[place]
+            chosen.append(picked_from[place])
         copies[s].wait()
         acc[...] += lax.dot_general(
-            picked[s - 1], tiles[s], contract, preferred_element_type=jnp.float32
+            jnp.concatenate(chosen, axis=0),
+            tiles[s],
+            contract,
+            preferred_element_type=jnp.float32,
         )
 
     scale = 1.0 / (members - 1)
@@ -139,55 +155,53 @@
     line = [
         move(base, False, lambda m: (m + 4 * d) % mem_size) for d in reversed(range(1, group))
     ]
-    around = [
-        move(base, False, beside),
-        move(base, True, same),
-        move(base, True, beside),
-    ]
     inc_other = move(increments.reshape(1, columns), True, same)
-    inc_other, around, line = lax.optimization_barrier((inc_other, around, line))
-
     whole = pl.BlockSpec(memory_space=pltpu.VMEM)
-    diff, bases = pl.pallas_call(
+    small = pltpu.CompilerParams(vmem_limit_bytes=4 * 1024 * 1024)
+    split = pl.pallas_call(
+        split_kernel,
+        out_shape=jax.ShapeDtypeStruct((3, rows, LANES), jnp.bfloat16),
+        in_specs=[whole],
+        out_specs=whole,
+        compiler_params=small,
+    )(base)
+    split, inc_other, line = lax.optimization_barrier((split, inc_other, line))
+
+    mine = pl.pallas_call(
         pack_kernel,
-        out_shape=(
-            jax.ShapeDtypeStruct((group - 1, rows, LANES), jnp.bfloat16),
-            jax.ShapeDtypeStruct((4, rows, LANES), jnp.float32),
-        ),
-        in_specs=[whole] * (group + 3),
-        out_specs=(whole,) * 2,
-        compiler_params=pltpu.CompilerParams(vmem_limit_bytes=4 * 1024 * 1024),
+        out_shape=jax.ShapeDtypeStruct((group + 2, rows, LANES), jnp.bfloat16),
+        in_specs=[whole] * group,
+        out_specs=whole,
+        compiler_params=small,
         cost_estimate=pl.CostEstimate(
             flops=PACK_COST, bytes_accessed=8 * columns * 4, transcendentals=0
         ),
-    )(base, *around, *line)
-    diffs = [
-        diff,
-        move(diff, False, beside),
-        move(diff, True, same),
-        move(diff, True, beside),
+    )(split, *line)
+    groups = [
+        mine,
+        move(mine, False, beside),
+        move(mine, True, same),
+        move(mine, True, beside),
     ]
-    bases = [bases, move(bases, False, lambda m: m ^ 1)]
-    diffs += [move(x, False, lambda m: m ^ 1) for x in diffs]
+    groups += [move(x, False, lambda m: m ^ 1) for x in groups]
 
     vectors = mem_size * block_count
     return pl.pallas_call(
         functools.partial(product_kernel, group),
         out_shape=jax.ShapeDtypeStruct((1, columns), jnp.float32),
         in_specs=[pl.BlockSpec(memory_space=pltpu.SMEM)]
-        + [whole] * 12
+        + [whole] * 10
         + [pl.BlockSpec(memory_space=pltpu.HBM)],
         out_specs=whole,
         scratch_shapes=[
             pltpu.VMEM((slots, block_size, block_size), jnp.bfloat16),
             pltpu.VMEM((mem_size * (rows + 1), LANES), jnp.float32),
             pltpu.VMEM((2 * block_count, mem_size, block_size), jnp.bfloat16),
-            pltpu.VMEM((slots - 1, vectors, block_size), jnp.bfloat16),
             pltpu.VMEM((vectors, block_size), jnp.float32),
             pltpu.SemaphoreType.DMA((slots,)),
         ],
         compiler_params=pltpu.CompilerParams(vmem_limit_bytes=VMEM_LIMIT),
-    )(offsets.T, *bases, *diffs, increments, inc_other, taper)
+    )(offsets.T, *groups, increments, inc_other, taper)
 
 
 def solution(mesh):

time: 30.2 us -> 26.2 us (0.87)
  starting transfers between devices: 16.6 us -> 11.7 us
  waiting for transfers between devices: 7.84 us -> 8.7 us
    ppermute x15 -> x11, starting transfers between devices: 16.6 us -> 11.7 us  [one(): return lax.ppermute(x, ('lon', 'mem'), perm)]
    ppermute x15 -> x11, waiting for transfers between devices: 7.84 us -> 8.7 us  [one(): return lax.ppermute(x, ('lon', 'mem'), perm)]
  transfers between devices with their start and end apart: 15 -> 11, of which waited for: 8 -> 7; matrix products, arithmetic and copies ran while one was open for 0% -> 0% of each run, Pallas kernels for 0% -> 0%
where the time goes in v6:
time: 26.2 us; the launch traced here: 26 us
  starting transfers between devices  11.7 us (45%)
  waiting for transfers between devices  8.7 us (33%)
  Pallas kernels  4.82 us (18%)
  local copies, waits for them, and re-layouts  0.81 us (3%)
    ppermute x11, starting transfers between devices, one(): return lax.ppermute(x, ('lon', 'mem'), perm)  11.7 us
    ppermute x11, waiting for transfers between devices, one(): return lax.ppermute(x, ('lon', 'mem'), perm)  8.7 us
    pallas_call x1, Pallas kernels, on_device(): pl.pallas_call(functools.partial(product_kernel, group), out_shape=jax.Sh...  4.79 us
    unnamed x6, local copies, waits for them, and re-layouts  0.81 us
  transfers between devices with their start and end apart: 11, of which 7 were waited for; matrix products, arithmetic and copies ran while one was open for 0% of the time, Pallas kernels for 0%

profile of v6, /device:TPU:0, one launch (start us, length us, event | category | flops | bytes accessed | tf_op | source)
XLA Modules:
  0.0 26.0 jit_solution(2650897744770320693)
XLA Ops:
  0.0 5.0 %collective-permute-start.3 = (f32[96,128]{1,0:T(8,128)}, f32[96,128]{1,0:T(8,128)S(1)}, u32[]{:S(2)}, u32[]{:S(2)}) collective-permute-start(f32[96,128]{1,0:T(8,128)} %bitcast.2), channel_id=1, source_target_pairs={{4,0},{5,1},{6,2},{7,3},{8,4},{9,5},{10,6},{11,7},{12,8},{13,9},{1... | collective-permute-start | bytes 147464 | tf_op jit(solution)/shard_map/ppermute | solution.py:130
  5.0 0.0 collective-permute-start.2
  5.1 1.0 %collective-permute-start.1 = (f32[96,128]{1,0:T(8,128)}, f32[96,128]{1,0:T(8,128)S(1)}, u32[]{:S(2)}, u32[]{:S(2)}) collective-permute-start(f32[96,128]{1,0:T(8,128)} %bitcast.4), channel_id=1, source_target_pairs={{12,0},{13,1},{14,2},{15,3},{0,4},{1,5},{2,6},{3,7},{4,8},{5,9},{6... | collective-permute-start | bytes 147464 | tf_op jit(solution)/shard_map/ppermute | solution.py:130
  6.1 1.5 %collective-permute-start = (bf16[1,12288]{1,0:T(2,128)(2,1)}, bf16[1,12288]{1,0:T(2,128)(2,1)S(1)}, u32[]{:S(2)}, u32[]{:S(2)}) collective-permute-start(bf16[1,12288]{1,0:T(2,128)(2,1)} %refs_8_.1), channel_id=1, source_target_pairs={{16,0},{17,1},{18,2},{19,3},{20,4},{21,5},{22,6},{23,7},{24,8},{25... | collective-permute-start | bytes 73736 | tf_op jit(solution)/shard_map/ppermute | solution.py:130
  7.6 0.0 copy-start.1
  7.6 0.8 %copy-done.1 = f32[1,12288]{1,0:T(1,128)S(1)} copy-done((f32[1,12288]{1,0:T(1,128)S(1)}, f32[1,12288]{1,0:T(1,128)}, u32[]{:S(2)}) %copy-start.1) | copy-done | bytes 49176
  8.4 0.0 copy-start
  8.4 0.0 copy-start.2
  8.4 1.9 %collective-permute-done.refs_9_ = bf16[1,12288]{1,0:T(2,128)(2,1)S(1)} collective-permute-done((bf16[1,12288]{1,0:T(2,128)(2,1)}, bf16[1,12288]{1,0:T(2,128)(2,1)S(1)}, u32[]{:S(2)}, u32[]{:S(2)}) %collective-permute-start) | collective-permute-done | bytes 24608 | tf_op jit(solution)/shard_map/ppermute | solution.py:130
  10.4 0.0 collective-permute-done.3.refs_2_
  10.4 0.0 collective-permute-done.2.refs_1_
  10.4 0.8 %collective-permute-done.1.refs_0_ = f32[96,128]{1,0:T(8,128)S(1)} collective-permute-done((f32[96,128]{1,0:T(8,128)}, f32[96,128]{1,0:T(8,128)S(1)}, u32[]{:S(2)}, u32[]{:S(2)}) %collective-permute-start.1) | collective-permute-done | bytes 49184 | tf_op jit(solution)/shard_map/ppermute | solution.py:130
  11.2 2.5 %collective-permute-start.6 = (bf16[6,96,128]{2,1,0:T(8,128)(2,1)S(1)}, bf16[6,96,128]{2,1,0:T(8,128)(2,1)S(1)}, u32[]{:S(2)}, u32[]{:S(2)}) collective-permute-start(bf16[6,96,128]{2,1,0:T(8,128)(2,1)S(1)} %shard_map.47.refs_0_), channel_id=1, source_target_pairs={{18,0},{19,1},{16,2},{17,3},{22,4},{23,5},{20,6},{21,7},{26,8},{27... | collective-permute-start | bytes 442376 | tf_op jit(solution)/shard_map/ppermute | solution.py:130
  13.7 0.5 %collective-permute-start.5 = (bf16[6,96,128]{2,1,0:T(8,128)(2,1)S(1)}, bf16[6,96,128]{2,1,0:T(8,128)(2,1)S(1)}, u32[]{:S(2)}, u32[]{:S(2)}) collective-permute-start(bf16[6,96,128]{2,1,0:T(8,128)(2,1)S(1)} %shard_map.47.refs_0_), channel_id=1, source_target_pairs={{16,0},{17,1},{18,2},{19,3},{20,4},{21,5},{22,6},{23,7},{24,8},{25... | collective-permute-start | bytes 442376 | tf_op jit(solution)/shard_map/ppermute | solution.py:130
  14.2 0.5 %collective-permute-start.4 = (bf16[6,96,128]{2,1,0:T(8,128)(2,1)S(1)}, bf16[6,96,128]{2,1,0:T(8,128)(2,1)S(1)}, u32[]{:S(2)}, u32[]{:S(2)}) collective-permute-start(bf16[6,96,128]{2,1,0:T(8,128)(2,1)S(1)} %shard_map.47.refs_0_), channel_id=1, source_target_pairs={{2,0},{3,1},{0,2},{1,3},{6,4},{7,5},{4,6},{5,7},{10,8},{11,9},{8,1... | collective-permute-start | bytes 442376 | tf_op jit(solution)/shard_map/ppermute | solution.py:130
  14.7 0.0 collective-permute-start.7
  14.7 4.1 %collective-permute-done.6.refs_3_ = bf16[6,96,128]{2,1,0:T(8,128)(2,1)S(1)} collective-permute-done((bf16[6,96,128]{2,1,0:T(8,128)(2,1)S(1)}, bf16[6,96,128]{2,1,0:T(8,128)(2,1)S(1)}, u32[]{:S(2)}, u32[]{:S(2)}) %collective-permute-start.6) | collective-permute-done | bytes 147488 | tf_op jit(solution)/shard_map/ppermute | solution.py:130
  18.9 0.0 collective-permute-start.10
  18.9 0.8 %collective-permute-done.5.refs_2_ = bf16[6,96,128]{2,1,0:T(8,128)(2,1)S(1)} collective-permute-done((bf16[6,96,128]{2,1,0:T(8,128)(2,1)S(1)}, bf16[6,96,128]{2,1,0:T(8,128)(2,1)S(1)}, u32[]{:S(2)}, u32[]{:S(2)}) %collective-permute-start.5) | collective-permute-done | bytes 147488 | tf_op jit(solution)/shard_map/ppermute | solution.py:130
  19.6 0.0 collective-permute-start.9
  19.6 0.0 collective-permute-done.4.refs_1_
  19.6 0.5 %collective-permute-start.8 = (bf16[6,96,128]{2,1,0:T(8,128)(2,1)S(1)}, bf16[6,96,128]{2,1,0:T(8,128)(2,1)S(1)}, u32[]{:S(2)}, u32[]{:S(2)}) collective-permute-start(bf16[6,96,128]{2,1,0:T(8,128)(2,1)S(1)} %collective-permute-done.4.refs_1_), channel_id=1, source_target_pairs={{1,0},{0,1},{3,2},{2,3},{5,4},{4,5},{7,6},{6,7},{9,8},{8,9},{11,10... | collective-permute-start | bytes 442376 | tf_op jit(solution)/shard_map/ppermute | solution.py:130
  20.2 0.0 collective-permute-done.7.refs_4_
  20.2 0.1 collective-permute-done.10.refs_7_
  20.2 0.8 %collective-permute-done.9.refs_6_ = bf16[6,96,128]{2,1,0:T(8,128)(2,1)S(1)} collective-permute-done((bf16[6,96,128]{2,1,0:T(8,128)(2,1)S(1)}, bf16[6,96,128]{2,1,0:T(8,128)(2,1)S(1)}, u32[]{:S(2)}, u32[]{:S(2)}) %collective-permute-start.9) | collective-permute-done | bytes 147488 | tf_op jit(solution)/shard_map/ppermute | solution.py:130
  21.0 0.2 collective-permute-done.8.refs_5_
  21.2 0.0 copy-done
  21.2 0.0 copy-done.2
  21.2 4.8 %shard_map.48 = f32[1,12288]{1,0:T(1,128)} custom-call(s32[7,24]{1,0:T(8,128)S(1)} %bitcast.6, bf16[6,96,128]{2,1,0:T(8,128)(2,1)S(1)} %shard_map.47.refs_0_, bf16[6,96,128]{2,1,0:T(8,128)(2,1)S(1)} %collective-permute-done.4.refs_1_, bf16[6,96,128]{2,1,0:T(8,128)(2,1)S(1)} %collective-permute-done.5.refs_2_, ...), custom_call_target="tpu_custom_call" | custom-call | tf_op jit(solution)/shard_map/pallas_call | solution.py:189
  (2 shorter events, 0.0 us)
Async XLA Ops:
  0.0 10.4 %collective-permute-start.3 = (f32[96,128]{1,0:T(8,128)}, f32[96,128]{1,0:T(8,128)S(1)}, u32[]{:S(2)}, u32[]{:S(2)}) collective-permute-start(f32[96,128]{1,0:T(8,128)} %bitcast.2), channel_id=1, source_target_pairs={{4,0},{5,1},{6,2},{7,3},{8,4},{9,5},{10,6},{11,7},{12,8},{13,9},{1... | collective-permute-start | bytes 147464 | tf_op jit(solution)/shard_map/ppermute | solution.py:130
  5.0 5.3 %collective-permute-start.2 = (f32[96,128]{1,0:T(8,128)}, f32[96,128]{1,0:T(8,128)S(1)}, u32[]{:S(2)}, u32[]{:S(2)}) collective-permute-start(f32[96,128]{1,0:T(8,128)} %bitcast.3), channel_id=1, source_target_pairs={{8,0},{9,1},{10,2},{11,3},{12,4},{13,5},{14,6},{15,7},{0,8},{1,9},... | collective-permute-start | bytes 147464 | tf_op jit(solution)/shard_map/ppermute | solution.py:130
  5.1 6.1 %collective-permute-start.1 = (f32[96,128]{1,0:T(8,128)}, f32[96,128]{1,0:T(8,128)S(1)}, u32[]{:S(2)}, u32[]{:S(2)}) collective-permute-start(f32[96,128]{1,0:T(8,128)} %bitcast.4), channel_id=1, source_target_pairs={{12,0},{13,1},{14,2},{15,3},{0,4},{1,5},{2,6},{3,7},{4,8},{5,9},{6... | collective-permute-start | bytes 147464 | tf_op jit(solution)/shard_map/ppermute | solution.py:130
  6.1 4.3 %collective-permute-start = (bf16[1,12288]{1,0:T(2,128)(2,1)}, bf16[1,12288]{1,0:T(2,128)(2,1)S(1)}, u32[]{:S(2)}, u32[]{:S(2)}) collective-permute-start(bf16[1,12288]{1,0:T(2,128)(2,1)} %refs_8_.1), channel_id=1, source_target_pairs={{16,0},{17,1},{18,2},{19,3},{20,4},{21,5},{22,6},{23,7},{24,8},{25... | collective-permute-start | bytes 73736 | tf_op jit(solution)/shard_map/ppermute | solution.py:130
  7.6 0.8 %copy-start.1 = (f32[1,12288]{1,0:T(1,128)S(1)}, f32[1,12288]{1,0:T(1,128)}, u32[]{:S(2)}) copy-start(f32[1,12288]{1,0:T(1,128)} %param.4) | copy-start | bytes 147460
  8.4 12.8 %copy-start = (bf16[1,12288]{1,0:T(2,128)(2,1)S(1)}, bf16[1,12288]{1,0:T(2,128)(2,1)}, u32[]{:S(2)}) copy-start(bf16[1,12288]{1,0:T(2,128)(2,1)} %refs_8_.1) | copy-start | bytes 73732
  8.4 12.8 %copy-start.2 = (s32[24,7]{0,1:T(8,128)S(1)}, s32[24,7]{0,1:T(8,128)}, u32[]{:S(2)}) copy-start(s32[24,7]{0,1:T(8,128)} %param.6) | copy-start | bytes 2020
  11.2 7.7 %collective-permute-start.6 = (bf16[6,96,128]{2,1,0:T(8,128)(2,1)S(1)}, bf16[6,96,128]{2,1,0:T(8,128)(2,1)S(1)}, u32[]{:S(2)}, u32[]{:S(2)}) collective-permute-start(bf16[6,96,128]{2,1,0:T(8,128)(2,1)S(1)} %shard_map.47.refs_0_), channel_id=1, source_target_pairs={{18,0},{19,1},{16,2},{17,3},{22,4},{23,5},{20,6},{21,7},{26,8},{27... | collective-permute-start | bytes 442376 | tf_op jit(solution)/shard_map/ppermute | solution.py:130
  13.7 6.0 %collective-permute-start.5 = (bf16[6,96,128]{2,1,0:T(8,128)(2,1)S(1)}, bf16[6,96,128]{2,1,0:T(8,128)(2,1)S(1)}, u32[]{:S(2)}, u32[]{:S(2)}) collective-permute-start(bf16[6,96,128]{2,1,0:T(8,128)(2,1)S(1)} %shard_map.47.refs_0_), channel_id=1, source_target_pairs={{16,0},{17,1},{18,2},{19,3},{20,4},{21,5},{22,6},{23,7},{24,8},{25... | collective-permute-start | bytes 442376 | tf_op jit(solution)/shard_map/ppermute | solution.py:130
  14.2 5.4 %collective-permute-start.4 = (bf16[6,96,128]{2,1,0:T(8,128)(2,1)S(1)}, bf16[6,96,128]{2,1,0:T(8,128)(2,1)S(1)}, u32[]{:S(2)}, u32[]{:S(2)}) collective-permute-start(bf16[6,96,128]{2,1,0:T(8,128)(2,1)S(1)} %shard_map.47.refs_0_), channel_id=1, source_target_pairs={{2,0},{3,1},{0,2},{1,3},{6,4},{7,5},{4,6},{5,7},{10,8},{11,9},{8,1... | collective-permute-start | bytes 442376 | tf_op jit(solution)/shard_map/ppermute | solution.py:130
  14.7 5.4 %collective-permute-start.7 = (bf16[6,96,128]{2,1,0:T(8,128)(2,1)S(1)}, bf16[6,96,128]{2,1,0:T(8,128)(2,1)S(1)}, u32[]{:S(2)}, u32[]{:S(2)}) collective-permute-start(bf16[6,96,128]{2,1,0:T(8,128)(2,1)S(1)} %shard_map.47.refs_0_), channel_id=1, source_target_pairs={{1,0},{0,1},{3,2},{2,3},{5,4},{4,5},{7,6},{6,7},{9,8},{8,9},{11,10... | collective-permute-start | bytes 442376 | tf_op jit(solution)/shard_map/ppermute | solution.py:130
  18.9 1.4 %collective-permute-start.10 = (bf16[6,96,128]{2,1,0:T(8,128)(2,1)S(1)}, bf16[6,96,128]{2,1,0:T(8,128)(2,1)S(1)}, u32[]{:S(2)}, u32[]{:S(2)}) collective-permute-start(bf16[6,96,128]{2,1,0:T(8,128)(2,1)S(1)} %collective-permute-done.6.refs_3_), channel_id=1, source_target_pairs={{1,0},{0,1},{3,2},{2,3},{5,4},{4,5},{7,6},{6,7},{9,8},{8,9},{11,10... | collective-permute-start | bytes 442376 | tf_op jit(solution)/shard_map/ppermute | solution.py:130
  19.6 1.4 %collective-permute-start.9 = (bf16[6,96,128]{2,1,0:T(8,128)(2,1)S(1)}, bf16[6,96,128]{2,1,0:T(8,128)(2,1)S(1)}, u32[]{:S(2)}, u32[]{:S(2)}) collective-permute-start(bf16[6,96,128]{2,1,0:T(8,128)(2,1)S(1)} %collective-permute-done.5.refs_2_), channel_id=1, source_target_pairs={{1,0},{0,1},{3,2},{2,3},{5,4},{4,5},{7,6},{6,7},{9,8},{8,9},{11,10... | collective-permute-start | bytes 442376 | tf_op jit(solution)/shard_map/ppermute | solution.py:130
  19.6 1.6 %collective-permute-start.8 = (bf16[6,96,128]{2,1,0:T(8,128)(2,1)S(1)}, bf16[6,96,128]{2,1,0:T(8,128)(2,1)S(1)}, u32[]{:S(2)}, u32[]{:S(2)}) collective-permute-start(bf16[6,96,128]{2,1,0:T(8,128)(2,1)S(1)} %collective-permute-done.4.refs_1_), channel_id=1, source_target_pairs={{1,0},{0,1},{3,2},{2,3},{5,4},{4,5},{7,6},{6,7},{9,8},{8,9},{11,10... | collective-permute-start | bytes 442376 | tf_op jit(solution)/shard_map/ppermute | solution.py:130

commit v7 on v6

v7 whole, which is shorter than its diff:
```python
import functools

import jax
import jax.numpy as jnp
from jax import lax
from jax.experimental import pallas as pl
from jax.experimental.pallas import tpu as pltpu
from jax.sharding import PartitionSpec as P

LANES = 128
SUB = 8
VMEM_LIMIT = 49 * 1024 * 1024
PACK_COST = 20_000_000_000
OWN_COST = 1_500_000_000


def split_kernel(base_ref, split_ref):
    base = base_ref[...]
    high = base.astype(jnp.bfloat16)
    rest = base - high.astype(jnp.float32)
    middle = rest.astype(jnp.bfloat16)
    split_ref[0] = high
    split_ref[1] = middle
    split_ref[2] = (rest - middle.astype(jnp.float32)).astype(jnp.bfloat16)


def joined(parts):
    high, middle, low = (part.astype(jnp.float32) for part in parts)
    return high + middle + low


def pack_kernel(split_ref, *refs):
    line, out_ref = refs[:-1], refs[-1]
    base = joined([split_ref[i] for i in range(3)])
    out_ref[0:3] = split_ref[...]
    for j, ref in enumerate(line):
        out_ref[3 + j] = (ref[...] - base).astype(jnp.bfloat16)


def state_rows(lines, here, group):
    starts = [joined([ref[k, here, :] for k in range(3)]) for ref in lines]
    steps = [[ref[3 + k, here, :].astype(jnp.float32) for k in range(group - 1)] for ref in lines]
    return starts, steps


def perturb_rows(lines, pert, group):
    members = 4 * group
    rows = lines[0].shape[1]
    pitch = pert.shape[0] // members

    def chunk(r, carry):
        at = pl.multiple_of(r * 2 * SUB, 2 * SUB)
        starts, steps = state_rows(lines, pl.ds(at, 2 * SUB), group)
        total = sum(step for line in steps for step in line) + group * sum(starts)
        mean = total * (1.0 / members)
        m = 0
        for start, line in zip(starts, steps):
            start = start - mean
            for value in [start] + [start + step for step in line]:
                pert[pl.ds(m * pitch + at, 2 * SUB), :] = value
                m += 1
        return carry

    lax.fori_loop(0, rows // (2 * SUB), chunk, 0, unroll=2)


def spread_rows(pert, members, inc_ref, weighted_ref, wide_ref=None):
    block_count, _, block_size = weighted_ref.shape
    pitch = pert.shape[0] // members
    for i in range(block_count):
        for q in range(block_size // LANES):
            lanes = slice(q * LANES, (q + 1) * LANES)
            at = i * (block_size // LANES) + q
            inc = inc_ref[:, at * LANES : (at + 1) * LANES].astype(jnp.float32)
            part = pert[pl.ds(at, members, pitch), :]
            if wide_ref is not None:
                wide_ref[i, :, lanes] = part
            weighted_ref[i, :, lanes] = (part * inc).astype(jnp.bfloat16)


CONTRACT = (((1,), (1,)), ((), ()))


def own_kernel(group, *refs):
    lines, (inc_ref, taper_hbm) = refs[:4], refs[4:6]
    weighted_ref, wide_ref, acc_ref, tile, pert, sem = refs[6:]
    block_count, members, block_size = weighted_ref.shape
    copy = pltpu.make_async_copy(taper_hbm.at[0], tile, sem)
    copy.start()
    perturb_rows(lines, pert, group)
    spread_rows(pert, members, inc_ref, weighted_ref, wide_ref)
    copy.wait()
    acc_ref[...] = lax.dot_general(
        weighted_ref[...].reshape(block_count * members, block_size),
        tile[...],
        CONTRACT,
        preferred_element_type=jnp.float32,
    )


def product_kernel(group, off_ref, *refs):
    own_ref, wide_ref, first_ref = refs[:3]
    lines, (inc_ref, taper_hbm, out_ref) = refs[3:7], refs[7:10]
    tiles, pert, picked_from, acc, sems = refs[10:]
    slots, block_size, _ = taper_hbm.shape
    block_count, members, _ = own_ref.shape
    copies = []
    for s in range(1, slots):
        copies.append(pltpu.make_async_copy(taper_hbm.at[s], tiles.at[s - 1], sems.at[s - 1]))
        copies[-1].start()

    picked_from[0:block_count] = own_ref[...]
    perturb_rows(lines, pert, group)
    spread_rows(pert, members, inc_ref, picked_from.at[pl.ds(block_count, block_count)])

    for s in range(1, slots):
        chosen = []
        for i in range(block_count):
            place = i + off_ref[s - 1, i]
            place = jnp.where(place < 0, place + 2 * block_count, place)
            chosen.append(picked_from[place])
        copies[s - 1].wait()
        so_far = first_ref[...] if s == 1 else acc[...]
        acc[...] = so_far + lax.dot_general(
            jnp.concatenate(chosen, axis=0),
            tiles[s - 1],
            CONTRACT,
            preferred_element_type=jnp.float32,
        )

    scale = 1.0 / (members - 1)
    for i in range(block_count):
        for q in range(block_size // LANES):
            lanes = slice(q * LANES, (q + 1) * LANES)
            term = wide_ref[i, :, lanes] * acc[i * members : (i + 1) * members, lanes]
            row = jnp.sum(term, axis=0, keepdims=True) * scale
            out_ref[:, i * block_size + q * LANES : i * block_size + (q + 1) * LANES] = row


def mover(lon_size, mem_size):
    def one(x, step, mem_of):
        perm = []
        for l in range(lon_size):
            for m in range(mem_size):
                source = ((l + step) % lon_size) * mem_size + mem_of(m)
                perm.append((source, l * mem_size + m))
        return lax.ppermute(x, ("lon", "mem"), perm)

    def move(x, across, mem_of):
        if not across:
            return one(x, 0, mem_of)
        if lon_size == 2:
            return one(x, 1, mem_of)
        axis = x.ndim - 2 if x.shape[-2] > 1 else x.ndim - 1
        right, left = jnp.split(x, 2, axis=axis)
        return jnp.concatenate([one(right, 1, mem_of), one(left, -1, mem_of)], axis=axis)

    return move


def on_device(ensemble, increments, offsets, taper):
    lon_size, mem_size = lax.axis_size("lon"), lax.axis_size("mem")
    group = mem_size // 4
    slots, block_size, _ = taper.shape
    block_count = offsets.shape[0]
    columns = ensemble.shape[1]
    rows = columns // LANES
    move = mover(lon_size, mem_size)
    same, beside = (lambda m: m), (lambda m: m ^ 2)

    base = ensemble.reshape(rows, LANES)
    if group & (group - 1):
        turn = lambda d: lambda m: (m + 4 * d) % mem_size
    else:
        turn = lambda d: lambda m: m ^ (4 * d)
    line = [move(base, False, turn(d)) for d in range(1, group)]
    inc_other = move(increments.reshape(1, columns), True, same)
    whole = pl.BlockSpec(memory_space=pltpu.VMEM)
    small = pltpu.CompilerParams(vmem_limit_bytes=4 * 1024 * 1024)
    split = pl.pallas_call(
        split_kernel,
        out_shape=jax.ShapeDtypeStruct((3, rows, LANES), jnp.bfloat16),
        in_specs=[whole],
        out_specs=whole,
        compiler_params=small,
    )(base)
    split, inc_other, line = lax.optimization_barrier((split, inc_other, line))

    mine = pl.pallas_call(
        pack_kernel,
        out_shape=jax.ShapeDtypeStruct((group + 2, rows, LANES), jnp.bfloat16),
        in_specs=[whole] * group,
        out_specs=whole,
        compiler_params=small,
        cost_estimate=pl.CostEstimate(
            flops=PACK_COST, bytes_accessed=8 * columns * 4, transcendentals=0
        ),
    )(split, *line)
    y = move(mine, True, same)
    diag = move(mine, True, beside)
    x = move(mine, False, beside)
    own = [mine, x] + [move(v, False, lambda m: m ^ 1) for v in (mine, x)]
    other = [y, diag] + [move(v, False, lambda m: m ^ 1) for v in (y, diag)]

    vectors = mem_size * block_count
    hbm = pl.BlockSpec(memory_space=pltpu.HBM)
    weighted, wide, first = pl.pallas_call(
        functools.partial(own_kernel, group),
        out_shape=(
            jax.ShapeDtypeStruct((block_count, mem_size, block_size), jnp.bfloat16),
            jax.ShapeDtypeStruct((block_count, mem_size, block_size), jnp.float32),
            jax.ShapeDtypeStruct((vectors, block_size), jnp.float32),
        ),
        in_specs=[whole] * 5 + [hbm],
        out_specs=(whole,) * 3,
        scratch_shapes=[
            pltpu.VMEM((block_size, block_size), jnp.bfloat16),
            pltpu.VMEM((mem_size * (rows + 1), LANES), jnp.float32),
            pltpu.SemaphoreType.DMA,
        ],
        compiler_params=pltpu.CompilerParams(vmem_limit_bytes=VMEM_LIMIT),
        cost_estimate=pl.CostEstimate(
            flops=OWN_COST, bytes_accessed=block_size * block_size * 2, transcendentals=0
        ),
    )(*own, increments, taper)
    return pl.pallas_call(
        functools.partial(product_kernel, group),
        out_shape=jax.ShapeDtypeStruct((1, columns), jnp.float32),
        in_specs=[pl.BlockSpec(memory_space=pltpu.SMEM)] + [whole] * 8 + [hbm],
        out_specs=whole,
        scratch_shapes=[
            pltpu.VMEM((slots - 1, block_size, block_size), jnp.bfloat16),
            pltpu.VMEM((mem_size * (rows + 1), LANES), jnp.float32),
            pltpu.VMEM((2 * block_count, mem_size, block_size), jnp.bfloat16),
            pltpu.VMEM((vectors, block_size), jnp.float32),
            pltpu.SemaphoreType.DMA((slots - 1,)),
        ],
        compiler_params=pltpu.CompilerParams(vmem_limit_bytes=VMEM_LIMIT),
    )(offsets.T, weighted, wide, first, *other, inc_other, taper)


def solution(mesh):
    return jax.shard_map(
        on_device,
        mesh=mesh,
        in_specs=(P("mem", "lon"), P("mem", "lon"), P("lon", None), P()),
        out_specs=P("mem", "lon"),
        check_vma=False,
    )
```

time: 26.2 us -> 27.9 us (1.065)
  Pallas kernels: 4.82 us -> 6.11 us
  waiting for transfers between devices: 8.7 us -> 9.74 us
  starting transfers between devices: 11.7 us -> 10.9 us
    pallas_call x0 -> x1, Pallas kernels: none -> 1.45 us  [on_device(): pl.pallas_call(functools.partial(own_kernel, group), out_shape=(jax.Shape...]
    ppermute x11, waiting for transfers between devices: 8.7 us -> 9.74 us  [one(): return lax.ppermute(x, ('lon', 'mem'), perm)]
    ppermute x11, starting transfers between devices: 11.7 us -> 10.9 us  [one(): return lax.ppermute(x, ('lon', 'mem'), perm)]
  transfers between devices with their start and end apart: 11 -> 11, of which waited for: 7 -> 5; matrix products, arithmetic and copies ran while one was open for 0% -> 0% of each run, Pallas kernels for 0% -> 5%
where the time goes in v7:
time: 27.9 us; the launch traced here: 27.7 us
  starting transfers between devices  10.9 us (39%)
  waiting for transfers between devices  9.74 us (35%)
  Pallas kernels  6.11 us (22%)
  local copies, waits for them, and re-layouts  0.81 us (3%)
    ppermute x11, starting transfers between devices, one(): return lax.ppermute(x, ('lon', 'mem'), perm)  10.9 us
    ppermute x11, waiting for transfers between devices, one(): return lax.ppermute(x, ('lon', 'mem'), perm)  9.74 us
    pallas_call x1, Pallas kernels, on_device(): pl.pallas_call(functools.partial(product_kernel, group), out_shape=jax.Sh...  4.62 us
    pallas_call x1, Pallas kernels, on_device(): pl.pallas_call(functools.partial(own_kernel, group), out_shape=(jax.Shape...  1.45 us
    unnamed x6, local copies, waits for them, and re-layouts  0.81 us
  transfers between devices with their start and end apart: 11, of which 5 were waited for; matrix products, arithmetic and copies ran while one was open for 0% of the time, Pallas kernels for 5%

profile of v7, /device:TPU:0, one launch (start us, length us, event | category | flops | bytes accessed | tf_op | source)
XLA Modules:
  0.0 27.7 jit_solution(7393705324102828309)
XLA Ops:
  0.0 3.0 %collective-permute-start.1 = (f32[96,128]{1,0:T(8,128)}, f32[96,128]{1,0:T(8,128)S(1)}, u32[]{:S(2)}, u32[]{:S(2)}) collective-permute-start(f32[96,128]{1,0:T(8,128)} %bitcast.2), channel_id=1, source_target_pairs={{4,0},{5,1},{6,2},{7,3},{0,4},{1,5},{2,6},{3,7},{12,8},{13,9},{14,... | collective-permute-start | bytes 147464 | tf_op jit(solution)/shard_map/ppermute | solution.py:147
  3.0 2.6 %collective-permute-start.2 = (f32[96,128]{1,0:T(8,128)}, f32[96,128]{1,0:T(8,128)S(1)}, u32[]{:S(2)}, u32[]{:S(2)}) collective-permute-start(f32[96,128]{1,0:T(8,128)} %bitcast.3), channel_id=1, source_target_pairs={{8,0},{9,1},{10,2},{11,3},{12,4},{13,5},{14,6},{15,7},{0,8},{1,9},... | collective-permute-start | bytes 147464 | tf_op jit(solution)/shard_map/ppermute | solution.py:147
  5.6 0.0 collective-permute-start.3
  5.6 1.7 %collective-permute-start = (bf16[1,12288]{1,0:T(2,128)(2,1)}, bf16[1,12288]{1,0:T(2,128)(2,1)S(1)}, u32[]{:S(2)}, u32[]{:S(2)}) collective-permute-start(bf16[1,12288]{1,0:T(2,128)(2,1)} %refs_4_.1), channel_id=1, source_target_pairs={{16,0},{17,1},{18,2},{19,3},{20,4},{21,5},{22,6},{23,7},{24,8},{25... | collective-permute-start | bytes 73736 | tf_op jit(solution)/shard_map/ppermute | solution.py:147
  7.4 0.0 copy-start
  7.4 0.8 %copy-done = f32[1,12288]{1,0:T(1,128)S(1)} copy-done((f32[1,12288]{1,0:T(1,128)S(1)}, f32[1,12288]{1,0:T(1,128)}, u32[]{:S(2)}) %copy-start) | copy-done | bytes 49176
  8.2 0.0 copy-start.2
  8.2 1.7 %collective-permute-done.refs_7_ = bf16[1,12288]{1,0:T(2,128)(2,1)S(1)} collective-permute-done((bf16[1,12288]{1,0:T(2,128)(2,1)}, bf16[1,12288]{1,0:T(2,128)(2,1)S(1)}, u32[]{:S(2)}, u32[]{:S(2)}) %collective-permute-start) | collective-permute-done | bytes 24608 | tf_op jit(solution)/shard_map/ppermute | solution.py:147
  9.9 0.0 collective-permute-done.1.refs_0_
  9.9 0.0 collective-permute-done.2.refs_1_
  9.9 1.8 %collective-permute-done.3.refs_2_ = f32[96,128]{1,0:T(8,128)S(1)} collective-permute-done((f32[96,128]{1,0:T(8,128)}, f32[96,128]{1,0:T(8,128)S(1)}, u32[]{:S(2)}, u32[]{:S(2)}) %collective-permute-start.3) | collective-permute-done | bytes 49184 | tf_op jit(solution)/shard_map/ppermute | solution.py:147
  11.7 0.0 copy-start.1
  11.8 1.6 %collective-permute-start.4 = (bf16[6,96,128]{2,1,0:T(8,128)(2,1)S(1)}, bf16[6,96,128]{2,1,0:T(8,128)(2,1)S(1)}, u32[]{:S(2)}, u32[]{:S(2)}) collective-permute-start(bf16[6,96,128]{2,1,0:T(8,128)(2,1)S(1)} %shard_map.47.refs_0_), channel_id=1, source_target_pairs={{2,0},{3,1},{0,2},{1,3},{6,4},{7,5},{4,6},{5,7},{10,8},{11,9},{8,1... | collective-permute-start | bytes 442376 | tf_op jit(solution)/shard_map/ppermute | solution.py:147
  13.3 1.5 %collective-permute-start.8 = (bf16[6,96,128]{2,1,0:T(8,128)(2,1)S(1)}, bf16[6,96,128]{2,1,0:T(8,128)(2,1)S(1)}, u32[]{:S(2)}, u32[]{:S(2)}) collective-permute-start(bf16[6,96,128]{2,1,0:T(8,128)(2,1)S(1)} %shard_map.47.refs_0_), channel_id=1, source_target_pairs={{18,0},{19,1},{16,2},{17,3},{22,4},{23,5},{20,6},{21,7},{26,8},{27... | collective-permute-start | bytes 442376 | tf_op jit(solution)/shard_map/ppermute | solution.py:147
  14.8 0.5 %collective-permute-start.7 = (bf16[6,96,128]{2,1,0:T(8,128)(2,1)S(1)}, bf16[6,96,128]{2,1,0:T(8,128)(2,1)S(1)}, u32[]{:S(2)}, u32[]{:S(2)}) collective-permute-start(bf16[6,96,128]{2,1,0:T(8,128)(2,1)S(1)} %shard_map.47.refs_0_), channel_id=1, source_target_pairs={{16,0},{17,1},{18,2},{19,3},{20,4},{21,5},{22,6},{23,7},{24,8},{25... | collective-permute-start | bytes 442376 | tf_op jit(solution)/shard_map/ppermute | solution.py:147
  15.3 0.0 collective-permute-start.5
  15.3 2.7 %collective-permute-done.4.refs_1_ = bf16[6,96,128]{2,1,0:T(8,128)(2,1)S(1)} collective-permute-done((bf16[6,96,128]{2,1,0:T(8,128)(2,1)S(1)}, bf16[6,96,128]{2,1,0:T(8,128)(2,1)S(1)}, u32[]{:S(2)}, u32[]{:S(2)}) %collective-permute-start.4) | collective-permute-done | bytes 147488 | tf_op jit(solution)/shard_map/ppermute | solution.py:147
  18.0 0.0 collective-permute-start.6
  18.0 2.1 %collective-permute-done.8.refs_4_ = bf16[6,96,128]{2,1,0:T(8,128)(2,1)S(1)} collective-permute-done((bf16[6,96,128]{2,1,0:T(8,128)(2,1)S(1)}, bf16[6,96,128]{2,1,0:T(8,128)(2,1)S(1)}, u32[]{:S(2)}, u32[]{:S(2)}) %collective-permute-start.8) | collective-permute-done | bytes 147488 | tf_op jit(solution)/shard_map/ppermute | solution.py:147
  20.1 0.0 collective-permute-start.10
  20.1 1.4 %collective-permute-done.7.refs_3_ = bf16[6,96,128]{2,1,0:T(8,128)(2,1)S(1)} collective-permute-done((bf16[6,96,128]{2,1,0:T(8,128)(2,1)S(1)}, bf16[6,96,128]{2,1,0:T(8,128)(2,1)S(1)}, u32[]{:S(2)}, u32[]{:S(2)}) %collective-permute-start.7) | collective-permute-done | bytes 147488 | tf_op jit(solution)/shard_map/ppermute | solution.py:147
  21.5 0.0 collective-permute-start.9
  21.5 0.0 collective-permute-done.5.refs_2_
  21.5 0.0 collective-permute-done.6.refs_3_
  21.5 0.0 copy-done.2
  21.5 1.5 %shard_map.48 = (bf16[24,16,512]{2,1,0:T(8,128)(2,1)S(1)}, f32[24,16,512]{2,1,0:T(8,128)S(1)}, f32[384,512]{1,0:T(8,128)S(1)}) custom-call(bf16[6,96,128]{2,1,0:T(8,128)(2,1)S(1)} %shard_map.47.refs_0_, bf16[6,96,128]{2,1,0:T(8,128)(2,1)S(1)} %collective-permute-done.4.refs_1_, bf16[6,96,128]{2,1,0:T(8,128)(2,1)S(1)} %collective-permute-done.5.refs_2_, ...), custom_call_target="tpu_custom_call" | custom-call | flops 1500000000 | bytes 524288 | tf_op jit(solution)/shard_map/pallas_call | solution.py:207
  23.0 0.0 collective-permute-done.10.refs_6_
  23.0 0.0 collective-permute-done.9.refs_5_
  23.0 0.0 copy-done.1
  23.0 4.6 %shard_map.49 = f32[1,12288]{1,0:T(1,128)} custom-call(s32[7,24]{1,0:T(8,128)S(1)} %bitcast.6, bf16[24,16,512]{2,1,0:T(8,128)(2,1)S(1)} %get-tuple-element.17.refs_0_, f32[24,16,512]{2,1,0:T(8,128)S(1)} %get-tuple-element.18.refs_1_, f32[384,512]{1,0:T(8,128)S(1)} %get-tuple-element.19.refs_2_, bf16[6,96,128]{2,1,0:T(8,128)(2,1)S(1)} %collective-permute-done.7.refs_3_, ...), custom_call_target="tpu_custom_call" | custom-call | tf_op jit(solution)/shard_map/pallas_call | solution.py:226
  (2 shorter events, 0.0 us)
Async XLA Ops:
  0.0 9.9 %collective-permute-start.1 = (f32[96,128]{1,0:T(8,128)}, f32[96,128]{1,0:T(8,128)S(1)}, u32[]{:S(2)}, u32[]{:S(2)}) collective-permute-start(f32[96,128]{1,0:T(8,128)} %bitcast.2), channel_id=1, source_target_pairs={{4,0},{5,1},{6,2},{7,3},{0,4},{1,5},{2,6},{3,7},{12,8},{13,9},{14,... | collective-permute-start | bytes 147464 | tf_op jit(solution)/shard_map/ppermute | solution.py:147
  3.0 6.9 %collective-permute-start.2 = (f32[96,128]{1,0:T(8,128)}, f32[96,128]{1,0:T(8,128)S(1)}, u32[]{:S(2)}, u32[]{:S(2)}) collective-permute-start(f32[96,128]{1,0:T(8,128)} %bitcast.3), channel_id=1, source_target_pairs={{8,0},{9,1},{10,2},{11,3},{12,4},{13,5},{14,6},{15,7},{0,8},{1,9},... | collective-permute-start | bytes 147464 | tf_op jit(solution)/shard_map/ppermute | solution.py:147
  5.6 6.1 %collective-permute-start.3 = (f32[96,128]{1,0:T(8,128)}, f32[96,128]{1,0:T(8,128)S(1)}, u32[]{:S(2)}, u32[]{:S(2)}) collective-permute-start(f32[96,128]{1,0:T(8,128)} %bitcast.4), channel_id=1, source_target_pairs={{12,0},{13,1},{14,2},{15,3},{8,4},{9,5},{10,6},{11,7},{4,8},{5,9},... | collective-permute-start | bytes 147464 | tf_op jit(solution)/shard_map/ppermute | solution.py:147
  5.6 4.3 %collective-permute-start = (bf16[1,12288]{1,0:T(2,128)(2,1)}, bf16[1,12288]{1,0:T(2,128)(2,1)S(1)}, u32[]{:S(2)}, u32[]{:S(2)}) collective-permute-start(bf16[1,12288]{1,0:T(2,128)(2,1)} %refs_4_.1), channel_id=1, source_target_pairs={{16,0},{17,1},{18,2},{19,3},{20,4},{21,5},{22,6},{23,7},{24,8},{25... | collective-permute-start | bytes 73736 | tf_op jit(solution)/shard_map/ppermute | solution.py:147
  7.4 0.8 %copy-start = (f32[1,12288]{1,0:T(1,128)S(1)}, f32[1,12288]{1,0:T(1,128)}, u32[]{:S(2)}) copy-start(f32[1,12288]{1,0:T(1,128)} %param.4) | copy-start | bytes 147460
  8.2 13.4 %copy-start.2 = (bf16[1,12288]{1,0:T(2,128)(2,1)S(1)}, bf16[1,12288]{1,0:T(2,128)(2,1)}, u32[]{:S(2)}) copy-start(bf16[1,12288]{1,0:T(2,128)(2,1)} %refs_4_.1) | copy-start | bytes 73732
  11.7 11.3 %copy-start.1 = (s32[24,7]{0,1:T(8,128)S(1)}, s32[24,7]{0,1:T(8,128)}, u32[]{:S(2)}) copy-start(s32[24,7]{0,1:T(8,128)} %param.6) | copy-start | bytes 2020
  11.8 6.2 %collective-permute-start.4 = (bf16[6,96,128]{2,1,0:T(8,128)(2,1)S(1)}, bf16[6,96,128]{2,1,0:T(8,128)(2,1)S(1)}, u32[]{:S(2)}, u32[]{:S(2)}) collective-permute-start(bf16[6,96,128]{2,1,0:T(8,128)(2,1)S(1)} %shard_map.47.refs_0_), channel_id=1, source_target_pairs={{2,0},{3,1},{0,2},{1,3},{6,4},{7,5},{4,6},{5,7},{10,8},{11,9},{8,1... | collective-permute-start | bytes 442376 | tf_op jit(solution)/shard_map/ppermute | solution.py:147
  13.3 6.8 %collective-permute-start.8 = (bf16[6,96,128]{2,1,0:T(8,128)(2,1)S(1)}, bf16[6,96,128]{2,1,0:T(8,128)(2,1)S(1)}, u32[]{:S(2)}, u32[]{:S(2)}) collective-permute-start(bf16[6,96,128]{2,1,0:T(8,128)(2,1)S(1)} %shard_map.47.refs_0_), channel_id=1, source_target_pairs={{18,0},{19,1},{16,2},{17,3},{22,4},{23,5},{20,6},{21,7},{26,8},{27... | collective-permute-start | bytes 442376 | tf_op jit(solution)/shard_map/ppermute | solution.py:147
  14.8 6.7 %collective-permute-start.7 = (bf16[6,96,128]{2,1,0:T(8,128)(2,1)S(1)}, bf16[6,96,128]{2,1,0:T(8,128)(2,1)S(1)}, u32[]{:S(2)}, u32[]{:S(2)}) collective-permute-start(bf16[6,96,128]{2,1,0:T(8,128)(2,1)S(1)} %shard_map.47.refs_0_), channel_id=1, source_target_pairs={{16,0},{17,1},{18,2},{19,3},{20,4},{21,5},{22,6},{23,7},{24,8},{25... | collective-permute-start | bytes 442376 | tf_op jit(solution)/shard_map/ppermute | solution.py:147
  15.3 6.2 %collective-permute-start.5 = (bf16[6,96,128]{2,1,0:T(8,128)(2,1)S(1)}, bf16[6,96,128]{2,1,0:T(8,128)(2,1)S(1)}, u32[]{:S(2)}, u32[]{:S(2)}) collective-permute-start(bf16[6,96,128]{2,1,0:T(8,128)(2,1)S(1)} %shard_map.47.refs_0_), channel_id=1, source_target_pairs={{1,0},{0,1},{3,2},{2,3},{5,4},{4,5},{7,6},{6,7},{9,8},{8,9},{11,10... | collective-permute-start | bytes 442376 | tf_op jit(solution)/shard_map/ppermute | solution.py:147
  18.0 3.6 %collective-permute-start.6 = (bf16[6,96,128]{2,1,0:T(8,128)(2,1)S(1)}, bf16[6,96,128]{2,1,0:T(8,128)(2,1)S(1)}, u32[]{:S(2)}, u32[]{:S(2)}) collective-permute-start(bf16[6,96,128]{2,1,0:T(8,128)(2,1)S(1)} %collective-permute-done.4.refs_1_), channel_id=1, source_target_pairs={{1,0},{0,1},{3,2},{2,3},{5,4},{4,5},{7,6},{6,7},{9,8},{8,9},{11,10... | collective-permute-start | bytes 442376 | tf_op jit(solution)/shard_map/ppermute | solution.py:147
  20.1 2.9 %collective-permute-start.10 = (bf16[6,96,128]{2,1,0:T(8,128)(2,1)S(1)}, bf16[6,96,128]{2,1,0:T(8,128)(2,1)S(1)}, u32[]{:S(2)}, u32[]{:S(2)}) collective-permute-start(bf16[6,96,128]{2,1,0:T(8,128)(2,1)S(1)} %collective-permute-done.8.refs_4_), channel_id=1, source_target_pairs={{1,0},{0,1},{3,2},{2,3},{5,4},{4,5},{7,6},{6,7},{9,8},{8,9},{11,10... | collective-permute-start | bytes 442376 | tf_op jit(solution)/shard_map/ppermute | solution.py:147
  21.5 1.5 %collective-permute-start.9 = (bf16[6,96,128]{2,1,0:T(8,128)(2,1)S(1)}, bf16[6,96,128]{2,1,0:T(8,128)(2,1)S(1)}, u32[]{:S(2)}, u32[]{:S(2)}) collective-permute-start(bf16[6,96,128]{2,1,0:T(8,128)(2,1)S(1)} %collective-permute-done.7.refs_3_), channel_id=1, source_target_pairs={{1,0},{0,1},{3,2},{2,3},{5,4},{4,5},{7,6},{6,7},{9,8},{8,9},{11,10... | collective-permute-start | bytes 442376 | tf_op jit(solution)/shard_map/ppermute | solution.py:147

commit v8 on v6

--- a/solution.py
+++ b/solution.py
@@ -9,7 +9,7 @@
 
 LANES = 128
 SUB = 8
-VMEM_LIMIT = 51 * 1024 * 1024
+VMEM_LIMIT = 16 * 1024 * 1024
 PACK_COST = 20_000_000_000
 
 
@@ -38,18 +38,14 @@
 
 def product_kernel(group, off_ref, *refs):
     groups = refs[:8]
-    inc_own, inc_other, taper_hbm, out_ref = refs[8:12]
-    tiles, pert, picked_from, acc, sems = refs[12:]
+    inc_own, inc_other, tiles, out_ref = refs[8:12]
+    pert, picked_from, acc = refs[12:]
     slots, block_size, _ = tiles.shape
     members = 4 * group
     rows = groups[0].shape[1]
     pitch = pert.shape[0] // members
     quarters = block_size // LANES
     block_count = rows // quarters
-    copies = []
-    for s in range(slots):
-        copies.append(pltpu.make_async_copy(taper_hbm.at[s], tiles.at[s], sems.at[s]))
-        copies[-1].start()
 
     def weigh(side, inc_ref):
         lines = [groups[4 * c + 2 * side + j] for c in range(2) for j in range(2)]
@@ -87,7 +83,6 @@
 
     contract = (((1,), (1,)), ((), ()))
     vectors = block_count * members
-    copies[0].wait()
     acc[...] = lax.dot_general(
         picked_from[0:block_count].reshape(vectors, block_size),
         tiles[0],
@@ -100,7 +95,6 @@
             place = i + off_ref[s - 1, i]
             place = jnp.where(place < 0, place + 2 * block_count, place)
             chosen.append(picked_from[place])
-        copies[s].wait()
         acc[...] += lax.dot_general(
             jnp.concatenate(chosen, axis=0),
             tiles[s],
@@ -152,9 +146,11 @@
     same, beside = (lambda m: m), (lambda m: m ^ 2)
 
     base = ensemble.reshape(rows, LANES)
-    line = [
-        move(base, False, lambda m: (m + 4 * d) % mem_size) for d in reversed(range(1, group))
-    ]
+    if group & (group - 1):
+        turn = lambda d: lambda m: (m + 4 * d) % mem_size
+    else:
+        turn = lambda d: lambda m: m ^ (4 * d)
+    line = [move(base, False, turn(d)) for d in range(1, group)]
     inc_other = move(increments.reshape(1, columns), True, same)
     whole = pl.BlockSpec(memory_space=pltpu.VMEM)
     small = pltpu.CompilerParams(vmem_limit_bytes=4 * 1024 * 1024)
@@ -189,16 +185,12 @@
     return pl.pallas_call(
         functools.partial(product_kernel, group),
         out_shape=jax.ShapeDtypeStruct((1, columns), jnp.float32),
-        in_specs=[pl.BlockSpec(memory_space=pltpu.SMEM)]
-        + [whole] * 10
-        + [pl.BlockSpec(memory_space=pltpu.HBM)],
+        in_specs=[pl.BlockSpec(memory_space=pltpu.SMEM)] + [whole] * 11,
         out_specs=whole,
         scratch_shapes=[
-            pltpu.VMEM((slots, block_size, block_size), jnp.bfloat16),
             pltpu.VMEM((mem_size * (rows + 1), LANES), jnp.float32),
             pltpu.VMEM((2 * block_count, mem_size, block_size), jnp.bfloat16),
             pltpu.VMEM((vectors, block_size), jnp.float32),
-            pltpu.SemaphoreType.DMA((slots,)),
         ],
         compiler_params=pltpu.CompilerParams(vmem_limit_bytes=VMEM_LIMIT),
     )(offsets.T, *groups, increments, inc_other, taper)

time: 26.2 us -> 24.4 us (0.931)
  Pallas kernels: 4.82 us -> 3.58 us
  starting transfers between devices: 11.7 us -> 11.4 us
  waiting for transfers between devices: 8.7 us -> 8.43 us
    pallas_call x1, Pallas kernels: 4.79 us -> 3.54 us  [on_device(): pl.pallas_call(functools.partial(product_kernel, group), out_shape=jax.Sh...]
    ppermute x11, starting transfers between devices: 11.7 us -> 11.4 us  [one(): return lax.ppermute(x, ('lon', 'mem'), perm)]
    ppermute x11, waiting for transfers between devices: 8.7 us -> 8.43 us  [one(): return lax.ppermute(x, ('lon', 'mem'), perm)]
    unnamed x6 -> x8, local copies, waits for them, and re-layouts: 0.81 us -> 0.82 us
where the time goes in v8:
time: 24.4 us; the launch traced here: 24.2 us
  starting transfers between devices  11.4 us (47%)
  waiting for transfers between devices  8.43 us (35%)
  Pallas kernels  3.58 us (15%)
  local copies, waits for them, and re-layouts  0.82 us (3%)
    ppermute x11, starting transfers between devices, one(): return lax.ppermute(x, ('lon', 'mem'), perm)  11.4 us
    ppermute x11, waiting for transfers between devices, one(): return lax.ppermute(x, ('lon', 'mem'), perm)  8.43 us
    pallas_call x1, Pallas kernels, on_device(): pl.pallas_call(functools.partial(product_kernel, group), out_shape=jax.Sh...  3.54 us
    unnamed x8, local copies, waits for them, and re-layouts  0.82 us
  transfers between devices with their start and end apart: 11, of which 7 were waited for; matrix products, arithmetic and copies ran while one was open for 0% of the time, Pallas kernels for 0%

profile of v8, /device:TPU:0, one launch (start us, length us, event | category | flops | bytes accessed | tf_op | source)
XLA Modules:
  0.0 24.2 jit_solution(12072973598163638707)
XLA Ops:
  0.0 5.0 %collective-permute-start.3 = (f32[96,128]{1,0:T(8,128)}, f32[96,128]{1,0:T(8,128)S(1)}, u32[]{:S(2)}, u32[]{:S(2)}) collective-permute-start(f32[96,128]{1,0:T(8,128)} %bitcast.2), channel_id=1, source_target_pairs={{12,0},{13,1},{14,2},{15,3},{8,4},{9,5},{10,6},{11,7},{4,8},{5,9},... | collective-permute-start | bytes 147464 | tf_op jit(solution)/shard_map/ppermute | solution.py:124
  5.0 0.0 collective-permute-start.2
  5.1 0.6 %collective-permute-start.1 = (f32[96,128]{1,0:T(8,128)}, f32[96,128]{1,0:T(8,128)S(1)}, u32[]{:S(2)}, u32[]{:S(2)}) collective-permute-start(f32[96,128]{1,0:T(8,128)} %bitcast.4), channel_id=1, source_target_pairs={{4,0},{5,1},{6,2},{7,3},{0,4},{1,5},{2,6},{3,7},{12,8},{13,9},{14,... | collective-permute-start | bytes 147464 | tf_op jit(solution)/shard_map/ppermute | solution.py:124
  5.6 1.7 %collective-permute-start = (bf16[1,12288]{1,0:T(2,128)(2,1)}, bf16[1,12288]{1,0:T(2,128)(2,1)S(1)}, u32[]{:S(2)}, u32[]{:S(2)}) collective-permute-start(bf16[1,12288]{1,0:T(2,128)(2,1)} %refs_8_.1), channel_id=1, source_target_pairs={{16,0},{17,1},{18,2},{19,3},{20,4},{21,5},{22,6},{23,7},{24,8},{25... | collective-permute-start | bytes 73736 | tf_op jit(solution)/shard_map/ppermute | solution.py:124
  7.4 0.0 copy-start.2
  7.4 0.8 %copy-done.2 = f32[1,12288]{1,0:T(1,128)S(1)} copy-done((f32[1,12288]{1,0:T(1,128)S(1)}, f32[1,12288]{1,0:T(1,128)}, u32[]{:S(2)}) %copy-start.2) | copy-done | bytes 49176
  8.2 0.0 copy-start
  8.2 0.0 copy-start.1
  8.2 0.0 copy-start.3
  8.2 1.7 %collective-permute-done.refs_9_ = bf16[1,12288]{1,0:T(2,128)(2,1)S(1)} collective-permute-done((bf16[1,12288]{1,0:T(2,128)(2,1)}, bf16[1,12288]{1,0:T(2,128)(2,1)S(1)}, u32[]{:S(2)}, u32[]{:S(2)}) %collective-permute-start) | collective-permute-done | bytes 24608 | tf_op jit(solution)/shard_map/ppermute | solution.py:124
  9.9 0.0 collective-permute-done.3.refs_2_
  9.9 0.3 %collective-permute-done.2.refs_1_ = f32[96,128]{1,0:T(8,128)S(1)} collective-permute-done((f32[96,128]{1,0:T(8,128)}, f32[96,128]{1,0:T(8,128)S(1)}, u32[]{:S(2)}, u32[]{:S(2)}) %collective-permute-start.2) | collective-permute-done | bytes 49184 | tf_op jit(solution)/shard_map/ppermute | solution.py:124
  10.2 0.0 collective-permute-done.1.refs_0_
  10.3 2.5 %collective-permute-start.6 = (bf16[6,96,128]{2,1,0:T(8,128)(2,1)S(1)}, bf16[6,96,128]{2,1,0:T(8,128)(2,1)S(1)}, u32[]{:S(2)}, u32[]{:S(2)}) collective-permute-start(bf16[6,96,128]{2,1,0:T(8,128)(2,1)S(1)} %shard_map.47.refs_0_), channel_id=1, source_target_pairs={{18,0},{19,1},{16,2},{17,3},{22,4},{23,5},{20,6},{21,7},{26,8},{27... | collective-permute-start | bytes 442376 | tf_op jit(solution)/shard_map/ppermute | solution.py:124
  12.8 0.5 %collective-permute-start.5 = (bf16[6,96,128]{2,1,0:T(8,128)(2,1)S(1)}, bf16[6,96,128]{2,1,0:T(8,128)(2,1)S(1)}, u32[]{:S(2)}, u32[]{:S(2)}) collective-permute-start(bf16[6,96,128]{2,1,0:T(8,128)(2,1)S(1)} %shard_map.47.refs_0_), channel_id=1, source_target_pairs={{16,0},{17,1},{18,2},{19,3},{20,4},{21,5},{22,6},{23,7},{24,8},{25... | collective-permute-start | bytes 442376 | tf_op jit(solution)/shard_map/ppermute | solution.py:124
  13.3 0.5 %collective-permute-start.4 = (bf16[6,96,128]{2,1,0:T(8,128)(2,1)S(1)}, bf16[6,96,128]{2,1,0:T(8,128)(2,1)S(1)}, u32[]{:S(2)}, u32[]{:S(2)}) collective-permute-start(bf16[6,96,128]{2,1,0:T(8,128)(2,1)S(1)} %shard_map.47.refs_0_), channel_id=1, source_target_pairs={{2,0},{3,1},{0,2},{1,3},{6,4},{7,5},{4,6},{5,7},{10,8},{11,9},{8,1... | collective-permute-start | bytes 442376 | tf_op jit(solution)/shard_map/ppermute | solution.py:124
  13.8 0.0 collective-permute-start.7
  13.8 3.8 %collective-permute-done.6.refs_3_ = bf16[6,96,128]{2,1,0:T(8,128)(2,1)S(1)} collective-permute-done((bf16[6,96,128]{2,1,0:T(8,128)(2,1)S(1)}, bf16[6,96,128]{2,1,0:T(8,128)(2,1)S(1)}, u32[]{:S(2)}, u32[]{:S(2)}) %collective-permute-start.6) | collective-permute-done | bytes 147488 | tf_op jit(solution)/shard_map/ppermute | solution.py:124
  17.6 0.0 collective-permute-start.10
  17.6 1.5 %collective-permute-done.5.refs_2_ = bf16[6,96,128]{2,1,0:T(8,128)(2,1)S(1)} collective-permute-done((bf16[6,96,128]{2,1,0:T(8,128)(2,1)S(1)}, bf16[6,96,128]{2,1,0:T(8,128)(2,1)S(1)}, u32[]{:S(2)}, u32[]{:S(2)}) %collective-permute-start.5) | collective-permute-done | bytes 147488 | tf_op jit(solution)/shard_map/ppermute | solution.py:124
  19.1 0.0 collective-permute-start.9
  19.1 0.1 collective-permute-done.4.refs_1_
  19.2 0.5 %collective-permute-start.8 = (bf16[6,96,128]{2,1,0:T(8,128)(2,1)S(1)}, bf16[6,96,128]{2,1,0:T(8,128)(2,1)S(1)}, u32[]{:S(2)}, u32[]{:S(2)}) collective-permute-start(bf16[6,96,128]{2,1,0:T(8,128)(2,1)S(1)} %collective-permute-done.4.refs_1_), channel_id=1, source_target_pairs={{1,0},{0,1},{3,2},{2,3},{5,4},{4,5},{7,6},{6,7},{9,8},{8,9},{11,10... | collective-permute-start | bytes 442376 | tf_op jit(solution)/shard_map/ppermute | solution.py:124
  19.6 0.0 collective-permute-done.7.refs_4_
  19.6 0.0 collective-permute-done.10.refs_7_
  19.6 0.9 %collective-permute-done.9.refs_6_ = bf16[6,96,128]{2,1,0:T(8,128)(2,1)S(1)} collective-permute-done((bf16[6,96,128]{2,1,0:T(8,128)(2,1)S(1)}, bf16[6,96,128]{2,1,0:T(8,128)(2,1)S(1)}, u32[]{:S(2)}, u32[]{:S(2)}) %collective-permute-start.9) | collective-permute-done | bytes 147488 | tf_op jit(solution)/shard_map/ppermute | solution.py:124
  20.5 0.2 collective-permute-done.8.refs_5_
  20.7 0.0 copy-done
  20.7 0.0 copy-done.1
  20.7 0.0 copy-done.3
  20.7 3.5 %shard_map.48 = f32[1,12288]{1,0:T(1,128)} custom-call(s32[7,24]{1,0:T(8,128)S(1)} %bitcast.6, bf16[6,96,128]{2,1,0:T(8,128)(2,1)S(1)} %shard_map.47.refs_0_, bf16[6,96,128]{2,1,0:T(8,128)(2,1)S(1)} %collective-permute-done.4.refs_1_, bf16[6,96,128]{2,1,0:T(8,128)(2,1)S(1)} %collective-permute-done.5.refs_2_, ...), custom_call_target="tpu_custom_call" | custom-call | tf_op jit(solution)/shard_map/pallas_call | solution.py:185
  (2 shorter events, 0.0 us)
Async XLA Ops:
  0.0 9.9 %collective-permute-start.3 = (f32[96,128]{1,0:T(8,128)}, f32[96,128]{1,0:T(8,128)S(1)}, u32[]{:S(2)}, u32[]{:S(2)}) collective-permute-start(f32[96,128]{1,0:T(8,128)} %bitcast.2), channel_id=1, source_target_pairs={{12,0},{13,1},{14,2},{15,3},{8,4},{9,5},{10,6},{11,7},{4,8},{5,9},... | collective-permute-start | bytes 147464 | tf_op jit(solution)/shard_map/ppermute | solution.py:124
  5.0 5.2 %collective-permute-start.2 = (f32[96,128]{1,0:T(8,128)}, f32[96,128]{1,0:T(8,128)S(1)}, u32[]{:S(2)}, u32[]{:S(2)}) collective-permute-start(f32[96,128]{1,0:T(8,128)} %bitcast.3), channel_id=1, source_target_pairs={{8,0},{9,1},{10,2},{11,3},{12,4},{13,5},{14,6},{15,7},{0,8},{1,9},... | collective-permute-start | bytes 147464 | tf_op jit(solution)/shard_map/ppermute | solution.py:124
  5.1 5.2 %collective-permute-start.1 = (f32[96,128]{1,0:T(8,128)}, f32[96,128]{1,0:T(8,128)S(1)}, u32[]{:S(2)}, u32[]{:S(2)}) collective-permute-start(f32[96,128]{1,0:T(8,128)} %bitcast.4), channel_id=1, source_target_pairs={{4,0},{5,1},{6,2},{7,3},{0,4},{1,5},{2,6},{3,7},{12,8},{13,9},{14,... | collective-permute-start | bytes 147464 | tf_op jit(solution)/shard_map/ppermute | solution.py:124
  5.6 4.3 %collective-permute-start = (bf16[1,12288]{1,0:T(2,128)(2,1)}, bf16[1,12288]{1,0:T(2,128)(2,1)S(1)}, u32[]{:S(2)}, u32[]{:S(2)}) collective-permute-start(bf16[1,12288]{1,0:T(2,128)(2,1)} %refs_8_.1), channel_id=1, source_target_pairs={{16,0},{17,1},{18,2},{19,3},{20,4},{21,5},{22,6},{23,7},{24,8},{25... | collective-permute-start | bytes 73736 | tf_op jit(solution)/shard_map/ppermute | solution.py:124
  7.4 0.8 %copy-start.2 = (f32[1,12288]{1,0:T(1,128)S(1)}, f32[1,12288]{1,0:T(1,128)}, u32[]{:S(2)}) copy-start(f32[1,12288]{1,0:T(1,128)} %param.4) | copy-start | bytes 147460
  8.2 12.5 %copy-start = (bf16[8,512,512]{2,1,0:T(8,128)(2,1)S(1)}, bf16[8,512,512]{2,1,0:T(8,128)(2,1)}, u32[]{:S(2)}) copy-start(bf16[8,512,512]{2,1,0:T(8,128)(2,1)} %refs_10_.1) | copy-start | bytes 12582916
  8.2 12.5 %copy-start.1 = (bf16[1,12288]{1,0:T(2,128)(2,1)S(1)}, bf16[1,12288]{1,0:T(2,128)(2,1)}, u32[]{:S(2)}) copy-start(bf16[1,12288]{1,0:T(2,128)(2,1)} %refs_8_.1) | copy-start | bytes 73732
  8.2 12.5 %copy-start.3 = (s32[24,7]{0,1:T(8,128)S(1)}, s32[24,7]{0,1:T(8,128)}, u32[]{:S(2)}) copy-start(s32[24,7]{0,1:T(8,128)} %param.6) | copy-start | bytes 2020
  10.3 7.3 %collective-permute-start.6 = (bf16[6,96,128]{2,1,0:T(8,128)(2,1)S(1)}, bf16[6,96,128]{2,1,0:T(8,128)(2,1)S(1)}, u32[]{:S(2)}, u32[]{:S(2)}) collective-permute-start(bf16[6,96,128]{2,1,0:T(8,128)(2,1)S(1)} %shard_map.47.refs_0_), channel_id=1, source_target_pairs={{18,0},{19,1},{16,2},{17,3},{22,4},{23,5},{20,6},{21,7},{26,8},{27... | collective-permute-start | bytes 442376 | tf_op jit(solution)/shard_map/ppermute | solution.py:124
  12.8 6.3 %collective-permute-start.5 = (bf16[6,96,128]{2,1,0:T(8,128)(2,1)S(1)}, bf16[6,96,128]{2,1,0:T(8,128)(2,1)S(1)}, u32[]{:S(2)}, u32[]{:S(2)}) collective-permute-start(bf16[6,96,128]{2,1,0:T(8,128)(2,1)S(1)} %shard_map.47.refs_0_), channel_id=1, source_target_pairs={{16,0},{17,1},{18,2},{19,3},{20,4},{21,5},{22,6},{23,7},{24,8},{25... | collective-permute-start | bytes 442376 | tf_op jit(solution)/shard_map/ppermute | solution.py:124
  13.3 5.9 %collective-permute-start.4 = (bf16[6,96,128]{2,1,0:T(8,128)(2,1)S(1)}, bf16[6,96,128]{2,1,0:T(8,128)(2,1)S(1)}, u32[]{:S(2)}, u32[]{:S(2)}) collective-permute-start(bf16[6,96,128]{2,1,0:T(8,128)(2,1)S(1)} %shard_map.47.refs_0_), channel_id=1, source_target_pairs={{2,0},{3,1},{0,2},{1,3},{6,4},{7,5},{4,6},{5,7},{10,8},{11,9},{8,1... | collective-permute-start | bytes 442376 | tf_op jit(solution)/shard_map/ppermute | solution.py:124
  13.8 5.8 %collective-permute-start.7 = (bf16[6,96,128]{2,1,0:T(8,128)(2,1)S(1)}, bf16[6,96,128]{2,1,0:T(8,128)(2,1)S(1)}, u32[]{:S(2)}, u32[]{:S(2)}) collective-permute-start(bf16[6,96,128]{2,1,0:T(8,128)(2,1)S(1)} %shard_map.47.refs_0_), channel_id=1, source_target_pairs={{1,0},{0,1},{3,2},{2,3},{5,4},{4,5},{7,6},{6,7},{9,8},{8,9},{11,10... | collective-permute-start | bytes 442376 | tf_op jit(solution)/shard_map/ppermute | solution.py:124
  17.6 2.0 %collective-permute-start.10 = (bf16[6,96,128]{2,1,0:T(8,128)(2,1)S(1)}, bf16[6,96,128]{2,1,0:T(8,128)(2,1)S(1)}, u32[]{:S(2)}, u32[]{:S(2)}) collective-permute-start(bf16[6,96,128]{2,1,0:T(8,128)(2,1)S(1)} %collective-permute-done.6.refs_3_), channel_id=1, source_target_pairs={{1,0},{0,1},{3,2},{2,3},{5,4},{4,5},{7,6},{6,7},{9,8},{8,9},{11,10... | collective-permute-start | bytes 442376 | tf_op jit(solution)/shard_map/ppermute | solution.py:124
  19.1 1.4 %collective-permute-start.9 = (bf16[6,96,128]{2,1,0:T(8,128)(2,1)S(1)}, bf16[6,96,128]{2,1,0:T(8,128)(2,1)S(1)}, u32[]{:S(2)}, u32[]{:S(2)}) collective-permute-start(bf16[6,96,128]{2,1,0:T(8,128)(2,1)S(1)} %collective-permute-done.5.refs_2_), channel_id=1, source_target_pairs={{1,0},{0,1},{3,2},{2,3},{5,4},{4,5},{7,6},{6,7},{9,8},{8,9},{11,10... | collective-permute-start | bytes 442376 | tf_op jit(solution)/shard_map/ppermute | solution.py:124
  19.2 1.5 %collective-permute-start.8 = (bf16[6,96,128]{2,1,0:T(8,128)(2,1)S(1)}, bf16[6,96,128]{2,1,0:T(8,128)(2,1)S(1)}, u32[]{:S(2)}, u32[]{:S(2)}) collective-permute-start(bf16[6,96,128]{2,1,0:T(8,128)(2,1)S(1)} %collective-permute-done.4.refs_1_), channel_id=1, source_target_pairs={{1,0},{0,1},{3,2},{2,3},{5,4},{4,5},{7,6},{6,7},{9,8},{8,9},{11,10... | collective-permute-start | bytes 442376 | tf_op jit(solution)/shard_map/ppermute | solution.py:124

commit v9 on v8

--- a/solution.py
+++ b/solution.py
@@ -13,51 +13,61 @@
 PACK_COST = 20_000_000_000
 
 
-def split_kernel(base_ref, split_ref):
-    base = base_ref[...]
+def pair_kernel(base_ref, inc_ref, pair_ref):
+    pair_ref[0] = base_ref[...]
+    for r in range(base_ref.shape[0]):
+        part = inc_ref[:, r * LANES : (r + 1) * LANES]
+        pair_ref[1, r : r + 1, :] = part.astype(jnp.float32)
+
+
+def pack_kernel(pair_ref, *refs):
+    line, (diff_ref, mine_ref) = refs[:-2], refs[-2:]
+    base = pair_ref[0]
     high = base.astype(jnp.bfloat16)
     rest = base - high.astype(jnp.float32)
     middle = rest.astype(jnp.bfloat16)
-    split_ref[0] = high
-    split_ref[1] = middle
-    split_ref[2] = (rest - middle.astype(jnp.float32)).astype(jnp.bfloat16)
-
-
-def joined(parts):
-    high, middle, low = (part.astype(jnp.float32) for part in parts)
-    return high + middle + low
-
-
-def pack_kernel(split_ref, *refs):
-    line, out_ref = refs[:-1], refs[-1]
-    base = joined([split_ref[i] for i in range(3)])
-    out_ref[0:3] = split_ref[...]
+    mine_ref[0] = high
+    mine_ref[1] = middle
+    mine_ref[2] = (rest - middle.astype(jnp.float32)).astype(jnp.bfloat16)
     for j, ref in enumerate(line):
-        out_ref[3 + j] = (ref[...] - base).astype(jnp.bfloat16)
+        step = (ref[...] - base).astype(jnp.bfloat16)
+        diff_ref[j] = step
+        mine_ref[3 + j] = step
 
 
 def product_kernel(group, off_ref, *refs):
-    groups = refs[:8]
-    inc_own, inc_other, tiles, out_ref = refs[8:12]
-    pert, picked_from, acc = refs[12:]
+    half = len(refs[:14]) // 2
+    cores = refs[:half], refs[half : 2 * half]
+    inc_own, inc_other = refs[14], refs[3]
+    tiles, out_ref = refs[15:17]
+    pert, picked_from, acc = refs[17:]
     slots, block_size, _ = tiles.shape
     members = 4 * group
-    rows = groups[0].shape[1]
+    rows = inc_other.shape[1]
     pitch = pert.shape[0] // members
     quarters = block_size // LANES
     block_count = rows // quarters
 
-    def weigh(side, inc_ref):
-        lines = [groups[4 * c + 2 * side + j] for c in range(2) for j in range(2)]
+    def weigh(side, increment):
+        if side == 0:
+            lines = [pair for core in cores for pair in ((None, core[0]), core[1:3])]
+        else:
+            lines = [pair for core in cores for pair in (core[3:5], core[5:7])]
 
         def chunk(r, carry):
             at = pl.multiple_of(r * 2 * SUB, 2 * SUB)
             here = pl.ds(at, 2 * SUB)
-            starts = [joined([ref[k, here, :] for k in range(3)]) for ref in lines]
-            steps = [
-                [ref[3 + k, here, :].astype(jnp.float32) for k in range(group - 1)]
-                for ref in lines
-            ]
+            starts, steps = [], []
+            for base, ref in lines:
+                if base is None:
+                    high, middle, low = (ref[k, here, :].astype(jnp.float32) for k in range(3))
+                    starts.append(high + middle + low)
+                else:
+                    starts.append(base[0, here, :])
+                first = ref.shape[0] - (group - 1)
+                steps.append(
+                    [ref[first + k, here, :].astype(jnp.float32) for k in range(group - 1)]
+                )
             total = sum(step for line in steps for step in line) + group * sum(starts)
             mean = total * (1.0 / members)
             m = 0
@@ -74,12 +84,11 @@
             for q in range(quarters):
                 lanes = slice(q * LANES, (q + 1) * LANES)
                 at = i * quarters + q
-                inc = inc_ref[:, at * LANES : (at + 1) * LANES].astype(jnp.float32)
-                part = pert[pl.ds(at, members, pitch), :] * inc
+                part = pert[pl.ds(at, members, pitch), :] * increment(at)
                 picked_from[side * block_count + i, :, lanes] = part.astype(jnp.bfloat16)
 
-    weigh(1, inc_other)
-    weigh(0, inc_own)
+    weigh(1, lambda at: inc_other[1, at : at + 1, :])
+    weigh(0, lambda at: inc_own[1, at : at + 1, :])
 
     contract = (((1,), (1,)), ((), ()))
     vectors = block_count * members
@@ -151,41 +160,44 @@
     else:
         turn = lambda d: lambda m: m ^ (4 * d)
     line = [move(base, False, turn(d)) for d in range(1, group)]
-    inc_other = move(increments.reshape(1, columns), True, same)
     whole = pl.BlockSpec(memory_space=pltpu.VMEM)
     small = pltpu.CompilerParams(vmem_limit_bytes=4 * 1024 * 1024)
-    split = pl.pallas_call(
-        split_kernel,
-        out_shape=jax.ShapeDtypeStruct((3, rows, LANES), jnp.bfloat16),
-        in_specs=[whole],
+    pair = pl.pallas_call(
+        pair_kernel,
+        out_shape=jax.ShapeDtypeStruct((2, rows, LANES), jnp.float32),
+        in_specs=[whole] * 2,
         out_specs=whole,
         compiler_params=small,
-    )(base)
-    split, inc_other, line = lax.optimization_barrier((split, inc_other, line))
-
-    mine = pl.pallas_call(
+    )(base, increments)
+    base_x = move(base[None], False, beside)
+    base_diag = move(base[None], True, beside)
+    base_y = move(pair, True, same)
+    pair, line = lax.optimization_barrier((pair, line))
+
+    diff, mine = pl.pallas_call(
         pack_kernel,
-        out_shape=jax.ShapeDtypeStruct((group + 2, rows, LANES), jnp.bfloat16),
+        out_shape=(
+            jax.ShapeDtypeStruct((group - 1, rows, LANES), jnp.bfloat16),
+            jax.ShapeDtypeStruct((group + 2, rows, LANES), jnp.bfloat16),
+        ),
         in_specs=[whole] * group,
-        out_specs=whole,
+        out_specs=(whole, whole),
         compiler_params=small,
         cost_estimate=pl.CostEstimate(
             flops=PACK_COST, bytes_accessed=8 * columns * 4, transcendentals=0
         ),
-    )(split, *line)
-    groups = [
-        mine,
-        move(mine, False, beside),
-        move(mine, True, same),
-        move(mine, True, beside),
-    ]
-    groups += [move(x, False, lambda m: m ^ 1) for x in groups]
+    )(pair, *line)
+    x, y = move(diff, False, beside), move(diff, True, same)
+    diag = move(diff, True, beside)
+    mine, base_x, base_y, base_diag = lax.optimization_barrier((mine, base_x, base_y, base_diag))
+    lines = [mine, base_x, x, base_y, y, base_diag, diag]
+    lines += [move(v, False, lambda m: m ^ 1) for v in lines]
 
     vectors = mem_size * block_count
     return pl.pallas_call(
         functools.partial(product_kernel, group),
         out_shape=jax.ShapeDtypeStruct((1, columns), jnp.float32),
-        in_specs=[pl.BlockSpec(memory_space=pltpu.SMEM)] + [whole] * 11,
+        in_specs=[pl.BlockSpec(memory_space=pltpu.SMEM)] + [whole] * 16,
         out_specs=whole,
         scratch_shapes=[
             pltpu.VMEM((mem_size * (rows + 1), LANES), jnp.float32),
@@ -193,7 +205,7 @@
             pltpu.VMEM((vectors, block_size), jnp.float32),
         ],
         compiler_params=pltpu.CompilerParams(vmem_limit_bytes=VMEM_LIMIT),
-    )(offsets.T, *groups, increments, inc_other, taper)
+    )(offsets.T, *lines, pair, taper)
 
 
 def solution(mesh):

time: 24.4 us -> 24 us (0.984)
  waiting for transfers between devices: 8.43 us -> 4.73 us
  starting transfers between devices: 11.4 us -> 13.8 us
  local copies, waits for them, and re-layouts: 0.82 us -> 1.61 us
    ppermute x11 -> x16, waiting for transfers between devices: 8.43 us -> 4.73 us  [one(): return lax.ppermute(x, ('lon', 'mem'), perm)]
    ppermute x11 -> x16, starting transfers between devices: 11.4 us -> 13.8 us  [one(): return lax.ppermute(x, ('lon', 'mem'), perm)]
    unnamed x8, local copies, waits for them, and re-layouts: 0.82 us -> 1.61 us
  transfers between devices with their start and end apart: 11 -> 16, of which waited for: 7 -> 7; matrix products, arithmetic and copies ran while one was open for 0% -> 0% of each run, Pallas kernels for 0% -> 0%
where the time goes in v9:
time: 24 us; the launch traced here: 23.8 us
  starting transfers between devices  13.8 us (58%)
  waiting for transfers between devices  4.73 us (20%)
  Pallas kernels  3.55 us (15%)
  local copies, waits for them, and re-layouts  1.61 us (7%)
    ppermute x16, starting transfers between devices, one(): return lax.ppermute(x, ('lon', 'mem'), perm)  13.8 us
    ppermute x16, waiting for transfers between devices, one(): return lax.ppermute(x, ('lon', 'mem'), perm)  4.73 us
    pallas_call x1, Pallas kernels, on_device(): pl.pallas_call(functools.partial(product_kernel, group), out_shape=jax.Sh...  3.49 us
    unnamed x8, local copies, waits for them, and re-layouts  1.61 us
  transfers between devices with their start and end apart: 16, of which 7 were waited for; matrix products, arithmetic and copies ran while one was open for 0% of the time, Pallas kernels for 0%

profile of v9, /device:TPU:0, one launch (start us, length us, event | category | flops | bytes accessed | tf_op | source)
XLA Modules:
  0.0 23.8 jit_solution(12411651720022291636)
XLA Ops:
  0.0 5.0 %collective-permute-start.2 = (f32[96,128]{1,0:T(8,128)}, f32[96,128]{1,0:T(8,128)S(1)}, u32[]{:S(2)}, u32[]{:S(2)}) collective-permute-start(f32[96,128]{1,0:T(8,128)} %bitcast.3), channel_id=1, source_target_pairs={{12,0},{13,1},{14,2},{15,3},{8,4},{9,5},{10,6},{11,7},{4,8},{5,9},... | collective-permute-start | bytes 147464 | tf_op jit(solution)/shard_map/ppermute | solution.py:133
  5.0 0.0 collective-permute-start.1
  5.1 0.6 %collective-permute-start = (f32[96,128]{1,0:T(8,128)}, f32[96,128]{1,0:T(8,128)S(1)}, u32[]{:S(2)}, u32[]{:S(2)}) collective-permute-start(f32[96,128]{1,0:T(8,128)} %bitcast.5), channel_id=1, source_target_pairs={{4,0},{5,1},{6,2},{7,3},{0,4},{1,5},{2,6},{3,7},{12,8},{13,9},{14,... | collective-permute-start | bytes 147464 | tf_op jit(solution)/shard_map/ppermute | solution.py:133
  5.6 2.7 %collective-permute-start.5 = (f32[1,96,128]{2,1,0:T(8,128)}, f32[1,96,128]{2,1,0:T(8,128)S(1)}, u32[]{:S(2)}, u32[]{:S(2)}) collective-permute-start(f32[1,96,128]{2,1,0:T(8,128)} %bitcast.6), channel_id=1, source_target_pairs={{18,0},{19,1},{16,2},{17,3},{22,4},{23,5},{20,6},{21,7},{26,8},{27... | collective-permute-start | bytes 147464 | tf_op jit(solution)/shard_map/ppermute | solution.py:133
  8.3 0.5 %collective-permute-start.3 = (f32[1,96,128]{2,1,0:T(8,128)}, f32[1,96,128]{2,1,0:T(8,128)S(1)}, u32[]{:S(2)}, u32[]{:S(2)}) collective-permute-start(f32[1,96,128]{2,1,0:T(8,128)} %bitcast.7), channel_id=1, source_target_pairs={{2,0},{3,1},{0,2},{1,3},{6,4},{7,5},{4,6},{5,7},{10,8},{11,9},{8,1... | collective-permute-start | bytes 147464 | tf_op jit(solution)/shard_map/ppermute | solution.py:133
  8.8 0.0 copy-start.1
  8.8 0.8 %copy-done.1 = bf16[1,12288]{1,0:T(2,128)(2,1)S(1)} copy-done((bf16[1,12288]{1,0:T(2,128)(2,1)S(1)}, bf16[1,12288]{1,0:T(2,128)(2,1)}, u32[]{:S(2)}) %copy-start.1) | copy-done | bytes 24600
  9.6 0.0 copy-start.2
  9.6 0.8 %copy-done.2 = f32[1,12288]{1,0:T(1,128)S(1)} copy-done((f32[1,12288]{1,0:T(1,128)S(1)}, f32[1,12288]{1,0:T(1,128)}, u32[]{:S(2)}) %copy-start.2) | copy-done | bytes 49176
  10.5 0.0 copy-start
  10.5 0.0 copy-start.3
  10.5 0.0 collective-permute-done.2.refs_2_
  10.5 0.4 %collective-permute-start.4 = (f32[2,96,128]{2,1,0:T(8,128)S(1)}, f32[2,96,128]{2,1,0:T(8,128)S(1)}, u32[]{:S(2)}, u32[]{:S(2)}) collective-permute-start(f32[2,96,128]{2,1,0:T(8,128)S(1)} %shard_map.46.pair_ref.refs_14_), channel_id=1, source_target_pairs={{16,0},{17,1},{18,2},{19,3},{20,4},{21,5},{22,6},{23,7},{24,8},{25... | collective-permute-start | bytes 294920 | tf_op jit(solution)/shard_map/ppermute | solution.py:133
  10.8 0.0 collective-permute-done.1.refs_1_
  10.8 0.0 collective-permute-done.refs_0_
  10.9 2.7 %collective-permute-start.8 = (bf16[3,96,128]{2,1,0:T(8,128)(2,1)S(1)}, bf16[3,96,128]{2,1,0:T(8,128)(2,1)S(1)}, u32[]{:S(2)}, u32[]{:S(2)}) collective-permute-start(bf16[3,96,128]{2,1,0:T(8,128)(2,1)S(1)} %get-tuple-element.22), channel_id=1, source_target_pairs={{18,0},{19,1},{16,2},{17,3},{22,4},{23,5},{20,6},{21,7},{26,8},{27... | collective-permute-start | bytes 221192 | tf_op jit(solution)/shard_map/ppermute | solution.py:133
  13.6 0.5 %collective-permute-start.7 = (bf16[3,96,128]{2,1,0:T(8,128)(2,1)S(1)}, bf16[3,96,128]{2,1,0:T(8,128)(2,1)S(1)}, u32[]{:S(2)}, u32[]{:S(2)}) collective-permute-start(bf16[3,96,128]{2,1,0:T(8,128)(2,1)S(1)} %get-tuple-element.22), channel_id=1, source_target_pairs={{16,0},{17,1},{18,2},{19,3},{20,4},{21,5},{22,6},{23,7},{24,8},{25... | collective-permute-start | bytes 221192 | tf_op jit(solution)/shard_map/ppermute | solution.py:133
  14.1 0.0 collective-permute-done.5.refs_5_
  14.1 0.3 %collective-permute-start.6 = (bf16[3,96,128]{2,1,0:T(8,128)(2,1)S(1)}, bf16[3,96,128]{2,1,0:T(8,128)(2,1)S(1)}, u32[]{:S(2)}, u32[]{:S(2)}) collective-permute-start(bf16[3,96,128]{2,1,0:T(8,128)(2,1)S(1)} %get-tuple-element.22), channel_id=1, source_target_pairs={{2,0},{3,1},{0,2},{1,3},{6,4},{7,5},{4,6},{5,7},{10,8},{11,9},{8,1... | collective-permute-start | bytes 221192 | tf_op jit(solution)/shard_map/ppermute | solution.py:133
  14.4 0.0 collective-permute-done.3.refs_1_
  14.4 2.1 %collective-permute-done.4.refs_3_ = f32[2,96,128]{2,1,0:T(8,128)S(1)} collective-permute-done((f32[2,96,128]{2,1,0:T(8,128)S(1)}, f32[2,96,128]{2,1,0:T(8,128)S(1)}, u32[]{:S(2)}, u32[]{:S(2)}) %collective-permute-start.4) | collective-permute-done | bytes 98336 | tf_op jit(solution)/shard_map/ppermute | solution.py:133
  16.5 0.0 collective-permute-start.9
  16.5 0.5 %collective-permute-start.10 = (f32[1,96,128]{2,1,0:T(8,128)S(1)}, f32[1,96,128]{2,1,0:T(8,128)S(1)}, u32[]{:S(2)}, u32[]{:S(2)}) collective-permute-start(f32[1,96,128]{2,1,0:T(8,128)S(1)} %collective-permute-done.3.refs_1_), channel_id=1, source_target_pairs={{1,0},{0,1},{3,2},{2,3},{5,4},{4,5},{7,6},{6,7},{9,8},{8,9},{11,10... | collective-permute-start | bytes 147464 | tf_op jit(solution)/shard_map/ppermute | solution.py:133
  17.0 0.0 collective-permute-done.8.refs_6_
  17.0 0.0 collective-permute-start.14
  17.0 0.9 %collective-permute-done.7.refs_4_ = bf16[3,96,128]{2,1,0:T(8,128)(2,1)S(1)} collective-permute-done((bf16[3,96,128]{2,1,0:T(8,128)(2,1)S(1)}, bf16[3,96,128]{2,1,0:T(8,128)(2,1)S(1)}, u32[]{:S(2)}, u32[]{:S(2)}) %collective-permute-start.7) | collective-permute-done | bytes 73760 | tf_op jit(solution)/shard_map/ppermute | solution.py:133
  18.0 0.0 collective-permute-start.12
  18.0 0.5 %collective-permute-done.6.refs_2_ = bf16[3,96,128]{2,1,0:T(8,128)(2,1)S(1)} collective-permute-done((bf16[3,96,128]{2,1,0:T(8,128)(2,1)S(1)}, bf16[3,96,128]{2,1,0:T(8,128)(2,1)S(1)}, u32[]{:S(2)}, u32[]{:S(2)}) %collective-permute-start.6) | collective-permute-done | bytes 73760 | tf_op jit(solution)/shard_map/ppermute | solution.py:133
  18.5 0.0 collective-permute-start.15
  18.5 0.0 collective-permute-done.10.refs_8_
  18.5 0.5 %collective-permute-start.13 = (bf16[3,96,128]{2,1,0:T(8,128)(2,1)S(1)}, bf16[3,96,128]{2,1,0:T(8,128)(2,1)S(1)}, u32[]{:S(2)}, u32[]{:S(2)}) collective-permute-start(bf16[3,96,128]{2,1,0:T(8,128)(2,1)S(1)} %collective-permute-done.7.refs_4_), channel_id=1, source_target_pairs={{1,0},{0,1},{3,2},{2,3},{5,4},{4,5},{7,6},{6,7},{9,8},{8,9},{11,10... | collective-permute-start | bytes 221192 | tf_op jit(solution)/shard_map/ppermute | solution.py:133
  19.0 0.0 collective-permute-done.14.refs_12_
  19.0 0.1 collective-permute-start.11
  19.1 0.2 collective-permute-done.12.refs_10_
  19.3 0.5 %collective-permute-done.15.refs_13_ = bf16[3,96,128]{2,1,0:T(8,128)(2,1)S(1)} collective-permute-done((bf16[3,96,128]{2,1,0:T(8,128)(2,1)S(1)}, bf16[3,96,128]{2,1,0:T(8,128)(2,1)S(1)}, u32[]{:S(2)}, u32[]{:S(2)}) %collective-permute-start.15) | collective-permute-done | bytes 73760 | tf_op jit(solution)/shard_map/ppermute | solution.py:133
  19.7 0.2 collective-permute-done.13.refs_11_
  19.9 0.4 %collective-permute-done.11.refs_9_ = bf16[3,96,128]{2,1,0:T(8,128)(2,1)S(1)} collective-permute-done((bf16[3,96,128]{2,1,0:T(8,128)(2,1)S(1)}, bf16[3,96,128]{2,1,0:T(8,128)(2,1)S(1)}, u32[]{:S(2)}, u32[]{:S(2)}) %collective-permute-start.11) | collective-permute-done | bytes 73760 | tf_op jit(solution)/shard_map/ppermute | solution.py:133
  20.3 0.0 collective-permute-done.9.refs_7_
  20.3 0.0 copy-done
  20.3 0.0 copy-done.3
  20.3 3.5 %shard_map.48 = f32[1,12288]{1,0:T(1,128)} custom-call(s32[7,24]{1,0:T(8,128)S(1)} %bitcast.9, bf16[6,96,128]{2,1,0:T(8,128)(2,1)S(1)} %get-tuple-element.20.refs_0_, f32[1,96,128]{2,1,0:T(8,128)S(1)} %collective-permute-done.3.refs_1_, bf16[3,96,128]{2,1,0:T(8,128)(2,1)S(1)} %collective-permute-done.6.refs_2_, ...), custom_call_target="tpu_custom_call" | custom-call | tf_op jit(solution)/shard_map/pallas_call | solution.py:197
  (2 shorter events, 0.1 us)
Async XLA Ops:
  0.0 10.5 %collective-permute-start.2 = (f32[96,128]{1,0:T(8,128)}, f32[96,128]{1,0:T(8,128)S(1)}, u32[]{:S(2)}, u32[]{:S(2)}) collective-permute-start(f32[96,128]{1,0:T(8,128)} %bitcast.3), channel_id=1, source_target_pairs={{12,0},{13,1},{14,2},{15,3},{8,4},{9,5},{10,6},{11,7},{4,8},{5,9},... | collective-permute-start | bytes 147464 | tf_op jit(solution)/shard_map/ppermute | solution.py:133
  5.0 5.8 %collective-permute-start.1 = (f32[96,128]{1,0:T(8,128)}, f32[96,128]{1,0:T(8,128)S(1)}, u32[]{:S(2)}, u32[]{:S(2)}) collective-permute-start(f32[96,128]{1,0:T(8,128)} %bitcast.4), channel_id=1, source_target_pairs={{8,0},{9,1},{10,2},{11,3},{12,4},{13,5},{14,6},{15,7},{0,8},{1,9},... | collective-permute-start | bytes 147464 | tf_op jit(solution)/shard_map/ppermute | solution.py:133
  5.1 5.8 %collective-permute-start = (f32[96,128]{1,0:T(8,128)}, f32[96,128]{1,0:T(8,128)S(1)}, u32[]{:S(2)}, u32[]{:S(2)}) collective-permute-start(f32[96,128]{1,0:T(8,128)} %bitcast.5), channel_id=1, source_target_pairs={{4,0},{5,1},{6,2},{7,3},{0,4},{1,5},{2,6},{3,7},{12,8},{13,9},{14,... | collective-permute-start | bytes 147464 | tf_op jit(solution)/shard_map/ppermute | solution.py:133
  5.6 8.5 %collective-permute-start.5 = (f32[1,96,128]{2,1,0:T(8,128)}, f32[1,96,128]{2,1,0:T(8,128)S(1)}, u32[]{:S(2)}, u32[]{:S(2)}) collective-permute-start(f32[1,96,128]{2,1,0:T(8,128)} %bitcast.6), channel_id=1, source_target_pairs={{18,0},{19,1},{16,2},{17,3},{22,4},{23,5},{20,6},{21,7},{26,8},{27... | collective-permute-start | bytes 147464 | tf_op jit(solution)/shard_map/ppermute | solution.py:133
  8.3 6.2 %collective-permute-start.3 = (f32[1,96,128]{2,1,0:T(8,128)}, f32[1,96,128]{2,1,0:T(8,128)S(1)}, u32[]{:S(2)}, u32[]{:S(2)}) collective-permute-start(f32[1,96,128]{2,1,0:T(8,128)} %bitcast.7), channel_id=1, source_target_pairs={{2,0},{3,1},{0,2},{1,3},{6,4},{7,5},{4,6},{5,7},{10,8},{11,9},{8,1... | collective-permute-start | bytes 147464 | tf_op jit(solution)/shard_map/ppermute | solution.py:133
  8.8 0.8 %copy-start.1 = (bf16[1,12288]{1,0:T(2,128)(2,1)S(1)}, bf16[1,12288]{1,0:T(2,128)(2,1)}, u32[]{:S(2)}) copy-start(bf16[1,12288]{1,0:T(2,128)(2,1)} %inc_ref.1) | copy-start | bytes 73732
  9.6 0.8 %copy-start.2 = (f32[1,12288]{1,0:T(1,128)S(1)}, f32[1,12288]{1,0:T(1,128)}, u32[]{:S(2)}) copy-start(f32[1,12288]{1,0:T(1,128)} %param.4) | copy-start | bytes 147460
  10.5 9.8 %copy-start = (bf16[8,512,512]{2,1,0:T(8,128)(2,1)S(1)}, bf16[8,512,512]{2,1,0:T(8,128)(2,1)}, u32[]{:S(2)}) copy-start(bf16[8,512,512]{2,1,0:T(8,128)(2,1)} %refs_15_.1) | copy-start | bytes 12582916
  10.5 9.8 %copy-start.3 = (s32[24,7]{0,1:T(8,128)S(1)}, s32[24,7]{0,1:T(8,128)}, u32[]{:S(2)}) copy-start(s32[24,7]{0,1:T(8,128)} %param.6) | copy-start | bytes 2020
  10.5 6.0 %collective-permute-start.4 = (f32[2,96,128]{2,1,0:T(8,128)S(1)}, f32[2,96,128]{2,1,0:T(8,128)S(1)}, u32[]{:S(2)}, u32[]{:S(2)}) collective-permute-start(f32[2,96,128]{2,1,0:T(8,128)S(1)} %shard_map.46.pair_ref.refs_14_), channel_id=1, source_target_pairs={{16,0},{17,1},{18,2},{19,3},{20,4},{21,5},{22,6},{23,7},{24,8},{25... | collective-permute-start | bytes 294920 | tf_op jit(solution)/shard_map/ppermute | solution.py:133
  10.9 6.2 %collective-permute-start.8 = (bf16[3,96,128]{2,1,0:T(8,128)(2,1)S(1)}, bf16[3,96,128]{2,1,0:T(8,128)(2,1)S(1)}, u32[]{:S(2)}, u32[]{:S(2)}) collective-permute-start(bf16[3,96,128]{2,1,0:T(8,128)(2,1)S(1)} %get-tuple-element.22), channel_id=1, source_target_pairs={{18,0},{19,1},{16,2},{17,3},{22,4},{23,5},{20,6},{21,7},{26,8},{27... | collective-permute-start | bytes 221192 | tf_op jit(solution)/shard_map/ppermute | solution.py:133
  13.6 4.4 %collective-permute-start.7 = (bf16[3,96,128]{2,1,0:T(8,128)(2,1)S(1)}, bf16[3,96,128]{2,1,0:T(8,128)(2,1)S(1)}, u32[]{:S(2)}, u32[]{:S(2)}) collective-permute-start(bf16[3,96,128]{2,1,0:T(8,128)(2,1)S(1)} %get-tuple-element.22), channel_id=1, source_target_pairs={{16,0},{17,1},{18,2},{19,3},{20,4},{21,5},{22,6},{23,7},{24,8},{25... | collective-permute-start | bytes 221192 | tf_op jit(solution)/shard_map/ppermute | solution.py:133
  14.1 4.4 %collective-permute-start.6 = (bf16[3,96,128]{2,1,0:T(8,128)(2,1)S(1)}, bf16[3,96,128]{2,1,0:T(8,128)(2,1)S(1)}, u32[]{:S(2)}, u32[]{:S(2)}) collective-permute-start(bf16[3,96,128]{2,1,0:T(8,128)(2,1)S(1)} %get-tuple-element.22), channel_id=1, source_target_pairs={{2,0},{3,1},{0,2},{1,3},{6,4},{7,5},{4,6},{5,7},{10,8},{11,9},{8,1... | collective-permute-start | bytes 221192 | tf_op jit(solution)/shard_map/ppermute | solution.py:133
  16.5 3.7 %collective-permute-start.9 = (bf16[6,96,128]{2,1,0:T(8,128)(2,1)S(1)}, bf16[6,96,128]{2,1,0:T(8,128)(2,1)S(1)}, u32[]{:S(2)}, u32[]{:S(2)}) collective-permute-start(bf16[6,96,128]{2,1,0:T(8,128)(2,1)S(1)} %get-tuple-element.20.refs_0_), channel_id=1, source_target_pairs={{1,0},{0,1},{3,2},{2,3},{5,4},{4,5},{7,6},{6,7},{9,8},{8,9},{11,10... | collective-permute-start | bytes 442376 | tf_op jit(solution)/shard_map/ppermute | solution.py:133
  16.5 2.0 %collective-permute-start.10 = (f32[1,96,128]{2,1,0:T(8,128)S(1)}, f32[1,96,128]{2,1,0:T(8,128)S(1)}, u32[]{:S(2)}, u32[]{:S(2)}) collective-permute-start(f32[1,96,128]{2,1,0:T(8,128)S(1)} %collective-permute-done.3.refs_1_), channel_id=1, source_target_pairs={{1,0},{0,1},{3,2},{2,3},{5,4},{4,5},{7,6},{6,7},{9,8},{8,9},{11,10... | collective-permute-start | bytes 147464 | tf_op jit(solution)/shard_map/ppermute | solution.py:133
  17.0 2.0 %collective-permute-start.14 = (f32[1,96,128]{2,1,0:T(8,128)S(1)}, f32[1,96,128]{2,1,0:T(8,128)S(1)}, u32[]{:S(2)}, u32[]{:S(2)}) collective-permute-start(f32[1,96,128]{2,1,0:T(8,128)S(1)} %collective-permute-done.5.refs_5_), channel_id=1, source_target_pairs={{1,0},{0,1},{3,2},{2,3},{5,4},{4,5},{7,6},{6,7},{9,8},{8,9},{11,10... | collective-permute-start | bytes 147464 | tf_op jit(solution)/shard_map/ppermute | solution.py:133
  18.0 1.3 %collective-permute-start.12 = (f32[2,96,128]{2,1,0:T(8,128)S(1)}, f32[2,96,128]{2,1,0:T(8,128)S(1)}, u32[]{:S(2)}, u32[]{:S(2)}) collective-permute-start(f32[2,96,128]{2,1,0:T(8,128)S(1)} %collective-permute-done.4.refs_3_), channel_id=1, source_target_pairs={{1,0},{0,1},{3,2},{2,3},{5,4},{4,5},{7,6},{6,7},{9,8},{8,9},{11,10... | collective-permute-start | bytes 294920 | tf_op jit(solution)/shard_map/ppermute | solution.py:133
  18.5 1.3 %collective-permute-start.15 = (bf16[3,96,128]{2,1,0:T(8,128)(2,1)S(1)}, bf16[3,96,128]{2,1,0:T(8,128)(2,1)S(1)}, u32[]{:S(2)}, u32[]{:S(2)}) collective-permute-start(bf16[3,96,128]{2,1,0:T(8,128)(2,1)S(1)} %collective-permute-done.8.refs_6_), channel_id=1, source_target_pairs={{1,0},{0,1},{3,2},{2,3},{5,4},{4,5},{7,6},{6,7},{9,8},{8,9},{11,10... | collective-permute-start | bytes 221192 | tf_op jit(solution)/shard_map/ppermute | solution.py:133
  18.5 1.4 %collective-permute-start.13 = (bf16[3,96,128]{2,1,0:T(8,128)(2,1)S(1)}, bf16[3,96,128]{2,1,0:T(8,128)(2,1)S(1)}, u32[]{:S(2)}, u32[]{:S(2)}) collective-permute-start(bf16[3,96,128]{2,1,0:T(8,128)(2,1)S(1)} %collective-permute-done.7.refs_4_), channel_id=1, source_target_pairs={{1,0},{0,1},{3,2},{2,3},{5,4},{4,5},{7,6},{6,7},{9,8},{8,9},{11,10... | collective-permute-start | bytes 221192 | tf_op jit(solution)/shard_map/ppermute | solution.py:133
  19.0 1.3 %collective-permute-start.11 = (bf16[3,96,128]{2,1,0:T(8,128)(2,1)S(1)}, bf16[3,96,128]{2,1,0:T(8,128)(2,1)S(1)}, u32[]{:S(2)}, u32[]{:S(2)}) collective-permute-start(bf16[3,96,128]{2,1,0:T(8,128)(2,1)S(1)} %collective-permute-done.6.refs_2_), channel_id=1, source_target_pairs={{1,0},{0,1},{3,2},{2,3},{5,4},{4,5},{7,6},{6,7},{9,8},{8,9},{11,10... | collective-permute-start | bytes 221192 | tf_op jit(solution)/shard_map/ppermute | solution.py:133

commit v10 on v9

--- a/solution.py
+++ b/solution.py
@@ -11,9 +11,19 @@
 SUB = 8
 VMEM_LIMIT = 16 * 1024 * 1024
 PACK_COST = 20_000_000_000
-
-
-def pair_kernel(base_ref, inc_ref, pair_ref):
+FIRST_COST = 2_000_000_000
+
+
+def first_kernel(out_ref):
+    out_ref[...] = jnp.zeros_like(out_ref)
+
+
+def bases_kernel(x_ref, y_ref, diag_ref, out_ref):
+    for j, ref in enumerate((x_ref, y_ref, diag_ref)):
+        out_ref[j] = ref[0]
+
+
+def pair_kernel(first_ref, base_ref, inc_ref, pair_ref):
     pair_ref[0] = base_ref[...]
     for r in range(base_ref.shape[0]):
         part = inc_ref[:, r * LANES : (r + 1) * LANES]
@@ -36,11 +46,9 @@
 
 
 def product_kernel(group, off_ref, *refs):
-    half = len(refs[:14]) // 2
-    cores = refs[:half], refs[half : 2 * half]
-    inc_own, inc_other = refs[14], refs[3]
-    tiles, out_ref = refs[15:17]
-    pert, picked_from, acc = refs[17:]
+    cores = refs[:5], refs[5:10]
+    inc_other, inc_own, tiles, out_ref = refs[10:14]
+    pert, picked_from, acc = refs[14:]
     slots, block_size, _ = tiles.shape
     members = 4 * group
     rows = inc_other.shape[1]
@@ -50,9 +58,11 @@
 
     def weigh(side, increment):
         if side == 0:
-            lines = [pair for core in cores for pair in ((None, core[0]), core[1:3])]
+            lines = [pair for core in cores for pair in ((None, core[0]), (core[1].at[0], core[2]))]
         else:
-            lines = [pair for core in cores for pair in (core[3:5], core[5:7])]
+            lines = [
+                (core[1].at[j], core[2 + j]) for core in cores for j in (1, 2)
+            ]
 
         def chunk(r, carry):
             at = pl.multiple_of(r * 2 * SUB, 2 * SUB)
@@ -63,7 +73,7 @@
                     high, middle, low = (ref[k, here, :].astype(jnp.float32) for k in range(3))
                     starts.append(high + middle + low)
                 else:
-                    starts.append(base[0, here, :])
+                    starts.append(base[here, :])
                 first = ref.shape[0] - (group - 1)
                 steps.append(
                     [ref[first + k, here, :].astype(jnp.float32) for k in range(group - 1)]
@@ -162,15 +172,23 @@
     line = [move(base, False, turn(d)) for d in range(1, group)]
     whole = pl.BlockSpec(memory_space=pltpu.VMEM)
     small = pltpu.CompilerParams(vmem_limit_bytes=4 * 1024 * 1024)
+    first = pl.pallas_call(
+        first_kernel,
+        out_shape=jax.ShapeDtypeStruct((SUB, LANES), jnp.float32),
+        out_specs=whole,
+        compiler_params=small,
+        cost_estimate=pl.CostEstimate(flops=FIRST_COST, bytes_accessed=4096, transcendentals=0),
+    )()
     pair = pl.pallas_call(
         pair_kernel,
         out_shape=jax.ShapeDtypeStruct((2, rows, LANES), jnp.float32),
-        in_specs=[whole] * 2,
-        out_specs=whole,
-        compiler_params=small,
-    )(base, increments)
-    base_x = move(base[None], False, beside)
-    base_diag = move(base[None], True, beside)
+        in_specs=[whole] * 3,
+        out_specs=whole,
+        compiler_params=small,
+    )(first, base, increments)
+    later, _ = lax.optimization_barrier((base, first))
+    base_x = move(later[None], False, beside)
+    base_diag = move(later[None], True, beside)
     base_y = move(pair, True, same)
     pair, line = lax.optimization_barrier((pair, line))
 
@@ -190,14 +208,21 @@
     x, y = move(diff, False, beside), move(diff, True, same)
     diag = move(diff, True, beside)
     mine, base_x, base_y, base_diag = lax.optimization_barrier((mine, base_x, base_y, base_diag))
-    lines = [mine, base_x, x, base_y, y, base_diag, diag]
+    bases = pl.pallas_call(
+        bases_kernel,
+        out_shape=jax.ShapeDtypeStruct((3, rows, LANES), jnp.float32),
+        in_specs=[whole] * 3,
+        out_specs=whole,
+        compiler_params=small,
+    )(base_x, base_y, base_diag)
+    lines = [mine, bases, x, y, diag]
     lines += [move(v, False, lambda m: m ^ 1) for v in lines]
 
     vectors = mem_size * block_count
     return pl.pallas_call(
         functools.partial(product_kernel, group),
         out_shape=jax.ShapeDtypeStruct((1, columns), jnp.float32),
-        in_specs=[pl.BlockSpec(memory_space=pltpu.SMEM)] + [whole] * 16,
+        in_specs=[pl.BlockSpec(memory_space=pltpu.SMEM)] + [whole] * 13,
         out_specs=whole,
         scratch_shapes=[
             pltpu.VMEM((mem_size * (rows + 1), LANES), jnp.float32),
@@ -205,7 +230,7 @@
             pltpu.VMEM((vectors, block_size), jnp.float32),
         ],
         compiler_params=pltpu.CompilerParams(vmem_limit_bytes=VMEM_LIMIT),
-    )(offsets.T, *lines, pair, taper)
+    )(offsets.T, *lines, base_y, pair, taper)
 
 
 def solution(mesh):

time: 24 us -> 22.6 us (0.942)
  local copies, waits for them, and re-layouts: 1.61 us -> 0.02 us
  waiting for transfers between devices: 4.73 us -> 5.38 us
  starting transfers between devices: 13.8 us -> 13.4 us
    unnamed x8, local copies, waits for them, and re-layouts: 1.61 us -> 0.02 us
    ppermute x16 -> x14, waiting for transfers between devices: 4.73 us -> 5.38 us  [one(): return lax.ppermute(x, ('lon', 'mem'), perm)]
    ppermute x16 -> x14, starting transfers between devices: 13.8 us -> 13.4 us  [one(): return lax.ppermute(x, ('lon', 'mem'), perm)]
  transfers between devices with their start and end apart: 16 -> 14, of which waited for: 7 -> 7; matrix products, arithmetic and copies ran while one was open for 0% -> 0% of each run, Pallas kernels for 0% -> 0%
where the time goes in v10:
time: 22.6 us; the launch traced here: 22.4 us
  starting transfers between devices  13.4 us (59%)
  waiting for transfers between devices  5.38 us (24%)
  Pallas kernels  3.54 us (16%)
    ppermute x14, starting transfers between devices, one(): return lax.ppermute(x, ('lon', 'mem'), perm)  13.4 us
    ppermute x14, waiting for transfers between devices, one(): return lax.ppermute(x, ('lon', 'mem'), perm)  5.38 us
    pallas_call x1, Pallas kernels, on_device(): pl.pallas_call(functools.partial(product_kernel, group), out_shape=jax.Sh...  3.47 us
  transfers between devices with their start and end apart: 14, of which 7 were waited for; matrix products, arithmetic and copies ran while one was open for 0% of the time, Pallas kernels for 0%

profile of v10, /device:TPU:0, one launch (start us, length us, event | category | flops | bytes accessed | tf_op | source)
XLA Modules:
  0.0 22.4 jit_solution(6529677797790892343)
XLA Ops:
  0.0 0.0 copy-start.2
  0.0 0.0 copy-start.1
  0.0 5.0 %collective-permute-start.2 = (f32[96,128]{1,0:T(8,128)}, f32[96,128]{1,0:T(8,128)S(1)}, u32[]{:S(2)}, u32[]{:S(2)}) collective-permute-start(f32[96,128]{1,0:T(8,128)} %bitcast.3), channel_id=1, source_target_pairs={{12,0},{13,1},{14,2},{15,3},{8,4},{9,5},{10,6},{11,7},{4,8},{5,9},... | collective-permute-start | bytes 147464 | tf_op jit(solution)/shard_map/ppermute | solution.py:143
  5.1 0.0 collective-permute-start.1
  5.1 0.6 %collective-permute-start = (f32[96,128]{1,0:T(8,128)}, f32[96,128]{1,0:T(8,128)S(1)}, u32[]{:S(2)}, u32[]{:S(2)}) collective-permute-start(f32[96,128]{1,0:T(8,128)} %bitcast.5), channel_id=1, source_target_pairs={{4,0},{5,1},{6,2},{7,3},{0,4},{1,5},{2,6},{3,7},{12,8},{13,9},{14,... | collective-permute-start | bytes 147464 | tf_op jit(solution)/shard_map/ppermute | solution.py:143
  5.7 0.0 copy-done.2
  5.7 2.6 %collective-permute-start.5 = (f32[1,96,128]{2,1,0:T(8,128)S(1)}, f32[1,96,128]{2,1,0:T(8,128)S(1)}, u32[]{:S(2)}, u32[]{:S(2)}) collective-permute-start(f32[1,96,128]{2,1,0:T(8,128)S(1)} %bitcast.6), channel_id=1, source_target_pairs={{18,0},{19,1},{16,2},{17,3},{22,4},{23,5},{20,6},{21,7},{26,8},{27... | collective-permute-start | bytes 147464 | tf_op jit(solution)/shard_map/ppermute | solution.py:143
  8.3 0.5 %collective-permute-start.3 = (f32[1,96,128]{2,1,0:T(8,128)S(1)}, f32[1,96,128]{2,1,0:T(8,128)S(1)}, u32[]{:S(2)}, u32[]{:S(2)}) collective-permute-start(f32[1,96,128]{2,1,0:T(8,128)S(1)} %bitcast.7), channel_id=1, source_target_pairs={{2,0},{3,1},{0,2},{1,3},{6,4},{7,5},{4,6},{5,7},{10,8},{11,9},{8,1... | collective-permute-start | bytes 147464 | tf_op jit(solution)/shard_map/ppermute | solution.py:143
  8.8 0.0 copy-done.1
  8.9 0.0 copy-start
  8.9 0.0 copy-start.3
  8.9 0.0 collective-permute-done.2.refs_2_
  8.9 0.5 %collective-permute-start.4 = (f32[2,96,128]{2,1,0:T(8,128)S(1)}, f32[2,96,128]{2,1,0:T(8,128)S(1)}, u32[]{:S(2)}, u32[]{:S(2)}) collective-permute-start(f32[2,96,128]{2,1,0:T(8,128)S(1)} %shard_map.47.pair_ref.refs_11_), channel_id=1, source_target_pairs={{16,0},{17,1},{18,2},{19,3},{20,4},{21,5},{22,6},{23,7},{24,8},{25... | collective-permute-start | bytes 294920 | tf_op jit(solution)/shard_map/ppermute | solution.py:143
  9.4 0.9 %collective-permute-done.1.refs_1_ = f32[96,128]{1,0:T(8,128)S(1)} collective-permute-done((f32[96,128]{1,0:T(8,128)}, f32[96,128]{1,0:T(8,128)S(1)}, u32[]{:S(2)}, u32[]{:S(2)}) %collective-permute-start.1) | collective-permute-done | bytes 49184 | tf_op jit(solution)/shard_map/ppermute | solution.py:143
  10.3 0.0 collective-permute-done.refs_0_
  10.3 2.5 %collective-permute-start.8 = (bf16[3,96,128]{2,1,0:T(8,128)(2,1)S(1)}, bf16[3,96,128]{2,1,0:T(8,128)(2,1)S(1)}, u32[]{:S(2)}, u32[]{:S(2)}) collective-permute-start(bf16[3,96,128]{2,1,0:T(8,128)(2,1)S(1)} %get-tuple-element.26), channel_id=1, source_target_pairs={{18,0},{19,1},{16,2},{17,3},{22,4},{23,5},{20,6},{21,7},{26,8},{27... | collective-permute-start | bytes 221192 | tf_op jit(solution)/shard_map/ppermute | solution.py:143
  12.8 0.5 %collective-permute-start.7 = (bf16[3,96,128]{2,1,0:T(8,128)(2,1)S(1)}, bf16[3,96,128]{2,1,0:T(8,128)(2,1)S(1)}, u32[]{:S(2)}, u32[]{:S(2)}) collective-permute-start(bf16[3,96,128]{2,1,0:T(8,128)(2,1)S(1)} %get-tuple-element.26), channel_id=1, source_target_pairs={{16,0},{17,1},{18,2},{19,3},{20,4},{21,5},{22,6},{23,7},{24,8},{25... | collective-permute-start | bytes 221192 | tf_op jit(solution)/shard_map/ppermute | solution.py:143
  13.3 0.0 collective-permute-done.5.diag_ref
  13.3 0.5 %collective-permute-start.6 = (bf16[3,96,128]{2,1,0:T(8,128)(2,1)S(1)}, bf16[3,96,128]{2,1,0:T(8,128)(2,1)S(1)}, u32[]{:S(2)}, u32[]{:S(2)}) collective-permute-start(bf16[3,96,128]{2,1,0:T(8,128)(2,1)S(1)} %get-tuple-element.26), channel_id=1, source_target_pairs={{2,0},{3,1},{0,2},{1,3},{6,4},{7,5},{4,6},{5,7},{10,8},{11,9},{8,1... | collective-permute-start | bytes 221192 | tf_op jit(solution)/shard_map/ppermute | solution.py:143
  13.8 0.0 collective-permute-done.3.x_ref
  13.8 0.8 %collective-permute-done.4.y_ref.refs_10_ = f32[2,96,128]{2,1,0:T(8,128)S(1)} collective-permute-done((f32[2,96,128]{2,1,0:T(8,128)S(1)}, f32[2,96,128]{2,1,0:T(8,128)S(1)}, u32[]{:S(2)}, u32[]{:S(2)}) %collective-permute-start.4) | collective-permute-done | bytes 98336 | tf_op jit(solution)/shard_map/ppermute | solution.py:143
  14.6 0.1 collective-permute-start.10
  14.7 0.5 %collective-permute-start.9 = (bf16[6,96,128]{2,1,0:T(8,128)(2,1)S(1)}, bf16[6,96,128]{2,1,0:T(8,128)(2,1)S(1)}, u32[]{:S(2)}, u32[]{:S(2)}) collective-permute-start(bf16[6,96,128]{2,1,0:T(8,128)(2,1)S(1)} %get-tuple-element.22.refs_0_), channel_id=1, source_target_pairs={{1,0},{0,1},{3,2},{2,3},{5,4},{4,5},{7,6},{6,7},{9,8},{8,9},{11,10... | collective-permute-start | bytes 442376 | tf_op jit(solution)/shard_map/ppermute | solution.py:143
  15.2 0.8 %collective-permute-done.8.refs_4_ = bf16[3,96,128]{2,1,0:T(8,128)(2,1)S(1)} collective-permute-done((bf16[3,96,128]{2,1,0:T(8,128)(2,1)S(1)}, bf16[3,96,128]{2,1,0:T(8,128)(2,1)S(1)}, u32[]{:S(2)}, u32[]{:S(2)}) %collective-permute-start.8) | collective-permute-done | bytes 73760 | tf_op jit(solution)/shard_map/ppermute | solution.py:143
  16.0 0.0 collective-permute-start.13
  16.0 1.1 %collective-permute-done.7.refs_3_ = bf16[3,96,128]{2,1,0:T(8,128)(2,1)S(1)} collective-permute-done((bf16[3,96,128]{2,1,0:T(8,128)(2,1)S(1)}, bf16[3,96,128]{2,1,0:T(8,128)(2,1)S(1)}, u32[]{:S(2)}, u32[]{:S(2)}) %collective-permute-start.7) | collective-permute-done | bytes 73760 | tf_op jit(solution)/shard_map/ppermute | solution.py:143
  17.2 0.0 collective-permute-start.12
  17.2 0.5 %collective-permute-done.6.refs_2_ = bf16[3,96,128]{2,1,0:T(8,128)(2,1)S(1)} collective-permute-done((bf16[3,96,128]{2,1,0:T(8,128)(2,1)S(1)}, bf16[3,96,128]{2,1,0:T(8,128)(2,1)S(1)}, u32[]{:S(2)}, u32[]{:S(2)}) %collective-permute-start.6) | collective-permute-done | bytes 73760 | tf_op jit(solution)/shard_map/ppermute | solution.py:143
  17.7 0.0 collective-permute-start.11
  17.7 0.0 collective-permute-done.13.refs_9_
  17.7 0.7 %collective-permute-done.12.refs_8_ = bf16[3,96,128]{2,1,0:T(8,128)(2,1)S(1)} collective-permute-done((bf16[3,96,128]{2,1,0:T(8,128)(2,1)S(1)}, bf16[3,96,128]{2,1,0:T(8,128)(2,1)S(1)}, u32[]{:S(2)}, u32[]{:S(2)}) %collective-permute-start.12) | collective-permute-done | bytes 73760 | tf_op jit(solution)/shard_map/ppermute | solution.py:143
  18.4 0.5 %collective-permute-done.11.refs_7_ = bf16[3,96,128]{2,1,0:T(8,128)(2,1)S(1)} collective-permute-done((bf16[3,96,128]{2,1,0:T(8,128)(2,1)S(1)}, bf16[3,96,128]{2,1,0:T(8,128)(2,1)S(1)}, u32[]{:S(2)}, u32[]{:S(2)}) %collective-permute-start.11) | collective-permute-done | bytes 73760 | tf_op jit(solution)/shard_map/ppermute | solution.py:143
  18.9 0.0 collective-permute-done.10.refs_6_
  18.9 0.0 collective-permute-done.9.refs_5_
  18.9 0.0 copy-done
  18.9 0.0 copy-done.3
  18.9 3.5 %shard_map.50 = f32[1,12288]{1,0:T(1,128)} custom-call(s32[7,24]{1,0:T(8,128)S(1)} %bitcast.9, bf16[6,96,128]{2,1,0:T(8,128)(2,1)S(1)} %get-tuple-element.22.refs_0_, f32[3,96,128]{2,1,0:T(8,128)S(1)} %shard_map.49.refs_1_, bf16[3,96,128]{2,1,0:T(8,128)(2,1)S(1)} %collective-permute-done.6.refs_2_, bf16[3,96,128]{2,1,0:T(8,128)(2,1)S(1)} %collective-permute-done.7.refs_3_, ...), custom_call_target="tpu_custom_call" | custom-call | tf_op jit(solution)/shard_map/pallas_call | solution.py:222
  (4 shorter events, 0.1 us)
Async XLA Ops:
  0.0 5.7 %copy-start.2 = (f32[1,12288]{1,0:T(1,128)S(1)}, f32[1,12288]{1,0:T(1,128)}, u32[]{:S(2)}) copy-start(f32[1,12288]{1,0:T(1,128)} %param.4) | copy-start | bytes 147460
  0.0 8.8 %copy-start.1 = (bf16[1,12288]{1,0:T(2,128)(2,1)S(1)}, bf16[1,12288]{1,0:T(2,128)(2,1)}, u32[]{:S(2)}) copy-start(bf16[1,12288]{1,0:T(2,128)(2,1)} %inc_ref.1) | copy-start | bytes 73732
  0.0 8.9 %collective-permute-start.2 = (f32[96,128]{1,0:T(8,128)}, f32[96,128]{1,0:T(8,128)S(1)}, u32[]{:S(2)}, u32[]{:S(2)}) collective-permute-start(f32[96,128]{1,0:T(8,128)} %bitcast.3), channel_id=1, source_target_pairs={{12,0},{13,1},{14,2},{15,3},{8,4},{9,5},{10,6},{11,7},{4,8},{5,9},... | collective-permute-start | bytes 147464 | tf_op jit(solution)/shard_map/ppermute | solution.py:143
  5.1 5.2 %collective-permute-start.1 = (f32[96,128]{1,0:T(8,128)}, f32[96,128]{1,0:T(8,128)S(1)}, u32[]{:S(2)}, u32[]{:S(2)}) collective-permute-start(f32[96,128]{1,0:T(8,128)} %bitcast.4), channel_id=1, source_target_pairs={{8,0},{9,1},{10,2},{11,3},{12,4},{13,5},{14,6},{15,7},{0,8},{1,9},... | collective-permute-start | bytes 147464 | tf_op jit(solution)/shard_map/ppermute | solution.py:143
  5.1 5.2 %collective-permute-start = (f32[96,128]{1,0:T(8,128)}, f32[96,128]{1,0:T(8,128)S(1)}, u32[]{:S(2)}, u32[]{:S(2)}) collective-permute-start(f32[96,128]{1,0:T(8,128)} %bitcast.5), channel_id=1, source_target_pairs={{4,0},{5,1},{6,2},{7,3},{0,4},{1,5},{2,6},{3,7},{12,8},{13,9},{14,... | collective-permute-start | bytes 147464 | tf_op jit(solution)/shard_map/ppermute | solution.py:143
  5.7 7.6 %collective-permute-start.5 = (f32[1,96,128]{2,1,0:T(8,128)S(1)}, f32[1,96,128]{2,1,0:T(8,128)S(1)}, u32[]{:S(2)}, u32[]{:S(2)}) collective-permute-start(f32[1,96,128]{2,1,0:T(8,128)S(1)} %bitcast.6), channel_id=1, source_target_pairs={{18,0},{19,1},{16,2},{17,3},{22,4},{23,5},{20,6},{21,7},{26,8},{27... | collective-permute-start | bytes 147464 | tf_op jit(solution)/shard_map/ppermute | solution.py:143
  8.3 5.6 %collective-permute-start.3 = (f32[1,96,128]{2,1,0:T(8,128)S(1)}, f32[1,96,128]{2,1,0:T(8,128)S(1)}, u32[]{:S(2)}, u32[]{:S(2)}) collective-permute-start(f32[1,96,128]{2,1,0:T(8,128)S(1)} %bitcast.7), channel_id=1, source_target_pairs={{2,0},{3,1},{0,2},{1,3},{6,4},{7,5},{4,6},{5,7},{10,8},{11,9},{8,1... | collective-permute-start | bytes 147464 | tf_op jit(solution)/shard_map/ppermute | solution.py:143
  8.9 10.1 %copy-start = (bf16[8,512,512]{2,1,0:T(8,128)(2,1)S(1)}, bf16[8,512,512]{2,1,0:T(8,128)(2,1)}, u32[]{:S(2)}) copy-start(bf16[8,512,512]{2,1,0:T(8,128)(2,1)} %refs_12_.1) | copy-start | bytes 12582916
  8.9 10.1 %copy-start.3 = (s32[24,7]{0,1:T(8,128)S(1)}, s32[24,7]{0,1:T(8,128)}, u32[]{:S(2)}) copy-start(s32[24,7]{0,1:T(8,128)} %param.6) | copy-start | bytes 2020
  8.9 5.7 %collective-permute-start.4 = (f32[2,96,128]{2,1,0:T(8,128)S(1)}, f32[2,96,128]{2,1,0:T(8,128)S(1)}, u32[]{:S(2)}, u32[]{:S(2)}) collective-permute-start(f32[2,96,128]{2,1,0:T(8,128)S(1)} %shard_map.47.pair_ref.refs_11_), channel_id=1, source_target_pairs={{16,0},{17,1},{18,2},{19,3},{20,4},{21,5},{22,6},{23,7},{24,8},{25... | collective-permute-start | bytes 294920 | tf_op jit(solution)/shard_map/ppermute | solution.py:143
  10.3 5.8 %collective-permute-start.8 = (bf16[3,96,128]{2,1,0:T(8,128)(2,1)S(1)}, bf16[3,96,128]{2,1,0:T(8,128)(2,1)S(1)}, u32[]{:S(2)}, u32[]{:S(2)}) collective-permute-start(bf16[3,96,128]{2,1,0:T(8,128)(2,1)S(1)} %get-tuple-element.26), channel_id=1, source_target_pairs={{18,0},{19,1},{16,2},{17,3},{22,4},{23,5},{20,6},{21,7},{26,8},{27... | collective-permute-start | bytes 221192 | tf_op jit(solution)/shard_map/ppermute | solution.py:143
  12.8 4.4 %collective-permute-start.7 = (bf16[3,96,128]{2,1,0:T(8,128)(2,1)S(1)}, bf16[3,96,128]{2,1,0:T(8,128)(2,1)S(1)}, u32[]{:S(2)}, u32[]{:S(2)}) collective-permute-start(bf16[3,96,128]{2,1,0:T(8,128)(2,1)S(1)} %get-tuple-element.26), channel_id=1, source_target_pairs={{16,0},{17,1},{18,2},{19,3},{20,4},{21,5},{22,6},{23,7},{24,8},{25... | collective-permute-start | bytes 221192 | tf_op jit(solution)/shard_map/ppermute | solution.py:143
  13.3 4.4 %collective-permute-start.6 = (bf16[3,96,128]{2,1,0:T(8,128)(2,1)S(1)}, bf16[3,96,128]{2,1,0:T(8,128)(2,1)S(1)}, u32[]{:S(2)}, u32[]{:S(2)}) collective-permute-start(bf16[3,96,128]{2,1,0:T(8,128)(2,1)S(1)} %get-tuple-element.26), channel_id=1, source_target_pairs={{2,0},{3,1},{0,2},{1,3},{6,4},{7,5},{4,6},{5,7},{10,8},{11,9},{8,1... | collective-permute-start | bytes 221192 | tf_op jit(solution)/shard_map/ppermute | solution.py:143
  14.6 4.3 %collective-permute-start.10 = (f32[3,96,128]{2,1,0:T(8,128)S(1)}, f32[3,96,128]{2,1,0:T(8,128)S(1)}, u32[]{:S(2)}, u32[]{:S(2)}) collective-permute-start(f32[3,96,128]{2,1,0:T(8,128)S(1)} %shard_map.49.refs_1_), channel_id=1, source_target_pairs={{1,0},{0,1},{3,2},{2,3},{5,4},{4,5},{7,6},{6,7},{9,8},{8,9},{11,10... | collective-permute-start | bytes 442376 | tf_op jit(solution)/shard_map/ppermute | solution.py:143
  14.7 4.2 %collective-permute-start.9 = (bf16[6,96,128]{2,1,0:T(8,128)(2,1)S(1)}, bf16[6,96,128]{2,1,0:T(8,128)(2,1)S(1)}, u32[]{:S(2)}, u32[]{:S(2)}) collective-permute-start(bf16[6,96,128]{2,1,0:T(8,128)(2,1)S(1)} %get-tuple-element.22.refs_0_), channel_id=1, source_target_pairs={{1,0},{0,1},{3,2},{2,3},{5,4},{4,5},{7,6},{6,7},{9,8},{8,9},{11,10... | collective-permute-start | bytes 442376 | tf_op jit(solution)/shard_map/ppermute | solution.py:143
  16.0 1.6 %collective-permute-start.13 = (bf16[3,96,128]{2,1,0:T(8,128)(2,1)S(1)}, bf16[3,96,128]{2,1,0:T(8,128)(2,1)S(1)}, u32[]{:S(2)}, u32[]{:S(2)}) collective-permute-start(bf16[3,96,128]{2,1,0:T(8,128)(2,1)S(1)} %collective-permute-done.8.refs_4_), channel_id=1, source_target_pairs={{1,0},{0,1},{3,2},{2,3},{5,4},{4,5},{7,6},{6,7},{9,8},{8,9},{11,10... | collective-permute-start | bytes 221192 | tf_op jit(solution)/shard_map/ppermute | solution.py:143
  17.2 1.3 %collective-permute-start.12 = (bf16[3,96,128]{2,1,0:T(8,128)(2,1)S(1)}, bf16[3,96,128]{2,1,0:T(8,128)(2,1)S(1)}, u32[]{:S(2)}, u32[]{:S(2)}) collective-permute-start(bf16[3,96,128]{2,1,0:T(8,128)(2,1)S(1)} %collective-permute-done.7.refs_3_), channel_id=1, source_target_pairs={{1,0},{0,1},{3,2},{2,3},{5,4},{4,5},{7,6},{6,7},{9,8},{8,9},{11,10... | collective-permute-start | bytes 221192 | tf_op jit(solution)/shard_map/ppermute | solution.py:143
  17.7 1.3 %collective-permute-start.11 = (bf16[3,96,128]{2,1,0:T(8,128)(2,1)S(1)}, bf16[3,96,128]{2,1,0:T(8,128)(2,1)S(1)}, u32[]{:S(2)}, u32[]{:S(2)}) collective-permute-start(bf16[3,96,128]{2,1,0:T(8,128)(2,1)S(1)} %collective-permute-done.6.refs_2_), channel_id=1, source_target_pairs={{1,0},{0,1},{3,2},{2,3},{5,4},{4,5},{7,6},{6,7},{9,8},{8,9},{11,10... | collective-permute-start | bytes 221192 | tf_op jit(solution)/shard_map/ppermute | solution.py:143

commit v11 on v10

--- a/solution.py
+++ b/solution.py
@@ -48,7 +48,7 @@
 def product_kernel(group, off_ref, *refs):
     cores = refs[:5], refs[5:10]
     inc_other, inc_own, tiles, out_ref = refs[10:14]
-    pert, picked_from, acc = refs[14:]
+    pert, pert_other, picked_from, acc = refs[14:]
     slots, block_size, _ = tiles.shape
     members = 4 * group
     rows = inc_other.shape[1]
@@ -56,7 +56,7 @@
     quarters = block_size // LANES
     block_count = rows // quarters
 
-    def weigh(side, increment):
+    def weigh(side, pert, increment):
         if side == 0:
             lines = [pair for core in cores for pair in ((None, core[0]), (core[1].at[0], core[2]))]
         else:
@@ -64,8 +64,8 @@
                 (core[1].at[j], core[2 + j]) for core in cores for j in (1, 2)
             ]
 
-        def chunk(r, carry):
-            at = pl.multiple_of(r * 2 * SUB, 2 * SUB)
+        def chunk(r):
+            at = r * 2 * SUB
             here = pl.ds(at, 2 * SUB)
             starts, steps = [], []
             for base, ref in lines:
@@ -86,9 +86,9 @@
                 for value in [start] + [start + step for step in line]:
                     pert[pl.ds(m * pitch + at, 2 * SUB), :] = value
                     m += 1
-            return carry
-
-        lax.fori_loop(0, rows // (2 * SUB), chunk, 0, unroll=2)
+
+        for r in range(rows // (2 * SUB)):
+            chunk(r)
 
         for i in range(block_count):
             for q in range(quarters):
@@ -97,8 +97,7 @@
                 part = pert[pl.ds(at, members, pitch), :] * increment(at)
                 picked_from[side * block_count + i, :, lanes] = part.astype(jnp.bfloat16)
 
-    weigh(1, lambda at: inc_other[1, at : at + 1, :])
-    weigh(0, lambda at: inc_own[1, at : at + 1, :])
+    weigh(0, pert, lambda at: inc_own[1, at : at + 1, :])
 
     contract = (((1,), (1,)), ((), ()))
     vectors = block_count * members
@@ -108,6 +107,7 @@
         contract,
         preferred_element_type=jnp.float32,
     )
+    weigh(1, pert_other, lambda at: inc_other[1, at : at + 1, :])
     for s in range(1, slots):
         chosen = []
         for i in range(block_count):
@@ -226,6 +226,7 @@
         out_specs=whole,
         scratch_shapes=[
             pltpu.VMEM((mem_size * (rows + 1), LANES), jnp.float32),
+            pltpu.VMEM((mem_size * (rows + 1), LANES), jnp.float32),
             pltpu.VMEM((2 * block_count, mem_size, block_size), jnp.bfloat16),
             pltpu.VMEM((vectors, block_size), jnp.float32),
         ],

time: 22.6 us -> 22.4 us (level)
  no operation moved by 1% of the time
where the time goes in v11:
time: 22.4 us; the launch traced here: 22.3 us
  starting transfers between devices  13.4 us (60%)
  waiting for transfers between devices  5.38 us (24%)
  Pallas kernels  3.4 us (15%)
    ppermute x14, starting transfers between devices, one(): return lax.ppermute(x, ('lon', 'mem'), perm)  13.4 us
    ppermute x14, waiting for transfers between devices, one(): return lax.ppermute(x, ('lon', 'mem'), perm)  5.38 us
    pallas_call x1, Pallas kernels, on_device(): pl.pallas_call(functools.partial(product_kernel, group), out_shape=jax.Sh...  3.33 us
  transfers between devices with their start and end apart: 14, of which 7 were waited for; matrix products, arithmetic and copies ran while one was open for 0% of the time, Pallas kernels for 0%

profile of v11, /device:TPU:0, one launch (start us, length us, event | category | flops | bytes accessed | tf_op | source)
XLA Modules:
  0.0 22.3 jit_solution(1793189391207756434)
XLA Ops:
  0.0 0.0 copy-start.2
  0.0 0.0 copy-start.1
  0.0 5.0 %collective-permute-start.2 = (f32[96,128]{1,0:T(8,128)}, f32[96,128]{1,0:T(8,128)S(1)}, u32[]{:S(2)}, u32[]{:S(2)}) collective-permute-start(f32[96,128]{1,0:T(8,128)} %bitcast.3), channel_id=1, source_target_pairs={{12,0},{13,1},{14,2},{15,3},{8,4},{9,5},{10,6},{11,7},{4,8},{5,9},... | collective-permute-start | bytes 147464 | tf_op jit(solution)/shard_map/ppermute | solution.py:143
  5.1 0.0 collective-permute-start.1
  5.1 0.6 %collective-permute-start = (f32[96,128]{1,0:T(8,128)}, f32[96,128]{1,0:T(8,128)S(1)}, u32[]{:S(2)}, u32[]{:S(2)}) collective-permute-start(f32[96,128]{1,0:T(8,128)} %bitcast.5), channel_id=1, source_target_pairs={{4,0},{5,1},{6,2},{7,3},{0,4},{1,5},{2,6},{3,7},{12,8},{13,9},{14,... | collective-permute-start | bytes 147464 | tf_op jit(solution)/shard_map/ppermute | solution.py:143
  5.7 0.0 copy-done.2
  5.7 2.6 %collective-permute-start.5 = (f32[1,96,128]{2,1,0:T(8,128)S(1)}, f32[1,96,128]{2,1,0:T(8,128)S(1)}, u32[]{:S(2)}, u32[]{:S(2)}) collective-permute-start(f32[1,96,128]{2,1,0:T(8,128)S(1)} %bitcast.6), channel_id=1, source_target_pairs={{18,0},{19,1},{16,2},{17,3},{22,4},{23,5},{20,6},{21,7},{26,8},{27... | collective-permute-start | bytes 147464 | tf_op jit(solution)/shard_map/ppermute | solution.py:143
  8.3 0.5 %collective-permute-start.3 = (f32[1,96,128]{2,1,0:T(8,128)S(1)}, f32[1,96,128]{2,1,0:T(8,128)S(1)}, u32[]{:S(2)}, u32[]{:S(2)}) collective-permute-start(f32[1,96,128]{2,1,0:T(8,128)S(1)} %bitcast.7), channel_id=1, source_target_pairs={{2,0},{3,1},{0,2},{1,3},{6,4},{7,5},{4,6},{5,7},{10,8},{11,9},{8,1... | collective-permute-start | bytes 147464 | tf_op jit(solution)/shard_map/ppermute | solution.py:143
  8.8 0.0 copy-done.1
  8.9 0.0 copy-start
  8.9 0.0 copy-start.3
  8.9 0.0 collective-permute-done.2.refs_2_
  8.9 0.5 %collective-permute-start.4 = (f32[2,96,128]{2,1,0:T(8,128)S(1)}, f32[2,96,128]{2,1,0:T(8,128)S(1)}, u32[]{:S(2)}, u32[]{:S(2)}) collective-permute-start(f32[2,96,128]{2,1,0:T(8,128)S(1)} %shard_map.47.pair_ref.refs_11_), channel_id=1, source_target_pairs={{16,0},{17,1},{18,2},{19,3},{20,4},{21,5},{22,6},{23,7},{24,8},{25... | collective-permute-start | bytes 294920 | tf_op jit(solution)/shard_map/ppermute | solution.py:143
  9.4 0.9 %collective-permute-done.1.refs_1_ = f32[96,128]{1,0:T(8,128)S(1)} collective-permute-done((f32[96,128]{1,0:T(8,128)}, f32[96,128]{1,0:T(8,128)S(1)}, u32[]{:S(2)}, u32[]{:S(2)}) %collective-permute-start.1) | collective-permute-done | bytes 49184 | tf_op jit(solution)/shard_map/ppermute | solution.py:143
  10.3 0.0 collective-permute-done.refs_0_
  10.3 2.5 %collective-permute-start.8 = (bf16[3,96,128]{2,1,0:T(8,128)(2,1)S(1)}, bf16[3,96,128]{2,1,0:T(8,128)(2,1)S(1)}, u32[]{:S(2)}, u32[]{:S(2)}) collective-permute-start(bf16[3,96,128]{2,1,0:T(8,128)(2,1)S(1)} %get-tuple-element.26), channel_id=1, source_target_pairs={{18,0},{19,1},{16,2},{17,3},{22,4},{23,5},{20,6},{21,7},{26,8},{27... | collective-permute-start | bytes 221192 | tf_op jit(solution)/shard_map/ppermute | solution.py:143
  12.8 0.5 %collective-permute-start.7 = (bf16[3,96,128]{2,1,0:T(8,128)(2,1)S(1)}, bf16[3,96,128]{2,1,0:T(8,128)(2,1)S(1)}, u32[]{:S(2)}, u32[]{:S(2)}) collective-permute-start(bf16[3,96,128]{2,1,0:T(8,128)(2,1)S(1)} %get-tuple-element.26), channel_id=1, source_target_pairs={{16,0},{17,1},{18,2},{19,3},{20,4},{21,5},{22,6},{23,7},{24,8},{25... | collective-permute-start | bytes 221192 | tf_op jit(solution)/shard_map/ppermute | solution.py:143
  13.3 0.0 collective-permute-done.5.diag_ref
  13.3 0.5 %collective-permute-start.6 = (bf16[3,96,128]{2,1,0:T(8,128)(2,1)S(1)}, bf16[3,96,128]{2,1,0:T(8,128)(2,1)S(1)}, u32[]{:S(2)}, u32[]{:S(2)}) collective-permute-start(bf16[3,96,128]{2,1,0:T(8,128)(2,1)S(1)} %get-tuple-element.26), channel_id=1, source_target_pairs={{2,0},{3,1},{0,2},{1,3},{6,4},{7,5},{4,6},{5,7},{10,8},{11,9},{8,1... | collective-permute-start | bytes 221192 | tf_op jit(solution)/shard_map/ppermute | solution.py:143
  13.8 0.0 collective-permute-done.3.x_ref
  13.8 0.8 %collective-permute-done.4.y_ref.refs_10_ = f32[2,96,128]{2,1,0:T(8,128)S(1)} collective-permute-done((f32[2,96,128]{2,1,0:T(8,128)S(1)}, f32[2,96,128]{2,1,0:T(8,128)S(1)}, u32[]{:S(2)}, u32[]{:S(2)}) %collective-permute-start.4) | collective-permute-done | bytes 98336 | tf_op jit(solution)/shard_map/ppermute | solution.py:143
  14.6 0.1 collective-permute-start.10
  14.7 0.5 %collective-permute-start.9 = (bf16[6,96,128]{2,1,0:T(8,128)(2,1)S(1)}, bf16[6,96,128]{2,1,0:T(8,128)(2,1)S(1)}, u32[]{:S(2)}, u32[]{:S(2)}) collective-permute-start(bf16[6,96,128]{2,1,0:T(8,128)(2,1)S(1)} %get-tuple-element.22.refs_0_), channel_id=1, source_target_pairs={{1,0},{0,1},{3,2},{2,3},{5,4},{4,5},{7,6},{6,7},{9,8},{8,9},{11,10... | collective-permute-start | bytes 442376 | tf_op jit(solution)/shard_map/ppermute | solution.py:143
  15.2 0.8 %collective-permute-done.8.refs_4_ = bf16[3,96,128]{2,1,0:T(8,128)(2,1)S(1)} collective-permute-done((bf16[3,96,128]{2,1,0:T(8,128)(2,1)S(1)}, bf16[3,96,128]{2,1,0:T(8,128)(2,1)S(1)}, u32[]{:S(2)}, u32[]{:S(2)}) %collective-permute-start.8) | collective-permute-done | bytes 73760 | tf_op jit(solution)/shard_map/ppermute | solution.py:143
  16.0 0.0 collective-permute-start.13
  16.0 1.1 %collective-permute-done.7.refs_3_ = bf16[3,96,128]{2,1,0:T(8,128)(2,1)S(1)} collective-permute-done((bf16[3,96,128]{2,1,0:T(8,128)(2,1)S(1)}, bf16[3,96,128]{2,1,0:T(8,128)(2,1)S(1)}, u32[]{:S(2)}, u32[]{:S(2)}) %collective-permute-start.7) | collective-permute-done | bytes 73760 | tf_op jit(solution)/shard_map/ppermute | solution.py:143
  17.2 0.0 collective-permute-start.12
  17.2 0.5 %collective-permute-done.6.refs_2_ = bf16[3,96,128]{2,1,0:T(8,128)(2,1)S(1)} collective-permute-done((bf16[3,96,128]{2,1,0:T(8,128)(2,1)S(1)}, bf16[3,96,128]{2,1,0:T(8,128)(2,1)S(1)}, u32[]{:S(2)}, u32[]{:S(2)}) %collective-permute-start.6) | collective-permute-done | bytes 73760 | tf_op jit(solution)/shard_map/ppermute | solution.py:143
  17.7 0.0 collective-permute-start.11
  17.7 0.0 collective-permute-done.13.refs_9_
  17.7 0.7 %collective-permute-done.12.refs_8_ = bf16[3,96,128]{2,1,0:T(8,128)(2,1)S(1)} collective-permute-done((bf16[3,96,128]{2,1,0:T(8,128)(2,1)S(1)}, bf16[3,96,128]{2,1,0:T(8,128)(2,1)S(1)}, u32[]{:S(2)}, u32[]{:S(2)}) %collective-permute-start.12) | collective-permute-done | bytes 73760 | tf_op jit(solution)/shard_map/ppermute | solution.py:143
  18.4 0.5 %collective-permute-done.11.refs_7_ = bf16[3,96,128]{2,1,0:T(8,128)(2,1)S(1)} collective-permute-done((bf16[3,96,128]{2,1,0:T(8,128)(2,1)S(1)}, bf16[3,96,128]{2,1,0:T(8,128)(2,1)S(1)}, u32[]{:S(2)}, u32[]{:S(2)}) %collective-permute-start.11) | collective-permute-done | bytes 73760 | tf_op jit(solution)/shard_map/ppermute | solution.py:143
  18.9 0.0 collective-permute-done.10.refs_6_
  18.9 0.0 collective-permute-done.9.refs_5_
  18.9 0.0 copy-done
  18.9 0.0 copy-done.3
  18.9 3.3 %shard_map.50 = f32[1,12288]{1,0:T(1,128)} custom-call(s32[7,24]{1,0:T(8,128)S(1)} %bitcast.9, bf16[6,96,128]{2,1,0:T(8,128)(2,1)S(1)} %get-tuple-element.22.refs_0_, f32[3,96,128]{2,1,0:T(8,128)S(1)} %shard_map.49.refs_1_, bf16[3,96,128]{2,1,0:T(8,128)(2,1)S(1)} %collective-permute-done.6.refs_2_, bf16[3,96,128]{2,1,0:T(8,128)(2,1)S(1)} %collective-permute-done.7.refs_3_, ...), custom_call_target="tpu_custom_call" | custom-call | tf_op jit(solution)/shard_map/pallas_call | solution.py:222
  (4 shorter events, 0.1 us)
Async XLA Ops:
  0.0 5.7 %copy-start.2 = (f32[1,12288]{1,0:T(1,128)S(1)}, f32[1,12288]{1,0:T(1,128)}, u32[]{:S(2)}) copy-start(f32[1,12288]{1,0:T(1,128)} %param.4) | copy-start | bytes 147460
  0.0 8.8 %copy-start.1 = (bf16[1,12288]{1,0:T(2,128)(2,1)S(1)}, bf16[1,12288]{1,0:T(2,128)(2,1)}, u32[]{:S(2)}) copy-start(bf16[1,12288]{1,0:T(2,128)(2,1)} %inc_ref.1) | copy-start | bytes 73732
  0.0 8.9 %collective-permute-start.2 = (f32[96,128]{1,0:T(8,128)}, f32[96,128]{1,0:T(8,128)S(1)}, u32[]{:S(2)}, u32[]{:S(2)}) collective-permute-start(f32[96,128]{1,0:T(8,128)} %bitcast.3), channel_id=1, source_target_pairs={{12,0},{13,1},{14,2},{15,3},{8,4},{9,5},{10,6},{11,7},{4,8},{5,9},... | collective-permute-start | bytes 147464 | tf_op jit(solution)/shard_map/ppermute | solution.py:143
  5.1 5.2 %collective-permute-start.1 = (f32[96,128]{1,0:T(8,128)}, f32[96,128]{1,0:T(8,128)S(1)}, u32[]{:S(2)}, u32[]{:S(2)}) collective-permute-start(f32[96,128]{1,0:T(8,128)} %bitcast.4), channel_id=1, source_target_pairs={{8,0},{9,1},{10,2},{11,3},{12,4},{13,5},{14,6},{15,7},{0,8},{1,9},... | collective-permute-start | bytes 147464 | tf_op jit(solution)/shard_map/ppermute | solution.py:143
  5.1 5.2 %collective-permute-start = (f32[96,128]{1,0:T(8,128)}, f32[96,128]{1,0:T(8,128)S(1)}, u32[]{:S(2)}, u32[]{:S(2)}) collective-permute-start(f32[96,128]{1,0:T(8,128)} %bitcast.5), channel_id=1, source_target_pairs={{4,0},{5,1},{6,2},{7,3},{0,4},{1,5},{2,6},{3,7},{12,8},{13,9},{14,... | collective-permute-start | bytes 147464 | tf_op jit(solution)/shard_map/ppermute | solution.py:143
  5.7 7.6 %collective-permute-start.5 = (f32[1,96,128]{2,1,0:T(8,128)S(1)}, f32[1,96,128]{2,1,0:T(8,128)S(1)}, u32[]{:S(2)}, u32[]{:S(2)}) collective-permute-start(f32[1,96,128]{2,1,0:T(8,128)S(1)} %bitcast.6), channel_id=1, source_target_pairs={{18,0},{19,1},{16,2},{17,3},{22,4},{23,5},{20,6},{21,7},{26,8},{27... | collective-permute-start | bytes 147464 | tf_op jit(solution)/shard_map/ppermute | solution.py:143
  8.3 5.6 %collective-permute-start.3 = (f32[1,96,128]{2,1,0:T(8,128)S(1)}, f32[1,96,128]{2,1,0:T(8,128)S(1)}, u32[]{:S(2)}, u32[]{:S(2)}) collective-permute-start(f32[1,96,128]{2,1,0:T(8,128)S(1)} %bitcast.7), channel_id=1, source_target_pairs={{2,0},{3,1},{0,2},{1,3},{6,4},{7,5},{4,6},{5,7},{10,8},{11,9},{8,1... | collective-permute-start | bytes 147464 | tf_op jit(solution)/shard_map/ppermute | solution.py:143
  8.9 10.1 %copy-start = (bf16[8,512,512]{2,1,0:T(8,128)(2,1)S(1)}, bf16[8,512,512]{2,1,0:T(8,128)(2,1)}, u32[]{:S(2)}) copy-start(bf16[8,512,512]{2,1,0:T(8,128)(2,1)} %refs_12_.1) | copy-start | bytes 12582916
  8.9 10.1 %copy-start.3 = (s32[24,7]{0,1:T(8,128)S(1)}, s32[24,7]{0,1:T(8,128)}, u32[]{:S(2)}) copy-start(s32[24,7]{0,1:T(8,128)} %param.6) | copy-start | bytes 2020
  8.9 5.7 %collective-permute-start.4 = (f32[2,96,128]{2,1,0:T(8,128)S(1)}, f32[2,96,128]{2,1,0:T(8,128)S(1)}, u32[]{:S(2)}, u32[]{:S(2)}) collective-permute-start(f32[2,96,128]{2,1,0:T(8,128)S(1)} %shard_map.47.pair_ref.refs_11_), channel_id=1, source_target_pairs={{16,0},{17,1},{18,2},{19,3},{20,4},{21,5},{22,6},{23,7},{24,8},{25... | collective-permute-start | bytes 294920 | tf_op jit(solution)/shard_map/ppermute | solution.py:143
  10.3 5.8 %collective-permute-start.8 = (bf16[3,96,128]{2,1,0:T(8,128)(2,1)S(1)}, bf16[3,96,128]{2,1,0:T(8,128)(2,1)S(1)}, u32[]{:S(2)}, u32[]{:S(2)}) collective-permute-start(bf16[3,96,128]{2,1,0:T(8,128)(2,1)S(1)} %get-tuple-element.26), channel_id=1, source_target_pairs={{18,0},{19,1},{16,2},{17,3},{22,4},{23,5},{20,6},{21,7},{26,8},{27... | collective-permute-start | bytes 221192 | tf_op jit(solution)/shard_map/ppermute | solution.py:143
  12.8 4.4 %collective-permute-start.7 = (bf16[3,96,128]{2,1,0:T(8,128)(2,1)S(1)}, bf16[3,96,128]{2,1,0:T(8,128)(2,1)S(1)}, u32[]{:S(2)}, u32[]{:S(2)}) collective-permute-start(bf16[3,96,128]{2,1,0:T(8,128)(2,1)S(1)} %get-tuple-element.26), channel_id=1, source_target_pairs={{16,0},{17,1},{18,2},{19,3},{20,4},{21,5},{22,6},{23,7},{24,8},{25... | collective-permute-start | bytes 221192 | tf_op jit(solution)/shard_map/ppermute | solution.py:143
  13.3 4.4 %collective-permute-start.6 = (bf16[3,96,128]{2,1,0:T(8,128)(2,1)S(1)}, bf16[3,96,128]{2,1,0:T(8,128)(2,1)S(1)}, u32[]{:S(2)}, u32[]{:S(2)}) collective-permute-start(bf16[3,96,128]{2,1,0:T(8,128)(2,1)S(1)} %get-tuple-element.26), channel_id=1, source_target_pairs={{2,0},{3,1},{0,2},{1,3},{6,4},{7,5},{4,6},{5,7},{10,8},{11,9},{8,1... | collective-permute-start | bytes 221192 | tf_op jit(solution)/shard_map/ppermute | solution.py:143
  14.6 4.3 %collective-permute-start.10 = (f32[3,96,128]{2,1,0:T(8,128)S(1)}, f32[3,96,128]{2,1,0:T(8,128)S(1)}, u32[]{:S(2)}, u32[]{:S(2)}) collective-permute-start(f32[3,96,128]{2,1,0:T(8,128)S(1)} %shard_map.49.refs_1_), channel_id=1, source_target_pairs={{1,0},{0,1},{3,2},{2,3},{5,4},{4,5},{7,6},{6,7},{9,8},{8,9},{11,10... | collective-permute-start | bytes 442376 | tf_op jit(solution)/shard_map/ppermute | solution.py:143
  14.7 4.2 %collective-permute-start.9 = (bf16[6,96,128]{2,1,0:T(8,128)(2,1)S(1)}, bf16[6,96,128]{2,1,0:T(8,128)(2,1)S(1)}, u32[]{:S(2)}, u32[]{:S(2)}) collective-permute-start(bf16[6,96,128]{2,1,0:T(8,128)(2,1)S(1)} %get-tuple-element.22.refs_0_), channel_id=1, source_target_pairs={{1,0},{0,1},{3,2},{2,3},{5,4},{4,5},{7,6},{6,7},{9,8},{8,9},{11,10... | collective-permute-start | bytes 442376 | tf_op jit(solution)/shard_map/ppermute | solution.py:143
  16.0 1.6 %collective-permute-start.13 = (bf16[3,96,128]{2,1,0:T(8,128)(2,1)S(1)}, bf16[3,96,128]{2,1,0:T(8,128)(2,1)S(1)}, u32[]{:S(2)}, u32[]{:S(2)}) collective-permute-start(bf16[3,96,128]{2,1,0:T(8,128)(2,1)S(1)} %collective-permute-done.8.refs_4_), channel_id=1, source_target_pairs={{1,0},{0,1},{3,2},{2,3},{5,4},{4,5},{7,6},{6,7},{9,8},{8,9},{11,10... | collective-permute-start | bytes 221192 | tf_op jit(solution)/shard_map/ppermute | solution.py:143
  17.2 1.3 %collective-permute-start.12 = (bf16[3,96,128]{2,1,0:T(8,128)(2,1)S(1)}, bf16[3,96,128]{2,1,0:T(8,128)(2,1)S(1)}, u32[]{:S(2)}, u32[]{:S(2)}) collective-permute-start(bf16[3,96,128]{2,1,0:T(8,128)(2,1)S(1)} %collective-permute-done.7.refs_3_), channel_id=1, source_target_pairs={{1,0},{0,1},{3,2},{2,3},{5,4},{4,5},{7,6},{6,7},{9,8},{8,9},{11,10... | collective-permute-start | bytes 221192 | tf_op jit(solution)/shard_map/ppermute | solution.py:143
  17.7 1.3 %collective-permute-start.11 = (bf16[3,96,128]{2,1,0:T(8,128)(2,1)S(1)}, bf16[3,96,128]{2,1,0:T(8,128)(2,1)S(1)}, u32[]{:S(2)}, u32[]{:S(2)}) collective-permute-start(bf16[3,96,128]{2,1,0:T(8,128)(2,1)S(1)} %collective-permute-done.6.refs_2_), channel_id=1, source_target_pairs={{1,0},{0,1},{3,2},{2,3},{5,4},{4,5},{7,6},{6,7},{9,8},{8,9},{11,10... | collective-permute-start | bytes 221192 | tf_op jit(solution)/shard_map/ppermute | solution.py:143

commit v12 on v10

v12 whole, which is shorter than its diff:
```python
import functools

import jax
import jax.numpy as jnp
from jax import lax
from jax.experimental import pallas as pl
from jax.experimental.pallas import tpu as pltpu
from jax.sharding import PartitionSpec as P

LANES = 128
SUB = 8
VMEM_LIMIT = 16 * 1024 * 1024
PACK_COST = 20_000_000_000
FIRST_COST = 2_000_000_000


def first_kernel(out_ref):
    out_ref[...] = jnp.zeros_like(out_ref)


def pair_kernel(first_ref, base_ref, inc_ref, pair_ref):
    pair_ref[0] = base_ref[...]
    for r in range(base_ref.shape[0]):
        part = inc_ref[:, r * LANES : (r + 1) * LANES]
        pair_ref[1, r : r + 1, :] = part.astype(jnp.float32)


def pack_kernel(pair_ref, *refs):
    line, diff_ref = refs[:-1], refs[-1]
    for j, ref in enumerate(line):
        diff_ref[j] = (ref[...] - pair_ref[0]).astype(jnp.bfloat16)


def bundle_kernel(base_ref, diff_ref, out_ref):
    base = base_ref[0]
    high = base.astype(jnp.bfloat16)
    rest = base - high.astype(jnp.float32)
    middle = rest.astype(jnp.bfloat16)
    out_ref[0] = high
    out_ref[1] = middle
    out_ref[2] = (rest - middle.astype(jnp.float32)).astype(jnp.bfloat16)
    for j in range(diff_ref.shape[0]):
        out_ref[3 + j] = diff_ref[j]


def weigh(lines, group, inc_ref, pert, products):
    members = 4 * group
    pitch = pert.shape[0] // members
    block_count, _, block_size = products.shape
    quarters = block_size // LANES
    for at in range(0, block_count * quarters, 2 * SUB):
        here = slice(at, at + 2 * SUB)
        starts, steps = [], []
        for ref in lines:
            parts = [ref[k, here, :].astype(jnp.float32) for k in range(group + 2)]
            starts.append(parts[0] + parts[1] + parts[2])
            steps.append(parts[3:])
        total = sum(step for line in steps for step in line) + group * sum(starts)
        mean = total * (1.0 / members)
        m = 0
        for start, line in zip(starts, steps):
            start = start - mean
            for value in [start] + [start + step for step in line]:
                pert[pl.ds(m * pitch + at, 2 * SUB), :] = value
                m += 1
    for i in range(block_count):
        for q in range(quarters):
            at = i * quarters + q
            part = pert[pl.ds(at, members, pitch), :] * inc_ref[1, at : at + 1, :]
            products[i, :, q * LANES : (q + 1) * LANES] = part.astype(jnp.bfloat16)


def product_kernel(group, off_ref, *refs):
    own, other, (inc_own, inc_other, tiles, out_ref) = refs[:4], refs[4:8], refs[8:12]
    pert, pert_other, picked_from, acc = refs[12:]
    slots, block_size, _ = tiles.shape
    block_count, members = picked_from.shape[0] // 2, picked_from.shape[1]
    pitch = pert.shape[0] // members
    quarters = block_size // LANES
    weigh(own, group, inc_own, pert, picked_from.at[pl.ds(0, block_count)])

    contract = (((1,), (1,)), ((), ()))
    vectors = block_count * members
    acc[...] = lax.dot_general(
        picked_from[0:block_count].reshape(vectors, block_size),
        tiles[0],
        contract,
        preferred_element_type=jnp.float32,
    )
    weigh(other, group, inc_other, pert_other, picked_from.at[pl.ds(block_count, block_count)])
    for s in range(1, slots):
        chosen = []
        for i in range(block_count):
            place = i + off_ref[s - 1, i]
            place = jnp.where(place < 0, place + 2 * block_count, place)
            chosen.append(picked_from[place])
        acc[...] += lax.dot_general(
            jnp.concatenate(chosen, axis=0),
            tiles[s],
            contract,
            preferred_element_type=jnp.float32,
        )

    scale = 1.0 / (members - 1)
    for i in range(block_count):
        for q in range(quarters):
            lanes = slice(q * LANES, (q + 1) * LANES)
            term = (
                pert[pl.ds(i * quarters + q, members, pitch), :]
                * acc[i * members : (i + 1) * members, lanes]
            )
            row = jnp.sum(term, axis=0, keepdims=True) * scale
            out_ref[:, i * block_size + q * LANES : i * block_size + (q + 1) * LANES] = row


def mover(lon_size, mem_size):
    def one(x, step, mem_of):
        perm = []
        for l in range(lon_size):
            for m in range(mem_size):
                source = ((l + step) % lon_size) * mem_size + mem_of(m)
                perm.append((source, l * mem_size + m))
        return lax.ppermute(x, ("lon", "mem"), perm)

    def move(x, across, mem_of):
        if not across:
            return one(x, 0, mem_of)
        if lon_size == 2:
            return one(x, 1, mem_of)
        axis = x.ndim - 2 if x.shape[-2] > 1 else x.ndim - 1
        right, left = jnp.split(x, 2, axis=axis)
        return jnp.concatenate([one(right, 1, mem_of), one(left, -1, mem_of)], axis=axis)

    return move


def on_device(ensemble, increments, offsets, taper):
    lon_size, mem_size = lax.axis_size("lon"), lax.axis_size("mem")
    group = mem_size // 4
    slots, block_size, _ = taper.shape
    block_count = offsets.shape[0]
    columns = ensemble.shape[1]
    rows = columns // LANES
    move = mover(lon_size, mem_size)
    same, beside = (lambda m: m), (lambda m: m ^ 2)

    base = ensemble.reshape(rows, LANES)
    if group & (group - 1):
        turn = lambda d: lambda m: (m + 4 * d) % mem_size
    else:
        turn = lambda d: lambda m: m ^ (4 * d)
    line = [move(base, False, turn(d)) for d in range(1, group)]
    whole = pl.BlockSpec(memory_space=pltpu.VMEM)
    small = pltpu.CompilerParams(vmem_limit_bytes=4 * 1024 * 1024)
    first = pl.pallas_call(
        first_kernel,
        out_shape=jax.ShapeDtypeStruct((SUB, LANES), jnp.float32),
        out_specs=whole,
        compiler_params=small,
        cost_estimate=pl.CostEstimate(flops=FIRST_COST, bytes_accessed=4096, transcendentals=0),
    )()
    pair = pl.pallas_call(
        pair_kernel,
        out_shape=jax.ShapeDtypeStruct((2, rows, LANES), jnp.float32),
        in_specs=[whole] * 3,
        out_specs=whole,
        compiler_params=small,
    )(first, base, increments)
    later, _ = lax.optimization_barrier((base, first))
    base_x = move(later[None], False, beside)
    base_diag = move(later[None], True, beside)
    base_y = move(pair, True, same)
    pair, line = lax.optimization_barrier((pair, line))

    diff = pl.pallas_call(
        pack_kernel,
        out_shape=jax.ShapeDtypeStruct((group - 1, rows, LANES), jnp.bfloat16),
        in_specs=[whole] * group,
        out_specs=whole,
        compiler_params=small,
        cost_estimate=pl.CostEstimate(
            flops=PACK_COST, bytes_accessed=8 * columns * 4, transcendentals=0
        ),
    )(pair, *line)
    x, y = move(diff, False, beside), move(diff, True, same)
    diag = move(diff, True, beside)
    bundle = pl.pallas_call(
        bundle_kernel,
        out_shape=jax.ShapeDtypeStruct((group + 2, rows, LANES), jnp.bfloat16),
        in_specs=[whole] * 2,
        out_specs=whole,
        compiler_params=small,
    )
    mine = bundle(pair, diff)
    mine, base_y, base_diag = lax.optimization_barrier((mine, base_y, base_diag))
    lines = [mine, bundle(base_x, x), bundle(base_y, y), bundle(base_diag, diag)]
    lines += [move(v, False, lambda m: m ^ 1) for v in lines]
    own, others = [lines[i] for i in (0, 1, 4, 5)], [lines[i] for i in (2, 3, 6, 7)]

    vectors = mem_size * block_count
    room = pltpu.CompilerParams(vmem_limit_bytes=VMEM_LIMIT)
    spread = pltpu.VMEM((mem_size * (rows + 1), LANES), jnp.float32)
    return pl.pallas_call(
        functools.partial(product_kernel, group),
        out_shape=jax.ShapeDtypeStruct((1, columns), jnp.float32),
        in_specs=[pl.BlockSpec(memory_space=pltpu.SMEM)] + [whole] * 11,
        out_specs=whole,
        scratch_shapes=[
            spread,
            spread,
            pltpu.VMEM((2 * block_count, mem_size, block_size), jnp.bfloat16),
            pltpu.VMEM((vectors, block_size), jnp.float32),
        ],
        compiler_params=room,
    )(offsets.T, *own, *others, pair, base_y, taper)


def solution(mesh):
    return jax.shard_map(
        on_device,
        mesh=mesh,
        in_specs=(P("mem", "lon"), P("mem", "lon"), P("lon", None), P()),
        out_specs=P("mem", "lon"),
        check_vma=False,
    )
```

time: 22.6 us -> 23.1 us (1.022)
  starting transfers between devices: 13.4 us -> 14.6 us
  waiting for transfers between devices: 5.38 us -> 4.79 us
    ppermute x14 -> x13, starting transfers between devices: 13.4 us -> 14.6 us  [one(): return lax.ppermute(x, ('lon', 'mem'), perm)]
    ppermute x14 -> x13, waiting for transfers between devices: 5.38 us -> 4.79 us  [one(): return lax.ppermute(x, ('lon', 'mem'), perm)]
  transfers between devices with their start and end apart: 14 -> 13, of which waited for: 7 -> 6; matrix products, arithmetic and copies ran while one was open for 0% -> 0% of each run, Pallas kernels for 0% -> 0%
where the time goes in v12:
time: 23.1 us; the launch traced here: 23 us
  starting transfers between devices  14.6 us (63%)
  waiting for transfers between devices  4.79 us (21%)
  Pallas kernels  3.45 us (15%)
    ppermute x13, starting transfers between devices, one(): return lax.ppermute(x, ('lon', 'mem'), perm)  14.6 us
    ppermute x13, waiting for transfers between devices, one(): return lax.ppermute(x, ('lon', 'mem'), perm)  4.79 us
    pallas_call x1, Pallas kernels, on_device(): pl.pallas_call(functools.partial(product_kernel, group), out_shape=jax.Sh...  3.35 us
  transfers between devices with their start and end apart: 13, of which 6 were waited for; matrix products, arithmetic and copies ran while one was open for 0% of the time, Pallas kernels for 0%

profile of v12, /device:TPU:0, one launch (start us, length us, event | category | flops | bytes accessed | tf_op | source)
XLA Modules:
  0.0 23.0 jit_solution(17533366887209473294)
XLA Ops:
  0.0 0.0 copy-start.2
  0.0 0.0 copy-start.1
  0.0 5.0 %collective-permute-start.2 = (f32[96,128]{1,0:T(8,128)}, f32[96,128]{1,0:T(8,128)S(1)}, u32[]{:S(2)}, u32[]{:S(2)}) collective-permute-start(f32[96,128]{1,0:T(8,128)} %bitcast.3), channel_id=1, source_target_pairs={{12,0},{13,1},{14,2},{15,3},{8,4},{9,5},{10,6},{11,7},{4,8},{5,9},... | collective-permute-start | bytes 147464 | tf_op jit(solution)/shard_map/ppermute | solution.py:123
  5.1 0.0 collective-permute-start.1
  5.1 0.6 %collective-permute-start = (f32[96,128]{1,0:T(8,128)}, f32[96,128]{1,0:T(8,128)S(1)}, u32[]{:S(2)}, u32[]{:S(2)}) collective-permute-start(f32[96,128]{1,0:T(8,128)} %bitcast.5), channel_id=1, source_target_pairs={{4,0},{5,1},{6,2},{7,3},{0,4},{1,5},{2,6},{3,7},{12,8},{13,9},{14,... | collective-permute-start | bytes 147464 | tf_op jit(solution)/shard_map/ppermute | solution.py:123
  5.7 0.0 copy-done.2
  5.7 2.6 %collective-permute-start.4 = (f32[1,96,128]{2,1,0:T(8,128)S(1)}, f32[1,96,128]{2,1,0:T(8,128)S(1)}, u32[]{:S(2)}, u32[]{:S(2)}) collective-permute-start(f32[1,96,128]{2,1,0:T(8,128)S(1)} %bitcast.6), channel_id=1, source_target_pairs={{18,0},{19,1},{16,2},{17,3},{22,4},{23,5},{20,6},{21,7},{26,8},{27... | collective-permute-start | bytes 147464 | tf_op jit(solution)/shard_map/ppermute | solution.py:123
  8.3 0.0 copy-done.1
  8.3 0.0 copy-start
  8.3 0.0 copy-start.3
  8.4 0.6 %collective-permute-start.3 = (f32[2,96,128]{2,1,0:T(8,128)S(1)}, f32[2,96,128]{2,1,0:T(8,128)S(1)}, u32[]{:S(2)}, u32[]{:S(2)}) collective-permute-start(f32[2,96,128]{2,1,0:T(8,128)S(1)} %shard_map.47.pair_ref.base_ref.refs_8_), channel_id=1, source_target_pairs={{16,0},{17,1},{18,2},{19,3},{20,4},{21,5},{22,6},{23,7},{24,8},{25... | collective-permute-start | bytes 294920 | tf_op jit(solution)/shard_map/ppermute | solution.py:123
  8.9 0.0 collective-permute-done.2.refs_2_
  8.9 1.3 %collective-permute-done.1.refs_1_ = f32[96,128]{1,0:T(8,128)S(1)} collective-permute-done((f32[96,128]{1,0:T(8,128)}, f32[96,128]{1,0:T(8,128)S(1)}, u32[]{:S(2)}, u32[]{:S(2)}) %collective-permute-start.1) | collective-permute-done | bytes 49184 | tf_op jit(solution)/shard_map/ppermute | solution.py:123
  10.3 0.0 collective-permute-done.refs_0_
  10.3 1.6 %collective-permute-start.9 = (bf16[3,96,128]{2,1,0:T(8,128)(2,1)S(1)}, bf16[3,96,128]{2,1,0:T(8,128)(2,1)S(1)}, u32[]{:S(2)}, u32[]{:S(2)}) collective-permute-start(bf16[3,96,128]{2,1,0:T(8,128)(2,1)S(1)} %shard_map.48.diff_ref), channel_id=1, source_target_pairs={{16,0},{17,1},{18,2},{19,3},{20,4},{21,5},{22,6},{23,7},{24,8},{25... | collective-permute-start | bytes 221192 | tf_op jit(solution)/shard_map/ppermute | solution.py:123
  11.9 1.4 %collective-permute-start.10 = (bf16[3,96,128]{2,1,0:T(8,128)(2,1)S(1)}, bf16[3,96,128]{2,1,0:T(8,128)(2,1)S(1)}, u32[]{:S(2)}, u32[]{:S(2)}) collective-permute-start(bf16[3,96,128]{2,1,0:T(8,128)(2,1)S(1)} %shard_map.48.diff_ref), channel_id=1, source_target_pairs={{18,0},{19,1},{16,2},{17,3},{22,4},{23,5},{20,6},{21,7},{26,8},{27... | collective-permute-start | bytes 221192 | tf_op jit(solution)/shard_map/ppermute | solution.py:123
  13.3 0.5 %collective-permute-start.6 = (bf16[3,96,128]{2,1,0:T(8,128)(2,1)S(1)}, bf16[3,96,128]{2,1,0:T(8,128)(2,1)S(1)}, u32[]{:S(2)}, u32[]{:S(2)}) collective-permute-start(bf16[3,96,128]{2,1,0:T(8,128)(2,1)S(1)} %shard_map.48.diff_ref), channel_id=1, source_target_pairs={{2,0},{3,1},{0,2},{1,3},{6,4},{7,5},{4,6},{5,7},{10,8},{11,9},{8,1... | collective-permute-start | bytes 221192 | tf_op jit(solution)/shard_map/ppermute | solution.py:123
  13.8 0.0 collective-permute-done.4.base_ref
  13.8 1.5 %collective-permute-start.5 = (f32[1,96,128]{2,1,0:T(8,128)S(1)}, f32[1,96,128]{2,1,0:T(8,128)S(1)}, u32[]{:S(2)}, u32[]{:S(2)}) collective-permute-start(f32[1,96,128]{2,1,0:T(8,128)S(1)} %bitcast.8), channel_id=1, source_target_pairs={{2,0},{3,1},{0,2},{1,3},{6,4},{7,5},{4,6},{5,7},{10,8},{11,9},{8,1... | collective-permute-start | bytes 147464 | tf_op jit(solution)/shard_map/ppermute | solution.py:123
  15.3 0.0 collective-permute-done.3.base_ref.refs_9_
  15.4 0.1 collective-permute-start.7
  15.4 0.1 collective-permute-done.9.diff_ref
  15.5 0.5 %collective-permute-start.11 = (bf16[6,96,128]{2,1,0:T(8,128)(2,1)S(1)}, bf16[6,96,128]{2,1,0:T(8,128)(2,1)S(1)}, u32[]{:S(2)}, u32[]{:S(2)}) collective-permute-start(bf16[6,96,128]{2,1,0:T(8,128)(2,1)S(1)} %shard_map.51.refs_4_), channel_id=1, source_target_pairs={{1,0},{0,1},{3,2},{2,3},{5,4},{4,5},{7,6},{6,7},{9,8},{8,9},{11,10... | collective-permute-start | bytes 442376 | tf_op jit(solution)/shard_map/ppermute | solution.py:123
  16.0 1.3 %collective-permute-done.10.diff_ref = bf16[3,96,128]{2,1,0:T(8,128)(2,1)S(1)} collective-permute-done((bf16[3,96,128]{2,1,0:T(8,128)(2,1)S(1)}, bf16[3,96,128]{2,1,0:T(8,128)(2,1)S(1)}, u32[]{:S(2)}, u32[]{:S(2)}) %collective-permute-start.10) | collective-permute-done | bytes 73760 | tf_op jit(solution)/shard_map/ppermute | solution.py:123
  17.4 0.1 collective-permute-start.12
  17.4 0.7 %collective-permute-done.5.base_ref = f32[1,96,128]{2,1,0:T(8,128)S(1)} collective-permute-done((f32[1,96,128]{2,1,0:T(8,128)S(1)}, f32[1,96,128]{2,1,0:T(8,128)S(1)}, u32[]{:S(2)}, u32[]{:S(2)}) %collective-permute-start.5) | collective-permute-done | bytes 49184 | tf_op jit(solution)/shard_map/ppermute | solution.py:123
  18.2 0.0 collective-permute-done.6.diff_ref
  18.2 0.1 collective-permute-start.8
  18.3 0.0 collective-permute-done.7.refs_2_
  18.3 0.0 collective-permute-done.11.refs_6_
  18.3 0.5 %collective-permute-done.12.refs_7_ = bf16[6,96,128]{2,1,0:T(8,128)(2,1)S(1)} collective-permute-done((bf16[6,96,128]{2,1,0:T(8,128)(2,1)S(1)}, bf16[6,96,128]{2,1,0:T(8,128)(2,1)S(1)}, u32[]{:S(2)}, u32[]{:S(2)}) %collective-permute-start.12) | collective-permute-done | bytes 147488 | tf_op jit(solution)/shard_map/ppermute | solution.py:123
  18.8 0.8 %collective-permute-done.8.refs_3_ = bf16[6,96,128]{2,1,0:T(8,128)(2,1)S(1)} collective-permute-done((bf16[6,96,128]{2,1,0:T(8,128)(2,1)S(1)}, bf16[6,96,128]{2,1,0:T(8,128)(2,1)S(1)}, u32[]{:S(2)}, u32[]{:S(2)}) %collective-permute-start.8) | collective-permute-done | bytes 147488 | tf_op jit(solution)/shard_map/ppermute | solution.py:123
  19.6 0.0 copy-done
  19.6 0.0 copy-done.3
  19.6 3.3 %shard_map.53 = f32[1,12288]{1,0:T(1,128)} custom-call(s32[7,24]{1,0:T(8,128)S(1)} %bitcast.9, bf16[6,96,128]{2,1,0:T(8,128)(2,1)S(1)} %shard_map.49.refs_0_, bf16[6,96,128]{2,1,0:T(8,128)(2,1)S(1)} %shard_map.50.refs_1_, bf16[6,96,128]{2,1,0:T(8,128)(2,1)S(1)} %collective-permute-done.7.refs_2_, bf16[6,96,128]{2,1,0:T(8,128)(2,1)S(1)} %collective-permute-done.8.refs_3_, ...), custom_call_target="tpu_custom_call" | custom-call | tf_op jit(solution)/shard_map/pallas_call | solution.py:203
  (7 shorter events, 0.1 us)
Async XLA Ops:
  0.0 5.7 %copy-start.2 = (f32[1,12288]{1,0:T(1,128)S(1)}, f32[1,12288]{1,0:T(1,128)}, u32[]{:S(2)}) copy-start(f32[1,12288]{1,0:T(1,128)} %param.4) | copy-start | bytes 147460
  0.0 8.3 %copy-start.1 = (bf16[1,12288]{1,0:T(2,128)(2,1)S(1)}, bf16[1,12288]{1,0:T(2,128)(2,1)}, u32[]{:S(2)}) copy-start(bf16[1,12288]{1,0:T(2,128)(2,1)} %inc_ref.1) | copy-start | bytes 73732
  0.0 8.9 %collective-permute-start.2 = (f32[96,128]{1,0:T(8,128)}, f32[96,128]{1,0:T(8,128)S(1)}, u32[]{:S(2)}, u32[]{:S(2)}) collective-permute-start(f32[96,128]{1,0:T(8,128)} %bitcast.3), channel_id=1, source_target_pairs={{12,0},{13,1},{14,2},{15,3},{8,4},{9,5},{10,6},{11,7},{4,8},{5,9},... | collective-permute-start | bytes 147464 | tf_op jit(solution)/shard_map/ppermute | solution.py:123
  5.1 5.2 %collective-permute-start.1 = (f32[96,128]{1,0:T(8,128)}, f32[96,128]{1,0:T(8,128)S(1)}, u32[]{:S(2)}, u32[]{:S(2)}) collective-permute-start(f32[96,128]{1,0:T(8,128)} %bitcast.4), channel_id=1, source_target_pairs={{8,0},{9,1},{10,2},{11,3},{12,4},{13,5},{14,6},{15,7},{0,8},{1,9},... | collective-permute-start | bytes 147464 | tf_op jit(solution)/shard_map/ppermute | solution.py:123
  5.1 5.2 %collective-permute-start = (f32[96,128]{1,0:T(8,128)}, f32[96,128]{1,0:T(8,128)S(1)}, u32[]{:S(2)}, u32[]{:S(2)}) collective-permute-start(f32[96,128]{1,0:T(8,128)} %bitcast.5), channel_id=1, source_target_pairs={{4,0},{5,1},{6,2},{7,3},{0,4},{1,5},{2,6},{3,7},{12,8},{13,9},{14,... | collective-permute-start | bytes 147464 | tf_op jit(solution)/shard_map/ppermute | solution.py:123
  5.7 8.1 %collective-permute-start.4 = (f32[1,96,128]{2,1,0:T(8,128)S(1)}, f32[1,96,128]{2,1,0:T(8,128)S(1)}, u32[]{:S(2)}, u32[]{:S(2)}) collective-permute-start(f32[1,96,128]{2,1,0:T(8,128)S(1)} %bitcast.6), channel_id=1, source_target_pairs={{18,0},{19,1},{16,2},{17,3},{22,4},{23,5},{20,6},{21,7},{26,8},{27... | collective-permute-start | bytes 147464 | tf_op jit(solution)/shard_map/ppermute | solution.py:123
  8.3 11.3 %copy-start = (bf16[8,512,512]{2,1,0:T(8,128)(2,1)S(1)}, bf16[8,512,512]{2,1,0:T(8,128)(2,1)}, u32[]{:S(2)}) copy-start(bf16[8,512,512]{2,1,0:T(8,128)(2,1)} %refs_10_.1) | copy-start | bytes 12582916
  8.3 11.3 %copy-start.3 = (s32[24,7]{0,1:T(8,128)S(1)}, s32[24,7]{0,1:T(8,128)}, u32[]{:S(2)}) copy-start(s32[24,7]{0,1:T(8,128)} %param.6) | copy-start | bytes 2020
  8.4 7.0 %collective-permute-start.3 = (f32[2,96,128]{2,1,0:T(8,128)S(1)}, f32[2,96,128]{2,1,0:T(8,128)S(1)}, u32[]{:S(2)}, u32[]{:S(2)}) collective-permute-start(f32[2,96,128]{2,1,0:T(8,128)S(1)} %shard_map.47.pair_ref.base_ref.refs_8_), channel_id=1, source_target_pairs={{16,0},{17,1},{18,2},{19,3},{20,4},{21,5},{22,6},{23,7},{24,8},{25... | collective-permute-start | bytes 294920 | tf_op jit(solution)/shard_map/ppermute | solution.py:123
  10.3 5.2 %collective-permute-start.9 = (bf16[3,96,128]{2,1,0:T(8,128)(2,1)S(1)}, bf16[3,96,128]{2,1,0:T(8,128)(2,1)S(1)}, u32[]{:S(2)}, u32[]{:S(2)}) collective-permute-start(bf16[3,96,128]{2,1,0:T(8,128)(2,1)S(1)} %shard_map.48.diff_ref), channel_id=1, source_target_pairs={{16,0},{17,1},{18,2},{19,3},{20,4},{21,5},{22,6},{23,7},{24,8},{25... | collective-permute-start | bytes 221192 | tf_op jit(solution)/shard_map/ppermute | solution.py:123
  11.9 5.5 %collective-permute-start.10 = (bf16[3,96,128]{2,1,0:T(8,128)(2,1)S(1)}, bf16[3,96,128]{2,1,0:T(8,128)(2,1)S(1)}, u32[]{:S(2)}, u32[]{:S(2)}) collective-permute-start(bf16[3,96,128]{2,1,0:T(8,128)(2,1)S(1)} %shard_map.48.diff_ref), channel_id=1, source_target_pairs={{18,0},{19,1},{16,2},{17,3},{22,4},{23,5},{20,6},{21,7},{26,8},{27... | collective-permute-start | bytes 221192 | tf_op jit(solution)/shard_map/ppermute | solution.py:123
  13.3 4.9 %collective-permute-start.6 = (bf16[3,96,128]{2,1,0:T(8,128)(2,1)S(1)}, bf16[3,96,128]{2,1,0:T(8,128)(2,1)S(1)}, u32[]{:S(2)}, u32[]{:S(2)}) collective-permute-start(bf16[3,96,128]{2,1,0:T(8,128)(2,1)S(1)} %shard_map.48.diff_ref), channel_id=1, source_target_pairs={{2,0},{3,1},{0,2},{1,3},{6,4},{7,5},{4,6},{5,7},{10,8},{11,9},{8,1... | collective-permute-start | bytes 221192 | tf_op jit(solution)/shard_map/ppermute | solution.py:123
  13.8 4.3 %collective-permute-start.5 = (f32[1,96,128]{2,1,0:T(8,128)S(1)}, f32[1,96,128]{2,1,0:T(8,128)S(1)}, u32[]{:S(2)}, u32[]{:S(2)}) collective-permute-start(f32[1,96,128]{2,1,0:T(8,128)S(1)} %bitcast.8), channel_id=1, source_target_pairs={{2,0},{3,1},{0,2},{1,3},{6,4},{7,5},{4,6},{5,7},{10,8},{11,9},{8,1... | collective-permute-start | bytes 147464 | tf_op jit(solution)/shard_map/ppermute | solution.py:123
  15.4 2.9 %collective-permute-start.7 = (bf16[6,96,128]{2,1,0:T(8,128)(2,1)S(1)}, bf16[6,96,128]{2,1,0:T(8,128)(2,1)S(1)}, u32[]{:S(2)}, u32[]{:S(2)}) collective-permute-start(bf16[6,96,128]{2,1,0:T(8,128)(2,1)S(1)} %shard_map.49.refs_0_), channel_id=1, source_target_pairs={{1,0},{0,1},{3,2},{2,3},{5,4},{4,5},{7,6},{6,7},{9,8},{8,9},{11,10... | collective-permute-start | bytes 442376 | tf_op jit(solution)/shard_map/ppermute | solution.py:123
  15.5 2.8 %collective-permute-start.11 = (bf16[6,96,128]{2,1,0:T(8,128)(2,1)S(1)}, bf16[6,96,128]{2,1,0:T(8,128)(2,1)S(1)}, u32[]{:S(2)}, u32[]{:S(2)}) collective-permute-start(bf16[6,96,128]{2,1,0:T(8,128)(2,1)S(1)} %shard_map.51.refs_4_), channel_id=1, source_target_pairs={{1,0},{0,1},{3,2},{2,3},{5,4},{4,5},{7,6},{6,7},{9,8},{8,9},{11,10... | collective-permute-start | bytes 442376 | tf_op jit(solution)/shard_map/ppermute | solution.py:123
  17.4 1.4 %collective-permute-start.12 = (bf16[6,96,128]{2,1,0:T(8,128)(2,1)S(1)}, bf16[6,96,128]{2,1,0:T(8,128)(2,1)S(1)}, u32[]{:S(2)}, u32[]{:S(2)}) collective-permute-start(bf16[6,96,128]{2,1,0:T(8,128)(2,1)S(1)} %shard_map.52.refs_5_), channel_id=1, source_target_pairs={{1,0},{0,1},{3,2},{2,3},{5,4},{4,5},{7,6},{6,7},{9,8},{8,9},{11,10... | collective-permute-start | bytes 442376 | tf_op jit(solution)/shard_map/ppermute | solution.py:123
  18.2 1.4 %collective-permute-start.8 = (bf16[6,96,128]{2,1,0:T(8,128)(2,1)S(1)}, bf16[6,96,128]{2,1,0:T(8,128)(2,1)S(1)}, u32[]{:S(2)}, u32[]{:S(2)}) collective-permute-start(bf16[6,96,128]{2,1,0:T(8,128)(2,1)S(1)} %shard_map.50.refs_1_), channel_id=1, source_target_pairs={{1,0},{0,1},{3,2},{2,3},{5,4},{4,5},{7,6},{6,7},{9,8},{8,9},{11,10... | collective-permute-start | bytes 442376 | tf_op jit(solution)/shard_map/ppermute | solution.py:123

commit v13 on v11

--- a/solution.py
+++ b/solution.py
@@ -108,15 +108,20 @@
         preferred_element_type=jnp.float32,
     )
     weigh(1, pert_other, lambda at: inc_other[1, at : at + 1, :])
-    for s in range(1, slots):
-        chosen = []
+
+    def chosen(s):
+        blocks = []
         for i in range(block_count):
             place = i + off_ref[s - 1, i]
             place = jnp.where(place < 0, place + 2 * block_count, place)
-            chosen.append(picked_from[place])
+            blocks.append(picked_from[place])
+        return jnp.concatenate(blocks, axis=0)
+
+    for s in range(1, slots, 2):
+        both = range(s, min(s + 2, slots))
         acc[...] += lax.dot_general(
-            jnp.concatenate(chosen, axis=0),
-            tiles[s],
+            jnp.concatenate([chosen(k) for k in both], axis=1),
+            jnp.concatenate([tiles[k] for k in both], axis=1),
             contract,
             preferred_element_type=jnp.float32,
         )

time: 22.4 us -> 22.4 us (level)
  no operation moved by 1% of the time
where the time goes in v13:
time: 22.4 us; the launch traced here: 22.3 us
  starting transfers between devices  13.4 us (60%)
  waiting for transfers between devices  5.38 us (24%)
  Pallas kernels  3.4 us (15%)
    ppermute x14, starting transfers between devices, one(): return lax.ppermute(x, ('lon', 'mem'), perm)  13.4 us
    ppermute x14, waiting for transfers between devices, one(): return lax.ppermute(x, ('lon', 'mem'), perm)  5.38 us
    pallas_call x1, Pallas kernels, on_device(): pl.pallas_call(functools.partial(product_kernel, group), out_shape=jax.Sh...  3.33 us
  transfers between devices with their start and end apart: 14, of which 7 were waited for; matrix products, arithmetic and copies ran while one was open for 0% of the time, Pallas kernels for 0%

profile of v13, /device:TPU:0, one launch (start us, length us, event | category | flops | bytes accessed | tf_op | source)
XLA Modules:
  0.0 22.3 jit_solution(1793189391207756434)
XLA Ops:
  0.0 0.0 copy-start.2
  0.0 0.0 copy-start.1
  0.0 5.0 %collective-permute-start.2 = (f32[96,128]{1,0:T(8,128)}, f32[96,128]{1,0:T(8,128)S(1)}, u32[]{:S(2)}, u32[]{:S(2)}) collective-permute-start(f32[96,128]{1,0:T(8,128)} %bitcast.3), channel_id=1, source_target_pairs={{12,0},{13,1},{14,2},{15,3},{8,4},{9,5},{10,6},{11,7},{4,8},{5,9},... | collective-permute-start | bytes 147464 | tf_op jit(solution)/shard_map/ppermute | solution.py:148
  5.1 0.0 collective-permute-start.1
  5.1 0.6 %collective-permute-start = (f32[96,128]{1,0:T(8,128)}, f32[96,128]{1,0:T(8,128)S(1)}, u32[]{:S(2)}, u32[]{:S(2)}) collective-permute-start(f32[96,128]{1,0:T(8,128)} %bitcast.5), channel_id=1, source_target_pairs={{4,0},{5,1},{6,2},{7,3},{0,4},{1,5},{2,6},{3,7},{12,8},{13,9},{14,... | collective-permute-start | bytes 147464 | tf_op jit(solution)/shard_map/ppermute | solution.py:148
  5.7 0.0 copy-done.2
  5.7 2.6 %collective-permute-start.5 = (f32[1,96,128]{2,1,0:T(8,128)S(1)}, f32[1,96,128]{2,1,0:T(8,128)S(1)}, u32[]{:S(2)}, u32[]{:S(2)}) collective-permute-start(f32[1,96,128]{2,1,0:T(8,128)S(1)} %bitcast.6), channel_id=1, source_target_pairs={{18,0},{19,1},{16,2},{17,3},{22,4},{23,5},{20,6},{21,7},{26,8},{27... | collective-permute-start | bytes 147464 | tf_op jit(solution)/shard_map/ppermute | solution.py:148
  8.3 0.5 %collective-permute-start.3 = (f32[1,96,128]{2,1,0:T(8,128)S(1)}, f32[1,96,128]{2,1,0:T(8,128)S(1)}, u32[]{:S(2)}, u32[]{:S(2)}) collective-permute-start(f32[1,96,128]{2,1,0:T(8,128)S(1)} %bitcast.7), channel_id=1, source_target_pairs={{2,0},{3,1},{0,2},{1,3},{6,4},{7,5},{4,6},{5,7},{10,8},{11,9},{8,1... | collective-permute-start | bytes 147464 | tf_op jit(solution)/shard_map/ppermute | solution.py:148
  8.8 0.0 copy-done.1
  8.9 0.0 copy-start
  8.9 0.0 copy-start.3
  8.9 0.0 collective-permute-done.2.refs_2_
  8.9 0.5 %collective-permute-start.4 = (f32[2,96,128]{2,1,0:T(8,128)S(1)}, f32[2,96,128]{2,1,0:T(8,128)S(1)}, u32[]{:S(2)}, u32[]{:S(2)}) collective-permute-start(f32[2,96,128]{2,1,0:T(8,128)S(1)} %shard_map.47.pair_ref.refs_11_), channel_id=1, source_target_pairs={{16,0},{17,1},{18,2},{19,3},{20,4},{21,5},{22,6},{23,7},{24,8},{25... | collective-permute-start | bytes 294920 | tf_op jit(solution)/shard_map/ppermute | solution.py:148
  9.4 0.9 %collective-permute-done.1.refs_1_ = f32[96,128]{1,0:T(8,128)S(1)} collective-permute-done((f32[96,128]{1,0:T(8,128)}, f32[96,128]{1,0:T(8,128)S(1)}, u32[]{:S(2)}, u32[]{:S(2)}) %collective-permute-start.1) | collective-permute-done | bytes 49184 | tf_op jit(solution)/shard_map/ppermute | solution.py:148
  10.3 0.0 collective-permute-done.refs_0_
  10.3 2.5 %collective-permute-start.8 = (bf16[3,96,128]{2,1,0:T(8,128)(2,1)S(1)}, bf16[3,96,128]{2,1,0:T(8,128)(2,1)S(1)}, u32[]{:S(2)}, u32[]{:S(2)}) collective-permute-start(bf16[3,96,128]{2,1,0:T(8,128)(2,1)S(1)} %get-tuple-element.26), channel_id=1, source_target_pairs={{18,0},{19,1},{16,2},{17,3},{22,4},{23,5},{20,6},{21,7},{26,8},{27... | collective-permute-start | bytes 221192 | tf_op jit(solution)/shard_map/ppermute | solution.py:148
  12.8 0.5 %collective-permute-start.7 = (bf16[3,96,128]{2,1,0:T(8,128)(2,1)S(1)}, bf16[3,96,128]{2,1,0:T(8,128)(2,1)S(1)}, u32[]{:S(2)}, u32[]{:S(2)}) collective-permute-start(bf16[3,96,128]{2,1,0:T(8,128)(2,1)S(1)} %get-tuple-element.26), channel_id=1, source_target_pairs={{16,0},{17,1},{18,2},{19,3},{20,4},{21,5},{22,6},{23,7},{24,8},{25... | collective-permute-start | bytes 221192 | tf_op jit(solution)/shard_map/ppermute | solution.py:148
  13.3 0.0 collective-permute-done.5.diag_ref
  13.3 0.5 %collective-permute-start.6 = (bf16[3,96,128]{2,1,0:T(8,128)(2,1)S(1)}, bf16[3,96,128]{2,1,0:T(8,128)(2,1)S(1)}, u32[]{:S(2)}, u32[]{:S(2)}) collective-permute-start(bf16[3,96,128]{2,1,0:T(8,128)(2,1)S(1)} %get-tuple-element.26), channel_id=1, source_target_pairs={{2,0},{3,1},{0,2},{1,3},{6,4},{7,5},{4,6},{5,7},{10,8},{11,9},{8,1... | collective-permute-start | bytes 221192 | tf_op jit(solution)/shard_map/ppermute | solution.py:148
  13.8 0.0 collective-permute-done.3.x_ref
  13.8 0.8 %collective-permute-done.4.y_ref.refs_10_ = f32[2,96,128]{2,1,0:T(8,128)S(1)} collective-permute-done((f32[2,96,128]{2,1,0:T(8,128)S(1)}, f32[2,96,128]{2,1,0:T(8,128)S(1)}, u32[]{:S(2)}, u32[]{:S(2)}) %collective-permute-start.4) | collective-permute-done | bytes 98336 | tf_op jit(solution)/shard_map/ppermute | solution.py:148
  14.6 0.1 collective-permute-start.10
  14.7 0.5 %collective-permute-start.9 = (bf16[6,96,128]{2,1,0:T(8,128)(2,1)S(1)}, bf16[6,96,128]{2,1,0:T(8,128)(2,1)S(1)}, u32[]{:S(2)}, u32[]{:S(2)}) collective-permute-start(bf16[6,96,128]{2,1,0:T(8,128)(2,1)S(1)} %get-tuple-element.22.refs_0_), channel_id=1, source_target_pairs={{1,0},{0,1},{3,2},{2,3},{5,4},{4,5},{7,6},{6,7},{9,8},{8,9},{11,10... | collective-permute-start | bytes 442376 | tf_op jit(solution)/shard_map/ppermute | solution.py:148
  15.2 0.8 %collective-permute-done.8.refs_4_ = bf16[3,96,128]{2,1,0:T(8,128)(2,1)S(1)} collective-permute-done((bf16[3,96,128]{2,1,0:T(8,128)(2,1)S(1)}, bf16[3,96,128]{2,1,0:T(8,128)(2,1)S(1)}, u32[]{:S(2)}, u32[]{:S(2)}) %collective-permute-start.8) | collective-permute-done | bytes 73760 | tf_op jit(solution)/shard_map/ppermute | solution.py:148
  16.0 0.0 collective-permute-start.13
  16.0 1.1 %collective-permute-done.7.refs_3_ = bf16[3,96,128]{2,1,0:T(8,128)(2,1)S(1)} collective-permute-done((bf16[3,96,128]{2,1,0:T(8,128)(2,1)S(1)}, bf16[3,96,128]{2,1,0:T(8,128)(2,1)S(1)}, u32[]{:S(2)}, u32[]{:S(2)}) %collective-permute-start.7) | collective-permute-done | bytes 73760 | tf_op jit(solution)/shard_map/ppermute | solution.py:148
  17.2 0.0 collective-permute-start.12
  17.2 0.5 %collective-permute-done.6.refs_2_ = bf16[3,96,128]{2,1,0:T(8,128)(2,1)S(1)} collective-permute-done((bf16[3,96,128]{2,1,0:T(8,128)(2,1)S(1)}, bf16[3,96,128]{2,1,0:T(8,128)(2,1)S(1)}, u32[]{:S(2)}, u32[]{:S(2)}) %collective-permute-start.6) | collective-permute-done | bytes 73760 | tf_op jit(solution)/shard_map/ppermute | solution.py:148
  17.7 0.0 collective-permute-start.11
  17.7 0.0 collective-permute-done.13.refs_9_
  17.7 0.7 %collective-permute-done.12.refs_8_ = bf16[3,96,128]{2,1,0:T(8,128)(2,1)S(1)} collective-permute-done((bf16[3,96,128]{2,1,0:T(8,128)(2,1)S(1)}, bf16[3,96,128]{2,1,0:T(8,128)(2,1)S(1)}, u32[]{:S(2)}, u32[]{:S(2)}) %collective-permute-start.12) | collective-permute-done | bytes 73760 | tf_op jit(solution)/shard_map/ppermute | solution.py:148
  18.4 0.5 %collective-permute-done.11.refs_7_ = bf16[3,96,128]{2,1,0:T(8,128)(2,1)S(1)} collective-permute-done((bf16[3,96,128]{2,1,0:T(8,128)(2,1)S(1)}, bf16[3,96,128]{2,1,0:T(8,128)(2,1)S(1)}, u32[]{:S(2)}, u32[]{:S(2)}) %collective-permute-start.11) | collective-permute-done | bytes 73760 | tf_op jit(solution)/shard_map/ppermute | solution.py:148
  18.9 0.0 collective-permute-done.10.refs_6_
  18.9 0.0 collective-permute-done.9.refs_5_
  18.9 0.0 copy-done
  18.9 0.0 copy-done.3
  18.9 3.3 %shard_map.50 = f32[1,12288]{1,0:T(1,128)} custom-call(s32[7,24]{1,0:T(8,128)S(1)} %bitcast.9, bf16[6,96,128]{2,1,0:T(8,128)(2,1)S(1)} %get-tuple-element.22.refs_0_, f32[3,96,128]{2,1,0:T(8,128)S(1)} %shard_map.49.refs_1_, bf16[3,96,128]{2,1,0:T(8,128)(2,1)S(1)} %collective-permute-done.6.refs_2_, bf16[3,96,128]{2,1,0:T(8,128)(2,1)S(1)} %collective-permute-done.7.refs_3_, ...), custom_call_target="tpu_custom_call" | custom-call | tf_op jit(solution)/shard_map/pallas_call | solution.py:227
  (4 shorter events, 0.1 us)
Async XLA Ops:
  0.0 5.7 %copy-start.2 = (f32[1,12288]{1,0:T(1,128)S(1)}, f32[1,12288]{1,0:T(1,128)}, u32[]{:S(2)}) copy-start(f32[1,12288]{1,0:T(1,128)} %param.4) | copy-start | bytes 147460
  0.0 8.8 %copy-start.1 = (bf16[1,12288]{1,0:T(2,128)(2,1)S(1)}, bf16[1,12288]{1,0:T(2,128)(2,1)}, u32[]{:S(2)}) copy-start(bf16[1,12288]{1,0:T(2,128)(2,1)} %inc_ref.1) | copy-start | bytes 73732
  0.0 8.9 %collective-permute-start.2 = (f32[96,128]{1,0:T(8,128)}, f32[96,128]{1,0:T(8,128)S(1)}, u32[]{:S(2)}, u32[]{:S(2)}) collective-permute-start(f32[96,128]{1,0:T(8,128)} %bitcast.3), channel_id=1, source_target_pairs={{12,0},{13,1},{14,2},{15,3},{8,4},{9,5},{10,6},{11,7},{4,8},{5,9},... | collective-permute-start | bytes 147464 | tf_op jit(solution)/shard_map/ppermute | solution.py:148
  5.1 5.2 %collective-permute-start.1 = (f32[96,128]{1,0:T(8,128)}, f32[96,128]{1,0:T(8,128)S(1)}, u32[]{:S(2)}, u32[]{:S(2)}) collective-permute-start(f32[96,128]{1,0:T(8,128)} %bitcast.4), channel_id=1, source_target_pairs={{8,0},{9,1},{10,2},{11,3},{12,4},{13,5},{14,6},{15,7},{0,8},{1,9},... | collective-permute-start | bytes 147464 | tf_op jit(solution)/shard_map/ppermute | solution.py:148
  5.1 5.2 %collective-permute-start = (f32[96,128]{1,0:T(8,128)}, f32[96,128]{1,0:T(8,128)S(1)}, u32[]{:S(2)}, u32[]{:S(2)}) collective-permute-start(f32[96,128]{1,0:T(8,128)} %bitcast.5), channel_id=1, source_target_pairs={{4,0},{5,1},{6,2},{7,3},{0,4},{1,5},{2,6},{3,7},{12,8},{13,9},{14,... | collective-permute-start | bytes 147464 | tf_op jit(solution)/shard_map/ppermute | solution.py:148
  5.7 7.6 %collective-permute-start.5 = (f32[1,96,128]{2,1,0:T(8,128)S(1)}, f32[1,96,128]{2,1,0:T(8,128)S(1)}, u32[]{:S(2)}, u32[]{:S(2)}) collective-permute-start(f32[1,96,128]{2,1,0:T(8,128)S(1)} %bitcast.6), channel_id=1, source_target_pairs={{18,0},{19,1},{16,2},{17,3},{22,4},{23,5},{20,6},{21,7},{26,8},{27... | collective-permute-start | bytes 147464 | tf_op jit(solution)/shard_map/ppermute | solution.py:148
  8.3 5.6 %collective-permute-start.3 = (f32[1,96,128]{2,1,0:T(8,128)S(1)}, f32[1,96,128]{2,1,0:T(8,128)S(1)}, u32[]{:S(2)}, u32[]{:S(2)}) collective-permute-start(f32[1,96,128]{2,1,0:T(8,128)S(1)} %bitcast.7), channel_id=1, source_target_pairs={{2,0},{3,1},{0,2},{1,3},{6,4},{7,5},{4,6},{5,7},{10,8},{11,9},{8,1... | collective-permute-start | bytes 147464 | tf_op jit(solution)/shard_map/ppermute | solution.py:148
  8.9 10.1 %copy-start = (bf16[8,512,512]{2,1,0:T(8,128)(2,1)S(1)}, bf16[8,512,512]{2,1,0:T(8,128)(2,1)}, u32[]{:S(2)}) copy-start(bf16[8,512,512]{2,1,0:T(8,128)(2,1)} %refs_12_.1) | copy-start | bytes 12582916
  8.9 10.1 %copy-start.3 = (s32[24,7]{0,1:T(8,128)S(1)}, s32[24,7]{0,1:T(8,128)}, u32[]{:S(2)}) copy-start(s32[24,7]{0,1:T(8,128)} %param.6) | copy-start | bytes 2020
  8.9 5.7 %collective-permute-start.4 = (f32[2,96,128]{2,1,0:T(8,128)S(1)}, f32[2,96,128]{2,1,0:T(8,128)S(1)}, u32[]{:S(2)}, u32[]{:S(2)}) collective-permute-start(f32[2,96,128]{2,1,0:T(8,128)S(1)} %shard_map.47.pair_ref.refs_11_), channel_id=1, source_target_pairs={{16,0},{17,1},{18,2},{19,3},{20,4},{21,5},{22,6},{23,7},{24,8},{25... | collective-permute-start | bytes 294920 | tf_op jit(solution)/shard_map/ppermute | solution.py:148
  10.3 5.8 %collective-permute-start.8 = (bf16[3,96,128]{2,1,0:T(8,128)(2,1)S(1)}, bf16[3,96,128]{2,1,0:T(8,128)(2,1)S(1)}, u32[]{:S(2)}, u32[]{:S(2)}) collective-permute-start(bf16[3,96,128]{2,1,0:T(8,128)(2,1)S(1)} %get-tuple-element.26), channel_id=1, source_target_pairs={{18,0},{19,1},{16,2},{17,3},{22,4},{23,5},{20,6},{21,7},{26,8},{27... | collective-permute-start | bytes 221192 | tf_op jit(solution)/shard_map/ppermute | solution.py:148
  12.8 4.4 %collective-permute-start.7 = (bf16[3,96,128]{2,1,0:T(8,128)(2,1)S(1)}, bf16[3,96,128]{2,1,0:T(8,128)(2,1)S(1)}, u32[]{:S(2)}, u32[]{:S(2)}) collective-permute-start(bf16[3,96,128]{2,1,0:T(8,128)(2,1)S(1)} %get-tuple-element.26), channel_id=1, source_target_pairs={{16,0},{17,1},{18,2},{19,3},{20,4},{21,5},{22,6},{23,7},{24,8},{25... | collective-permute-start | bytes 221192 | tf_op jit(solution)/shard_map/ppermute | solution.py:148
  13.3 4.4 %collective-permute-start.6 = (bf16[3,96,128]{2,1,0:T(8,128)(2,1)S(1)}, bf16[3,96,128]{2,1,0:T(8,128)(2,1)S(1)}, u32[]{:S(2)}, u32[]{:S(2)}) collective-permute-start(bf16[3,96,128]{2,1,0:T(8,128)(2,1)S(1)} %get-tuple-element.26), channel_id=1, source_target_pairs={{2,0},{3,1},{0,2},{1,3},{6,4},{7,5},{4,6},{5,7},{10,8},{11,9},{8,1... | collective-permute-start | bytes 221192 | tf_op jit(solution)/shard_map/ppermute | solution.py:148
  14.6 4.3 %collective-permute-start.10 = (f32[3,96,128]{2,1,0:T(8,128)S(1)}, f32[3,96,128]{2,1,0:T(8,128)S(1)}, u32[]{:S(2)}, u32[]{:S(2)}) collective-permute-start(f32[3,96,128]{2,1,0:T(8,128)S(1)} %shard_map.49.refs_1_), channel_id=1, source_target_pairs={{1,0},{0,1},{3,2},{2,3},{5,4},{4,5},{7,6},{6,7},{9,8},{8,9},{11,10... | collective-permute-start | bytes 442376 | tf_op jit(solution)/shard_map/ppermute | solution.py:148
  14.7 4.2 %collective-permute-start.9 = (bf16[6,96,128]{2,1,0:T(8,128)(2,1)S(1)}, bf16[6,96,128]{2,1,0:T(8,128)(2,1)S(1)}, u32[]{:S(2)}, u32[]{:S(2)}) collective-permute-start(bf16[6,96,128]{2,1,0:T(8,128)(2,1)S(1)} %get-tuple-element.22.refs_0_), channel_id=1, source_target_pairs={{1,0},{0,1},{3,2},{2,3},{5,4},{4,5},{7,6},{6,7},{9,8},{8,9},{11,10... | collective-permute-start | bytes 442376 | tf_op jit(solution)/shard_map/ppermute | solution.py:148
  16.0 1.6 %collective-permute-start.13 = (bf16[3,96,128]{2,1,0:T(8,128)(2,1)S(1)}, bf16[3,96,128]{2,1,0:T(8,128)(2,1)S(1)}, u32[]{:S(2)}, u32[]{:S(2)}) collective-permute-start(bf16[3,96,128]{2,1,0:T(8,128)(2,1)S(1)} %collective-permute-done.8.refs_4_), channel_id=1, source_target_pairs={{1,0},{0,1},{3,2},{2,3},{5,4},{4,5},{7,6},{6,7},{9,8},{8,9},{11,10... | collective-permute-start | bytes 221192 | tf_op jit(solution)/shard_map/ppermute | solution.py:148
  17.2 1.3 %collective-permute-start.12 = (bf16[3,96,128]{2,1,0:T(8,128)(2,1)S(1)}, bf16[3,96,128]{2,1,0:T(8,128)(2,1)S(1)}, u32[]{:S(2)}, u32[]{:S(2)}) collective-permute-start(bf16[3,96,128]{2,1,0:T(8,128)(2,1)S(1)} %collective-permute-done.7.refs_3_), channel_id=1, source_target_pairs={{1,0},{0,1},{3,2},{2,3},{5,4},{4,5},{7,6},{6,7},{9,8},{8,9},{11,10... | collective-permute-start | bytes 221192 | tf_op jit(solution)/shard_map/ppermute | solution.py:148
  17.7 1.3 %collective-permute-start.11 = (bf16[3,96,128]{2,1,0:T(8,128)(2,1)S(1)}, bf16[3,96,128]{2,1,0:T(8,128)(2,1)S(1)}, u32[]{:S(2)}, u32[]{:S(2)}) collective-permute-start(bf16[3,96,128]{2,1,0:T(8,128)(2,1)S(1)} %collective-permute-done.6.refs_2_), channel_id=1, source_target_pairs={{1,0},{0,1},{3,2},{2,3},{5,4},{4,5},{7,6},{6,7},{9,8},{8,9},{11,10... | collective-permute-start | bytes 221192 | tf_op jit(solution)/shard_map/ppermute | solution.py:148

commit v14 on v13

--- a/solution.py
+++ b/solution.py
@@ -212,7 +212,7 @@
     )(pair, *line)
     x, y = move(diff, False, beside), move(diff, True, same)
     diag = move(diff, True, beside)
-    mine, base_x, base_y, base_diag = lax.optimization_barrier((mine, base_x, base_y, base_diag))
+    _, base_x, base_y, base_diag = lax.optimization_barrier((mine, base_x, base_y, base_diag))
     bases = pl.pallas_call(
         bases_kernel,
         out_shape=jax.ShapeDtypeStruct((3, rows, LANES), jnp.float32),

time: 22.4 us -> 22.4 us (level)
  starting transfers between devices: 13.4 us -> 12.9 us
  waiting for transfers between devices: 5.38 us -> 5.87 us
    ppermute x14, starting transfers between devices: 13.4 us -> 12.9 us  [one(): return lax.ppermute(x, ('lon', 'mem'), perm)]
    ppermute x14, waiting for transfers between devices: 5.38 us -> 5.87 us  [one(): return lax.ppermute(x, ('lon', 'mem'), perm)]
where the time goes in v14:
time: 22.4 us; the launch traced here: 22.3 us
  starting transfers between devices  12.9 us (58%)
  waiting for transfers between devices  5.87 us (26%)
  Pallas kernels  3.4 us (15%)
    ppermute x14, starting transfers between devices, one(): return lax.ppermute(x, ('lon', 'mem'), perm)  12.9 us
    ppermute x14, waiting for transfers between devices, one(): return lax.ppermute(x, ('lon', 'mem'), perm)  5.87 us
    pallas_call x1, Pallas kernels, on_device(): pl.pallas_call(functools.partial(product_kernel, group), out_shape=jax.Sh...  3.32 us
  transfers between devices with their start and end apart: 14, of which 7 were waited for; matrix products, arithmetic and copies ran while one was open for 0% of the time, Pallas kernels for 0%

profile of v14, /device:TPU:0, one launch (start us, length us, event | category | flops | bytes accessed | tf_op | source)
XLA Modules:
  0.0 22.3 jit_solution(4461730965546011519)
XLA Ops:
  0.0 0.0 copy-start.2
  0.0 0.0 copy-start.1
  0.0 5.0 %collective-permute-start.2 = (f32[96,128]{1,0:T(8,128)}, f32[96,128]{1,0:T(8,128)S(1)}, u32[]{:S(2)}, u32[]{:S(2)}) collective-permute-start(f32[96,128]{1,0:T(8,128)} %bitcast.3), channel_id=1, source_target_pairs={{12,0},{13,1},{14,2},{15,3},{8,4},{9,5},{10,6},{11,7},{4,8},{5,9},... | collective-permute-start | bytes 147464 | tf_op jit(solution)/shard_map/ppermute | solution.py:148
  5.1 0.0 collective-permute-start.1
  5.1 0.6 %collective-permute-start = (f32[96,128]{1,0:T(8,128)}, f32[96,128]{1,0:T(8,128)S(1)}, u32[]{:S(2)}, u32[]{:S(2)}) collective-permute-start(f32[96,128]{1,0:T(8,128)} %bitcast.5), channel_id=1, source_target_pairs={{4,0},{5,1},{6,2},{7,3},{0,4},{1,5},{2,6},{3,7},{12,8},{13,9},{14,... | collective-permute-start | bytes 147464 | tf_op jit(solution)/shard_map/ppermute | solution.py:148
  5.7 0.0 copy-done.2
  5.7 2.6 %collective-permute-start.5 = (f32[1,96,128]{2,1,0:T(8,128)S(1)}, f32[1,96,128]{2,1,0:T(8,128)S(1)}, u32[]{:S(2)}, u32[]{:S(2)}) collective-permute-start(f32[1,96,128]{2,1,0:T(8,128)S(1)} %bitcast.6), channel_id=1, source_target_pairs={{18,0},{19,1},{16,2},{17,3},{22,4},{23,5},{20,6},{21,7},{26,8},{27... | collective-permute-start | bytes 147464 | tf_op jit(solution)/shard_map/ppermute | solution.py:148
  8.3 0.5 %collective-permute-start.3 = (f32[1,96,128]{2,1,0:T(8,128)S(1)}, f32[1,96,128]{2,1,0:T(8,128)S(1)}, u32[]{:S(2)}, u32[]{:S(2)}) collective-permute-start(f32[1,96,128]{2,1,0:T(8,128)S(1)} %bitcast.7), channel_id=1, source_target_pairs={{2,0},{3,1},{0,2},{1,3},{6,4},{7,5},{4,6},{5,7},{10,8},{11,9},{8,1... | collective-permute-start | bytes 147464 | tf_op jit(solution)/shard_map/ppermute | solution.py:148
  8.8 0.0 copy-done.1
  8.9 0.0 copy-start
  8.9 0.0 copy-start.3
  8.9 0.0 collective-permute-done.2.refs_2_
  8.9 0.5 %collective-permute-start.4 = (f32[2,96,128]{2,1,0:T(8,128)S(1)}, f32[2,96,128]{2,1,0:T(8,128)S(1)}, u32[]{:S(2)}, u32[]{:S(2)}) collective-permute-start(f32[2,96,128]{2,1,0:T(8,128)S(1)} %shard_map.47.pair_ref.refs_11_), channel_id=1, source_target_pairs={{16,0},{17,1},{18,2},{19,3},{20,4},{21,5},{22,6},{23,7},{24,8},{25... | collective-permute-start | bytes 294920 | tf_op jit(solution)/shard_map/ppermute | solution.py:148
  9.4 0.9 %collective-permute-done.1.refs_1_ = f32[96,128]{1,0:T(8,128)S(1)} collective-permute-done((f32[96,128]{1,0:T(8,128)}, f32[96,128]{1,0:T(8,128)S(1)}, u32[]{:S(2)}, u32[]{:S(2)}) %collective-permute-start.1) | collective-permute-done | bytes 49184 | tf_op jit(solution)/shard_map/ppermute | solution.py:148
  10.3 0.0 collective-permute-done.refs_0_
  10.3 2.5 %collective-permute-start.8 = (bf16[3,96,128]{2,1,0:T(8,128)(2,1)S(1)}, bf16[3,96,128]{2,1,0:T(8,128)(2,1)S(1)}, u32[]{:S(2)}, u32[]{:S(2)}) collective-permute-start(bf16[3,96,128]{2,1,0:T(8,128)(2,1)S(1)} %get-tuple-element.24), channel_id=1, source_target_pairs={{18,0},{19,1},{16,2},{17,3},{22,4},{23,5},{20,6},{21,7},{26,8},{27... | collective-permute-start | bytes 221192 | tf_op jit(solution)/shard_map/ppermute | solution.py:148
  12.8 0.5 %collective-permute-start.7 = (bf16[3,96,128]{2,1,0:T(8,128)(2,1)S(1)}, bf16[3,96,128]{2,1,0:T(8,128)(2,1)S(1)}, u32[]{:S(2)}, u32[]{:S(2)}) collective-permute-start(bf16[3,96,128]{2,1,0:T(8,128)(2,1)S(1)} %get-tuple-element.24), channel_id=1, source_target_pairs={{16,0},{17,1},{18,2},{19,3},{20,4},{21,5},{22,6},{23,7},{24,8},{25... | collective-permute-start | bytes 221192 | tf_op jit(solution)/shard_map/ppermute | solution.py:148
  13.3 0.0 collective-permute-done.5.diag_ref
  13.3 0.5 %collective-permute-start.6 = (bf16[3,96,128]{2,1,0:T(8,128)(2,1)S(1)}, bf16[3,96,128]{2,1,0:T(8,128)(2,1)S(1)}, u32[]{:S(2)}, u32[]{:S(2)}) collective-permute-start(bf16[3,96,128]{2,1,0:T(8,128)(2,1)S(1)} %get-tuple-element.24), channel_id=1, source_target_pairs={{2,0},{3,1},{0,2},{1,3},{6,4},{7,5},{4,6},{5,7},{10,8},{11,9},{8,1... | collective-permute-start | bytes 221192 | tf_op jit(solution)/shard_map/ppermute | solution.py:148
  13.8 0.0 collective-permute-done.3.x_ref
  13.8 0.0 collective-permute-start.9
  13.8 0.8 %collective-permute-done.4.y_ref.refs_10_ = f32[2,96,128]{2,1,0:T(8,128)S(1)} collective-permute-done((f32[2,96,128]{2,1,0:T(8,128)S(1)}, f32[2,96,128]{2,1,0:T(8,128)S(1)}, u32[]{:S(2)}, u32[]{:S(2)}) %collective-permute-start.4) | collective-permute-done | bytes 98336 | tf_op jit(solution)/shard_map/ppermute | solution.py:148
  14.6 0.1 collective-permute-start.10
  14.7 1.3 %collective-permute-done.8.refs_4_ = bf16[3,96,128]{2,1,0:T(8,128)(2,1)S(1)} collective-permute-done((bf16[3,96,128]{2,1,0:T(8,128)(2,1)S(1)}, bf16[3,96,128]{2,1,0:T(8,128)(2,1)S(1)}, u32[]{:S(2)}, u32[]{:S(2)}) %collective-permute-start.8) | collective-permute-done | bytes 73760 | tf_op jit(solution)/shard_map/ppermute | solution.py:148
  16.0 0.0 collective-permute-start.13
  16.0 1.1 %collective-permute-done.7.refs_3_ = bf16[3,96,128]{2,1,0:T(8,128)(2,1)S(1)} collective-permute-done((bf16[3,96,128]{2,1,0:T(8,128)(2,1)S(1)}, bf16[3,96,128]{2,1,0:T(8,128)(2,1)S(1)}, u32[]{:S(2)}, u32[]{:S(2)}) %collective-permute-start.7) | collective-permute-done | bytes 73760 | tf_op jit(solution)/shard_map/ppermute | solution.py:148
  17.2 0.0 collective-permute-start.12
  17.2 0.5 %collective-permute-done.6.refs_2_ = bf16[3,96,128]{2,1,0:T(8,128)(2,1)S(1)} collective-permute-done((bf16[3,96,128]{2,1,0:T(8,128)(2,1)S(1)}, bf16[3,96,128]{2,1,0:T(8,128)(2,1)S(1)}, u32[]{:S(2)}, u32[]{:S(2)}) %collective-permute-start.6) | collective-permute-done | bytes 73760 | tf_op jit(solution)/shard_map/ppermute | solution.py:148
  17.7 0.0 collective-permute-start.11
  17.7 0.0 collective-permute-done.9.refs_5_
  17.7 0.0 collective-permute-done.13.refs_9_
  17.7 0.7 %collective-permute-done.12.refs_8_ = bf16[3,96,128]{2,1,0:T(8,128)(2,1)S(1)} collective-permute-done((bf16[3,96,128]{2,1,0:T(8,128)(2,1)S(1)}, bf16[3,96,128]{2,1,0:T(8,128)(2,1)S(1)}, u32[]{:S(2)}, u32[]{:S(2)}) %collective-permute-start.12) | collective-permute-done | bytes 73760 | tf_op jit(solution)/shard_map/ppermute | solution.py:148
  18.4 0.5 %collective-permute-done.11.refs_7_ = bf16[3,96,128]{2,1,0:T(8,128)(2,1)S(1)} collective-permute-done((bf16[3,96,128]{2,1,0:T(8,128)(2,1)S(1)}, bf16[3,96,128]{2,1,0:T(8,128)(2,1)S(1)}, u32[]{:S(2)}, u32[]{:S(2)}) %collective-permute-start.11) | collective-permute-done | bytes 73760 | tf_op jit(solution)/shard_map/ppermute | solution.py:148
  18.9 0.0 collective-permute-done.10.refs_6_
  18.9 0.0 copy-done
  18.9 0.0 copy-done.3
  18.9 3.3 %shard_map.50 = f32[1,12288]{1,0:T(1,128)} custom-call(s32[7,24]{1,0:T(8,128)S(1)} %bitcast.9, bf16[6,96,128]{2,1,0:T(8,128)(2,1)S(1)} %get-tuple-element.19.refs_0_, f32[3,96,128]{2,1,0:T(8,128)S(1)} %shard_map.49.refs_1_, bf16[3,96,128]{2,1,0:T(8,128)(2,1)S(1)} %collective-permute-done.6.refs_2_, bf16[3,96,128]{2,1,0:T(8,128)(2,1)S(1)} %collective-permute-done.7.refs_3_, ...), custom_call_target="tpu_custom_call" | custom-call | tf_op jit(solution)/shard_map/pallas_call | solution.py:227
  (4 shorter events, 0.1 us)
Async XLA Ops:
  0.0 5.7 %copy-start.2 = (f32[1,12288]{1,0:T(1,128)S(1)}, f32[1,12288]{1,0:T(1,128)}, u32[]{:S(2)}) copy-start(f32[1,12288]{1,0:T(1,128)} %param.4) | copy-start | bytes 147460
  0.0 8.8 %copy-start.1 = (bf16[1,12288]{1,0:T(2,128)(2,1)S(1)}, bf16[1,12288]{1,0:T(2,128)(2,1)}, u32[]{:S(2)}) copy-start(bf16[1,12288]{1,0:T(2,128)(2,1)} %inc_ref.1) | copy-start | bytes 73732
  0.0 8.9 %collective-permute-start.2 = (f32[96,128]{1,0:T(8,128)}, f32[96,128]{1,0:T(8,128)S(1)}, u32[]{:S(2)}, u32[]{:S(2)}) collective-permute-start(f32[96,128]{1,0:T(8,128)} %bitcast.3), channel_id=1, source_target_pairs={{12,0},{13,1},{14,2},{15,3},{8,4},{9,5},{10,6},{11,7},{4,8},{5,9},... | collective-permute-start | bytes 147464 | tf_op jit(solution)/shard_map/ppermute | solution.py:148
  5.1 5.2 %collective-permute-start.1 = (f32[96,128]{1,0:T(8,128)}, f32[96,128]{1,0:T(8,128)S(1)}, u32[]{:S(2)}, u32[]{:S(2)}) collective-permute-start(f32[96,128]{1,0:T(8,128)} %bitcast.4), channel_id=1, source_target_pairs={{8,0},{9,1},{10,2},{11,3},{12,4},{13,5},{14,6},{15,7},{0,8},{1,9},... | collective-permute-start | bytes 147464 | tf_op jit(solution)/shard_map/ppermute | solution.py:148
  5.1 5.2 %collective-permute-start = (f32[96,128]{1,0:T(8,128)}, f32[96,128]{1,0:T(8,128)S(1)}, u32[]{:S(2)}, u32[]{:S(2)}) collective-permute-start(f32[96,128]{1,0:T(8,128)} %bitcast.5), channel_id=1, source_target_pairs={{4,0},{5,1},{6,2},{7,3},{0,4},{1,5},{2,6},{3,7},{12,8},{13,9},{14,... | collective-permute-start | bytes 147464 | tf_op jit(solution)/shard_map/ppermute | solution.py:148
  5.7 7.6 %collective-permute-start.5 = (f32[1,96,128]{2,1,0:T(8,128)S(1)}, f32[1,96,128]{2,1,0:T(8,128)S(1)}, u32[]{:S(2)}, u32[]{:S(2)}) collective-permute-start(f32[1,96,128]{2,1,0:T(8,128)S(1)} %bitcast.6), channel_id=1, source_target_pairs={{18,0},{19,1},{16,2},{17,3},{22,4},{23,5},{20,6},{21,7},{26,8},{27... | collective-permute-start | bytes 147464 | tf_op jit(solution)/shard_map/ppermute | solution.py:148
  8.3 5.6 %collective-permute-start.3 = (f32[1,96,128]{2,1,0:T(8,128)S(1)}, f32[1,96,128]{2,1,0:T(8,128)S(1)}, u32[]{:S(2)}, u32[]{:S(2)}) collective-permute-start(f32[1,96,128]{2,1,0:T(8,128)S(1)} %bitcast.7), channel_id=1, source_target_pairs={{2,0},{3,1},{0,2},{1,3},{6,4},{7,5},{4,6},{5,7},{10,8},{11,9},{8,1... | collective-permute-start | bytes 147464 | tf_op jit(solution)/shard_map/ppermute | solution.py:148
  8.9 10.1 %copy-start = (bf16[8,512,512]{2,1,0:T(8,128)(2,1)S(1)}, bf16[8,512,512]{2,1,0:T(8,128)(2,1)}, u32[]{:S(2)}) copy-start(bf16[8,512,512]{2,1,0:T(8,128)(2,1)} %refs_12_.1) | copy-start | bytes 12582916
  8.9 10.1 %copy-start.3 = (s32[24,7]{0,1:T(8,128)S(1)}, s32[24,7]{0,1:T(8,128)}, u32[]{:S(2)}) copy-start(s32[24,7]{0,1:T(8,128)} %param.6) | copy-start | bytes 2020
  8.9 5.7 %collective-permute-start.4 = (f32[2,96,128]{2,1,0:T(8,128)S(1)}, f32[2,96,128]{2,1,0:T(8,128)S(1)}, u32[]{:S(2)}, u32[]{:S(2)}) collective-permute-start(f32[2,96,128]{2,1,0:T(8,128)S(1)} %shard_map.47.pair_ref.refs_11_), channel_id=1, source_target_pairs={{16,0},{17,1},{18,2},{19,3},{20,4},{21,5},{22,6},{23,7},{24,8},{25... | collective-permute-start | bytes 294920 | tf_op jit(solution)/shard_map/ppermute | solution.py:148
  10.3 5.8 %collective-permute-start.8 = (bf16[3,96,128]{2,1,0:T(8,128)(2,1)S(1)}, bf16[3,96,128]{2,1,0:T(8,128)(2,1)S(1)}, u32[]{:S(2)}, u32[]{:S(2)}) collective-permute-start(bf16[3,96,128]{2,1,0:T(8,128)(2,1)S(1)} %get-tuple-element.24), channel_id=1, source_target_pairs={{18,0},{19,1},{16,2},{17,3},{22,4},{23,5},{20,6},{21,7},{26,8},{27... | collective-permute-start | bytes 221192 | tf_op jit(solution)/shard_map/ppermute | solution.py:148
  12.8 4.4 %collective-permute-start.7 = (bf16[3,96,128]{2,1,0:T(8,128)(2,1)S(1)}, bf16[3,96,128]{2,1,0:T(8,128)(2,1)S(1)}, u32[]{:S(2)}, u32[]{:S(2)}) collective-permute-start(bf16[3,96,128]{2,1,0:T(8,128)(2,1)S(1)} %get-tuple-element.24), channel_id=1, source_target_pairs={{16,0},{17,1},{18,2},{19,3},{20,4},{21,5},{22,6},{23,7},{24,8},{25... | collective-permute-start | bytes 221192 | tf_op jit(solution)/shard_map/ppermute | solution.py:148
  13.3 4.4 %collective-permute-start.6 = (bf16[3,96,128]{2,1,0:T(8,128)(2,1)S(1)}, bf16[3,96,128]{2,1,0:T(8,128)(2,1)S(1)}, u32[]{:S(2)}, u32[]{:S(2)}) collective-permute-start(bf16[3,96,128]{2,1,0:T(8,128)(2,1)S(1)} %get-tuple-element.24), channel_id=1, source_target_pairs={{2,0},{3,1},{0,2},{1,3},{6,4},{7,5},{4,6},{5,7},{10,8},{11,9},{8,1... | collective-permute-start | bytes 221192 | tf_op jit(solution)/shard_map/ppermute | solution.py:148
  13.8 3.8 %collective-permute-start.9 = (bf16[6,96,128]{2,1,0:T(8,128)(2,1)S(1)}, bf16[6,96,128]{2,1,0:T(8,128)(2,1)S(1)}, u32[]{:S(2)}, u32[]{:S(2)}) collective-permute-start(bf16[6,96,128]{2,1,0:T(8,128)(2,1)S(1)} %get-tuple-element.19.refs_0_), channel_id=1, source_target_pairs={{1,0},{0,1},{3,2},{2,3},{5,4},{4,5},{7,6},{6,7},{9,8},{8,9},{11,10... | collective-permute-start | bytes 442376 | tf_op jit(solution)/shard_map/ppermute | solution.py:148
  14.6 4.3 %collective-permute-start.10 = (f32[3,96,128]{2,1,0:T(8,128)S(1)}, f32[3,96,128]{2,1,0:T(8,128)S(1)}, u32[]{:S(2)}, u32[]{:S(2)}) collective-permute-start(f32[3,96,128]{2,1,0:T(8,128)S(1)} %shard_map.49.refs_1_), channel_id=1, source_target_pairs={{1,0},{0,1},{3,2},{2,3},{5,4},{4,5},{7,6},{6,7},{9,8},{8,9},{11,10... | collective-permute-start | bytes 442376 | tf_op jit(solution)/shard_map/ppermute | solution.py:148
  16.0 1.6 %collective-permute-start.13 = (bf16[3,96,128]{2,1,0:T(8,128)(2,1)S(1)}, bf16[3,96,128]{2,1,0:T(8,128)(2,1)S(1)}, u32[]{:S(2)}, u32[]{:S(2)}) collective-permute-start(bf16[3,96,128]{2,1,0:T(8,128)(2,1)S(1)} %collective-permute-done.8.refs_4_), channel_id=1, source_target_pairs={{1,0},{0,1},{3,2},{2,3},{5,4},{4,5},{7,6},{6,7},{9,8},{8,9},{11,10... | collective-permute-start | bytes 221192 | tf_op jit(solution)/shard_map/ppermute | solution.py:148
  17.2 1.3 %collective-permute-start.12 = (bf16[3,96,128]{2,1,0:T(8,128)(2,1)S(1)}, bf16[3,96,128]{2,1,0:T(8,128)(2,1)S(1)}, u32[]{:S(2)}, u32[]{:S(2)}) collective-permute-start(bf16[3,96,128]{2,1,0:T(8,128)(2,1)S(1)} %collective-permute-done.7.refs_3_), channel_id=1, source_target_pairs={{1,0},{0,1},{3,2},{2,3},{5,4},{4,5},{7,6},{6,7},{9,8},{8,9},{11,10... | collective-permute-start | bytes 221192 | tf_op jit(solution)/shard_map/ppermute | solution.py:148
  17.7 1.3 %collective-permute-start.11 = (bf16[3,96,128]{2,1,0:T(8,128)(2,1)S(1)}, bf16[3,96,128]{2,1,0:T(8,128)(2,1)S(1)}, u32[]{:S(2)}, u32[]{:S(2)}) collective-permute-start(bf16[3,96,128]{2,1,0:T(8,128)(2,1)S(1)} %collective-permute-done.6.refs_2_), channel_id=1, source_target_pairs={{1,0},{0,1},{3,2},{2,3},{5,4},{4,5},{7,6},{6,7},{9,8},{8,9},{11,10... | collective-permute-start | bytes 221192 | tf_op jit(solution)/shard_map/ppermute | solution.py:148
